TPU v7x, 256 devices: a whole 4x4x8 slice. The times are simulated.
256 devices in a mesh: section: 4 (over y), ctx: 64 (over x, z, core).
Axes of the slice: x: 4, y: 4, z: 8, core: 2. Of those that a mesh axis runs over, the one named last changes fastest.
Arguments:
- section_in: bfloat16 [4, 16384, 4096], P('section', 'ctx'), may hold values from -6 to 6
- proj_weight: bfloat16 [4, 4096, 256], P('section'), may hold values from -0.09375 to 0.09375
- conv_weight: bfloat16 [4, 4, 4352], P('section'), may hold values from -3 to 3
- log_decay: float32 [4, 16384, 64], P('section', 'ctx'), as said below
- step_size: float32 [4, 16384, 64], P('section', 'ctx'), may hold values from 0.5 to 2
- skip_gain: float32 [4, 64], P('section'), may hold values from 1 to 10
- norm_gain: bfloat16 [4, 4096], P('section'), may hold values from 0.5 to 1.5
- carry_state: float32 [4, 64, 128, 64], P('section'), may hold values from -192 to 192
- carry_rows: bfloat16 [4, 3, 4352], P('section'), may hold values from -6 to 6
Outputs:
- handed_rows: bfloat16 [4, 16384, 4096], P('section', 'ctx')
Inputs may be any that keep to these rules, and one draw needn't show every extreme that they name: `log_decay`: every entry is negative.
All inputs are finite; a program needn't handle non-finite values.
Results may differ from a plain program's by a relative error of at most 0.004.
Values may be sent and summed in bfloat16 or wider, within the bound.
No kernel may reach another device: no remote copies, remote signals or barrier semaphores. Data moves between devices by JAX's collectives and lax.ppermute only.
A program may use at most 320 MiB of HBM per device.

v0:
```python
import jax
import jax.numpy as jnp
from jax import lax
from jax.sharding import PartitionSpec as P

HEAD_COUNT = 64
HEAD_DIM = 64
STATE = 128
CONV = 4
GROUP = 256


def from_behind(value, axis, steps):
    count = lax.axis_size(axis)
    initial, last = (max(0, -steps), min(count, count - steps))
    return lax.ppermute(value, axis, [(source, source + steps) for source in range(initial, last)])


def carried_in(x, axis, join, neutral):
    place = lax.axis_index(axis)
    gathered = jax.tree.map(
        lambda a, kind: lax.all_gather(a.astype(kind), axis), x, (jnp.bfloat16, jnp.bfloat16)
    )
    state = jax.tree.map(lambda a, e: jnp.zeros_like(a) + jnp.asarray(e, a.dtype), x, neutral)

    def one(hop, state):
        return join(
            state,
            jax.tree.map(
                lambda a, own: lax.dynamic_index_in_dim(a, hop, 0, False).astype(own.dtype),
                gathered,
                x,
            ),
        )

    return lax.fori_loop(0, place, one, state)


def from_behind_2(value, axis, steps):
    count = lax.axis_size(axis)
    pairs = [(source, (source + steps) % count) for source in range(count)]
    return lax.ppermute(value, axis, pairs)


def combine_states(earlier, later):
    return (earlier[0] * later[0], later[0][:, None, None] * earlier[1] + later[1])


def intra_block(inputs):
    block_queries, block_keys, block_vals, block_cum, block_steps = inputs
    causal_mask = jnp.tril(jnp.ones((GROUP, GROUP), jnp.bool_))[None, :, :]
    scores = jnp.dot(block_queries, block_keys.T, preferred_element_type=jnp.float32)
    head_cum = block_cum.T
    head_steps = block_steps.T
    spread = head_cum[:, :, None] - head_cum[:, None, :]
    decays = jnp.where(causal_mask, jnp.exp(jnp.where(causal_mask, spread, 0.0)), 0.0)
    weights = (decays * scores[None, :, :] * head_steps[:, None, :]).astype(jnp.bfloat16)
    return jnp.einsum("hqk,khp->qhp", weights, block_vals, preferred_element_type=jnp.float32)


def per_device(
    section_in,
    proj_weight,
    conv_weight,
    log_decay,
    step_size,
    skip_gain,
    norm_gain,
    carry_state,
    carry_rows,
):
    current = section_in[0]
    projection = proj_weight[0]
    conv_taps = conv_weight[0]
    skip_term = skip_gain[0]
    gain_row = norm_gain[0]
    tokens = current.shape[0]
    channels = current.shape[1]
    blocks = tokens // GROUP
    first_device = lax.axis_index("ctx") == 0
    projected = jnp.dot(current, projection, preferred_element_type=jnp.float32).astype(
        jnp.bfloat16
    )
    wide_rows = jnp.concatenate([current, projected], axis=1)
    rim_rows = from_behind(wide_rows[tokens - (CONV - 1) :], "ctx", 1)
    rim_rows = jnp.where(first_device, carry_rows[0], rim_rows)
    padded = jnp.concatenate([rim_rows, wide_rows], axis=0)
    conv_sum = jnp.zeros(wide_rows.shape, jnp.float32)
    for tap_id in range(CONV):
        conv_sum = conv_sum + conv_taps[tap_id].astype(jnp.float32) * padded[
            tap_id : tap_id + tokens
        ].astype(jnp.float32)
    activated = jax.nn.silu(conv_sum).astype(jnp.bfloat16)
    values = activated[:, :channels].reshape(blocks, GROUP, HEAD_COUNT, HEAD_DIM)
    keys_in = activated[:, channels : channels + STATE].reshape(blocks, GROUP, STATE)
    queries = activated[:, channels + STATE :].reshape(blocks, GROUP, STATE)
    cumulative = jnp.cumsum(log_decay[0].reshape(blocks, GROUP, HEAD_COUNT), axis=1)
    step_blocks = step_size[0].reshape(blocks, GROUP, HEAD_COUNT)
    intra_out = lax.map(intra_block, (queries, keys_in, values, cumulative, step_blocks))
    to_end = jnp.exp(cumulative[:, -1:, :] - cumulative) * step_blocks
    factor = (to_end[:, :, :, None] * keys_in.astype(jnp.float32)[:, :, None, :]).astype(
        jnp.bfloat16
    )
    fresh_state = jnp.einsum("bqhn,bqhp->bhnp", factor, values, preferred_element_type=jnp.float32)
    block_decay = jnp.exp(cumulative[:, -1, :])
    running = jnp.zeros((HEAD_COUNT, STATE, HEAD_DIM), jnp.float32)
    running_decay = jnp.ones((HEAD_COUNT,), jnp.float32)
    local_starts = running
    prefix_decays = running_decay
    running = block_decay[0][:, None, None] * running + fresh_state[0]
    running_decay = running_decay * block_decay[0]
    identity = (
        jnp.ones((HEAD_COUNT,), jnp.float32),
        jnp.zeros((HEAD_COUNT, STATE, HEAD_DIM), jnp.float32),
    )
    before_decay, before_state = carried_in(
        (running_decay, running), "ctx", combine_states, identity
    )
    incoming = before_state + before_decay[:, None, None] * carry_state[0]
    start_states = jnp.stack([local_starts + prefix_decays[:, None, None] * incoming])
    query_float = queries.astype(jnp.float32)
    carried = jnp.exp(cumulative)[:, :, :, None] * jnp.einsum(
        "bqn,bhnp->bqhp", query_float, start_states, precision=lax.Precision.HIGHEST
    )
    output = (
        intra_out + carried + skip_term[None, None, 0:HEAD_COUNT, None] * values.astype(jnp.float32)
    )
    mean_sq = jnp.mean(output * output, axis=3, keepdims=True)
    normed = (output * lax.rsqrt(mean_sq + 1e-05)).reshape(tokens, (HEAD_COUNT - 0) * HEAD_DIM)
    handed = from_behind_2(
        (current.astype(jnp.float32) + gain_row.astype(jnp.float32) * normed).astype(jnp.bfloat16),
        "section",
        1,
    )
    return handed[None]


def solution(mesh):
    return jax.shard_map(
        per_device,
        mesh=mesh,
        in_specs=(
            P("section", "ctx", None),
            P("section", None, None),
            P("section", None, None),
            P("section", "ctx", None),
            P("section", "ctx", None),
            P("section", None),
            P("section", None),
            P("section", None, None, None),
            P("section", None, None),
        ),
        out_specs=P("section", "ctx", None),
        check_vma=False,
    )
```

profile of v0, /device:TPU:231, one launch (start us, length us, event | category | flops | bytes accessed | tf_op | source)
XLA Modules:
  0.0 941.4 jit_solution(15882152901430873872)
XLA Ops:
  31.6 39.3 %all-gather = bf16[64,1,64]{2,1,0:T(2,128)(2,1)S(1)} all-gather(bf16[1,1,64]{2,1,0:T(2,128)(2,1)S(1)} %get-tuple-element.113), channel_id=2, replica_groups=mesh['section'=4,'ctx'=64] {'ctx'}, dimensions={0}, use_global_device_ids=true | all-gather | bytes 8320 | tf_op jit(solution)/shard_map/all_gather | solution.py:22
  77.3 190.8 %all-gather.4.cloned.1.call-done = bf16[4096,128,64]{1,2,0:T(8,128)(2,1)} async-done(((bf16[64,128,64]{1,2,0:T(8,128)(2,1)}), bf16[4096,128,64]{1,2,0:T(8,128)(2,1)}) %all-gather.4.cloned.1.call-update) | async-done | bytes 67108880 | tf_op jit(solution)/shard_map/all_gather | solution.py:22
  270.5 591.7 %while.3 = (s32[]{:T(128)}, f32[64]{0:T(128)S(1)}, f32[64,128,64]{2,1,0:T(8,128)}, s32[]{:T(128)}, bf16[64,64]{1,0:T(8,128)(2,1)S(1)}, /*index=5*/bf16[64,64,128...) while((s32[]{:T(128)}, f32[64]{0:T(128)S(1)}, f32[64,128,64]{2,1,0:T(8,128)}, s32[]{:T(128)}, ...), condition=%wide.region_3.4_spmd, body=%wide.region_2.3_spmd.sunk | while | flops 1572997 | bytes 9506175 | solution.py:36
  274.7 5.2 convert_add_fusion.2
  284.1 5.2 convert_add_fusion.2
  293.5 5.2 convert_add_fusion.2
  302.8 5.2 convert_add_fusion.2
  312.2 5.2 convert_add_fusion.2
  321.6 5.2 convert_add_fusion.2
  331.0 5.2 convert_add_fusion.2
  340.4 5.2 convert_add_fusion.2
  349.8 5.2 convert_add_fusion.2
  359.2 5.2 convert_add_fusion.2
  368.6 5.2 convert_add_fusion.2
  378.0 5.2 convert_add_fusion.2
  462.5 5.2 convert_add_fusion.2
  528.3 5.2 convert_add_fusion.2
  641.0 5.2 convert_add_fusion.2
  706.7 5.2 convert_add_fusion.2
  819.4 5.2 convert_add_fusion.2
  862.3 5.9 fusion.8
  875.7 5.9 multiply_reduce_fusion
  884.1 5.6 copy.69
  894.5 38.7 %collective-permute-done.1 = bf16[256,4096]{1,0:T(8,128)(2,1)S(1)} collective-permute-done((bf16[256,4096]{1,0:T(8,128)(2,1)S(1)}, bf16[256,4096]{1,0:T(8,128)(2,1)S(1)}, u32[]{:S(2)}, u32[]{:S(2)}) %collective-permute-start.1) | collective-permute-done | bytes 2097184 | tf_op jit(solution)/shard_map/ppermute | solution.py:42
  (807 shorter events, 551.2 us)
Async XLA Ops:
  6.5 6.4 copy-start.7
  6.5 7.5 copy-start.5
  6.5 7.6 copy-start.4
  6.5 8.4 copy-start.9
  6.5 261.5 %all-gather.4.cloned.1.call-start = ((), (), s32[]{:S(2)}) async-start(), calls=%async_computation | async-start | bytes 68157440 | tf_op jit(solution)/shard_map/all_gather | solution.py:22
  11.6 3.3 collective-permute-start
  31.6 44.0 %copy-start.14 = (bf16[1,4096]{1,0:T(2,128)(2,1)S(1)}, bf16[1,4096]{1,0:T(2,128)(2,1)}, u32[]{:S(2)}) copy-start(bf16[1,4096]{1,0:T(2,128)(2,1)} %param.17) | copy-start | bytes 24580
  284.1 5.3 copy-start.13
  302.8 5.3 copy-start.13
  321.6 5.3 copy-start.13
  331.0 5.3 copy-start.13
  349.8 5.3 copy-start.13
  368.6 5.3 copy-start.13
  396.8 5.3 copy-start.13
  415.6 5.3 copy-start.13
  434.3 5.3 copy-start.13
  443.7 5.3 copy-start.13
  462.5 5.3 copy-start.13
  481.3 5.3 copy-start.13
  500.1 5.3 copy-start.13
  509.5 5.3 copy-start.13
  528.3 5.3 copy-start.13
  547.0 5.3 copy-start.13
  893.2 40.0 %collective-permute-start.1 = (bf16[256,4096]{1,0:T(8,128)(2,1)S(1)}, bf16[256,4096]{1,0:T(8,128)(2,1)S(1)}, u32[]{:S(2)}, u32[]{:S(2)}) collective-permute-start(bf16[256,4096]{1,0:T(8,128)(2,1)S(1)} %add_convert_fusion), channel_id=1, source_target_pairs={{0,64},{64,128},{128,192},{192,0},{1,65},{65,129},{129,193},{193,1... | collective-permute-start | bytes 6291464 | tf_op jit(solution)/shard_map/ppermute | solution.py:42
  (243 other events, 669.0 us)
Sparse Core Ops, SparseCore 0:
  31.7 236.3 all-gather.3
where the time goes:
time: 944 us; the launch traced here: 941 us
  other arithmetic  385 us (41%)
  local copies, waits for them, and re-layouts  252 us (27%)
  waiting for transfers between devices  230 us (24%)
  blocking collectives  39.3 us (4%)
  matrix products  18 us (2%)
  between operations  13.7 us (1%)
    add x63, other arithmetic, combine_states(): later[0][:, None, None] * earlier[1] + later[1]  331 us
    dynamic_slice x126, local copies, waits for them, and re-layouts, one(): lax.dynamic_index_in_dim(a, hop, 0, False).astype(own.dtype)  193 us
    all_gather x1, waiting for transfers between devices, carried_in(): lax.all_gather(a.astype(kind), axis)  191 us
    all_gather x1, blocking collectives, carried_in(): lax.all_gather(a.astype(kind), axis)  39.3 us
    ppermute x1, waiting for transfers between devices, from_behind_2(): return lax.ppermute(value, axis, pairs)  38.7 us
    mul x63, other arithmetic, combine_states(): earlier[0] * later[0]  34.5 us
    while x504, local copies, waits for them, and re-layouts  32.9 us
  transfers between devices with their start and end apart: 3, of which 3 were waited for; matrix products, arithmetic and copies ran while one was open for 1% of the time, Pallas kernels for 0%

commit v1 on v0

v1 whole, which is shorter than its diff:
```python
import functools

import jax
import jax.numpy as jnp
from jax import lax
from jax.experimental import pallas as pl
from jax.experimental.pallas import tpu as pltpu
from jax.sharding import Mesh
from jax.sharding import PartitionSpec as P

HEADS = 64
DIM = 64
STATE = 128
TOK = 256
CH = 4096
LANES = 512
GROUPS = 8
ROWS = 16
LOG2E = 1.4426950408889634
CTX = ("x", "z", "core")
F32 = jnp.float32
BF16 = jnp.bfloat16
PARAMS = pltpu.CompilerParams(vmem_limit_bytes=56 * 2**20)


def dot(a, b):
    return jnp.dot(a, b, preferred_element_type=F32)


def parts(x, count):
    out = []
    for _ in range(count):
        piece = x.astype(BF16)
        out.append(piece)
        x = x - piece.astype(F32)
    return out


def iota(shape, axis):
    return lax.broadcasted_iota(jnp.int32, shape, axis)


def spread_matrix(rows, group, width):
    head = iota((rows, width), 1) // DIM + group * (LANES // DIM)
    return (iota((rows, width), 0) % HEADS == head).astype(F32).astype(BF16)


def conv_silu(pad, x, halo, taps):
    pad[0:16, :] = halo.astype(F32)
    pad[16:272, :] = x.astype(F32)
    total = taps[0:1] * pad[13:269, :]
    for j in range(1, 4):
        total = total + taps[j : j + 1] * pad[13 + j : 269 + j, :]
    return (total / (1.0 + jnp.exp(-total))).astype(BF16)


def first_kernel(
    first, u, halo, weight, taps, rates, steps, carried_bc, vals, bc, log_col, log_row, decay, pay, pad, lhs
):
    w = weight[...]
    projected = dot(u[...], w).astype(BF16)
    halo_bc = dot(halo[...], w).astype(BF16).astype(F32)
    halo_bc = jnp.where(first[0] == 1, carried_bc[...].astype(F32), halo_bc)
    for i in range(2):
        cols = slice(i * 128, (i + 1) * 128)
        bc[:, cols] = conv_silu(
            pad.at[i],
            projected[:, cols],
            halo_bc[:, cols],
            taps[:, CH + i * 128 : CH + (i + 1) * 128].astype(F32),
        )
    lhs[...] = bc[:, 0:128].astype(F32).T.astype(BF16)
    tri = (iota((TOK, TOK), 0) >= iota((TOK, TOK), 1)).astype(F32).astype(BF16)
    cum = sum(dot(tri, piece) for piece in parts(rates[...], 3))
    step = steps[...]
    last = cum[TOK - 1 : TOK]
    log2cum = cum * LOG2E
    log_col[...] = jnp.concatenate([log2cum, jnp.zeros_like(cum)], axis=1)
    row = log2cum - jnp.log2(step)
    log_row[...] = jnp.concatenate([row, row], axis=1).T[0:HEADS]
    to_end = jnp.concatenate(parts(jnp.exp(last - cum) * step, 2), axis=1)
    decay[...] = jnp.concatenate(parts(jnp.exp(cum), 2), axis=1)
    hi, mid, lo = parts(jnp.exp(last), 3)
    kind = iota((ROWS, HEADS), 0) // 4
    end_decay = jnp.where(
        kind == 0,
        hi.astype(F32),
        jnp.where(kind == 1, mid.astype(F32), jnp.where(kind == 2, lo.astype(F32), 0.0)),
    ).astype(BF16)
    row4 = iota((ROWS, 128), 0) % 4

    def one(q, _):
        base = pl.multiple_of(q * LANES, LANES)
        scale = dot(to_end, spread_matrix(2 * HEADS, q, LANES))
        ends = dot(end_decay, spread_matrix(HEADS, q, LANES))
        scaled = []
        for i in range(4):
            cols = pl.ds(pl.multiple_of(base + i * 128, 128), 128)
            act = conv_silu(pad.at[i], u[:, cols], halo[:, cols], taps[:, cols].astype(F32))
            vals[:, cols] = act
            scaled.append((act.astype(F32) * scale[:, i * 128 : (i + 1) * 128]).astype(BF16))
        fresh = dot(lhs[...], jnp.concatenate(scaled, axis=1)).astype(BF16)
        tail = jnp.zeros((ROWS, 128), F32)
        for i in range(4):
            tail = jnp.where(row4 == i, ends[:, i * 128 : (i + 1) * 128], tail)
        tail = tail.astype(BF16)
        core, x = q // 4, q % 4
        for g in range(8):
            owner = (x * 8 + g) * 2 + core
            pay[owner, :, 0:LANES] = fresh[g * ROWS : (g + 1) * ROWS]
            pay[owner, :, LANES : LANES + 128] = tail
        return 0

    lax.fori_loop(0, GROUPS, one, 0)


def scan_kernel(blocks, got, start, out):
    def one(i, state):
        out[i] = state.astype(BF16)
        tail = got[i, :, LANES : LANES + 128].astype(F32)
        tail = tail[0:4] + tail[4:8] + tail[8:12]
        ends = jnp.concatenate([tail[i : i + 1] for i in range(4)], axis=1)
        return state * ends + got[i, :, 0:LANES].astype(F32)

    lax.fori_loop(0, blocks, one, start[...])


def last_kernel(u, vals, bc, log_col, log_row, decay, starts, skip, gain, out, scores):
    q = pl.program_id(0)

    @pl.when(q == 0)
    def _():
        scores[...] = lax.dot_general(
            bc[:, 128:256], bc[:, 0:128], (((1,), (1,)), ((), ())), preferred_element_type=F32
        )

    core, x = q // 4, q % 4
    state = jnp.concatenate([starts[(x * 8 + g) * 2 + core] for g in range(8)], axis=0)
    carried = dot(bc[:, 128:256], state) * dot(decay[...], spread_matrix(2 * HEADS, q, LANES))
    cols = pltpu.roll(log_col[...], (128 - 8 * q) % 128, 1)
    rows = log_row[pl.ds(pl.multiple_of(q * 8, 8), 8), :]
    half = TOK // 2
    causal = iota((half, half), 0) >= iota((half, half), 1)
    left = iota((TOK, 128), 1) < DIM
    same = (iota((128, 128), 0) // DIM == iota((128, 128), 1) // DIM).astype(F32).astype(BF16)
    for i in range(4):
        lane = slice(i * 128, (i + 1) * 128)
        value = vals[:, lane]
        both = []
        for h in (2 * i, 2 * i + 1):
            col = cols[:, h : h + 1]
            row = rows[h : h + 1]
            top = jnp.exp2(jnp.where(causal, col[:half] - row[:, :half], -jnp.inf)) * scores[:half, :half]
            low_left = jnp.exp2(col[half:] - row[:, :half]) * scores[half:, :half]
            low_right = jnp.exp2(jnp.where(causal, col[half:] - row[:, half:], -jnp.inf)) * scores[half:, half:]
            low = jnp.concatenate([low_left.astype(BF16), low_right.astype(BF16)], axis=1)
            both.append(
                jnp.concatenate([dot(top.astype(BF16), value[:half]), dot(low, value)], axis=0)
            )
        result = jnp.where(left, both[0], both[1]) + carried[:, lane] + skip[:, lane] * value.astype(F32)
        mean_sq = dot((result * result).astype(BF16), same) * (1.0 / DIM)
        normed = result * lax.rsqrt(mean_sq + 1e-05)
        out[:, lane] = (u[:, lane].astype(F32) + gain[:, lane].astype(F32) * normed).astype(BF16)


def whole(*shape):
    return pl.BlockSpec(shape, lambda q: (0,) * len(shape))


def per_device(
    section_in, proj_weight, conv_weight, log_decay, step_size, skip_gain, norm_gain, carry_state, carry_rows
):
    u = section_in[0]
    place = lax.axis_index(CTX)
    first = place == 0
    behind = lax.ppermute(u[TOK - 16 :], CTX, [(i, i + 1) for i in range(63)])
    before = jnp.concatenate([jnp.zeros((13, CH + 256), BF16), carry_rows[0]], axis=0)
    halo = jnp.where(first, before[:, :CH], behind)
    vmem = pl.BlockSpec(memory_space=pltpu.VMEM)
    vals, bc, log_col, log_row, decay, pay = pl.pallas_call(
        first_kernel,
        out_shape=(
            jax.ShapeDtypeStruct((TOK, CH), BF16),
            jax.ShapeDtypeStruct((TOK, 256), BF16),
            jax.ShapeDtypeStruct((TOK, 128), F32),
            jax.ShapeDtypeStruct((HEADS, TOK), F32),
            jax.ShapeDtypeStruct((TOK, 128), BF16),
            jax.ShapeDtypeStruct((64, ROWS, LANES + 128), BF16),
        ),
        in_specs=[pl.BlockSpec(memory_space=pltpu.SMEM)] + [vmem] * 7,
        out_specs=[vmem] * 6,
        scratch_shapes=[pltpu.VMEM((4, 272, 128), F32), pltpu.VMEM((128, TOK), BF16)],
        compiler_params=PARAMS,
        name="first",
    )(
        first.astype(jnp.int32)[None],
        u,
        halo,
        proj_weight[0],
        conv_weight[0],
        log_decay[0],
        step_size[0],
        before[:, CH:],
    )
    got = lax.all_to_all(pay, CTX, 0, 0)
    head = (lax.axis_index("core") * 4 + lax.axis_index("x")) * 8
    start = lax.dynamic_slice(carry_state[0], (head, lax.axis_index("z") * ROWS, 0), (8, ROWS, DIM))
    start = start.transpose(1, 0, 2).reshape(ROWS, LANES)
    back = pl.pallas_call(
        functools.partial(scan_kernel, 64),
        out_shape=jax.ShapeDtypeStruct((64, ROWS, LANES), BF16),
        in_specs=[vmem] * 2,
        out_specs=vmem,
        compiler_params=PARAMS,
        name="scan",
    )(got, start)
    starts = lax.all_to_all(back, CTX, 0, 0)
    wide = pl.BlockSpec((TOK, LANES), lambda q: (0, q))
    line = pl.BlockSpec((1, LANES), lambda q: (0, q))
    rows = pl.pallas_call(
        last_kernel,
        grid=(GROUPS,),
        out_shape=jax.ShapeDtypeStruct((TOK, CH), BF16),
        in_specs=[
            wide,
            wide,
            whole(TOK, 256),
            whole(TOK, 128),
            whole(HEADS, TOK),
            whole(TOK, 128),
            whole(64, ROWS, LANES),
            line,
            line,
        ],
        out_specs=wide,
        scratch_shapes=[pltpu.VMEM((TOK, TOK), F32)],
        compiler_params=PARAMS,
        name="last",
    )(u, vals, bc, log_col, log_row, decay, starts, jnp.repeat(skip_gain, DIM, axis=1), norm_gain)
    handed = lax.ppermute(rows, "section", [(i, (i + 1) % 4) for i in range(4)])
    return handed[None]


def solution(mesh):
    split = Mesh(mesh.devices.reshape(4, 4, 8, 2), ("section",) + CTX)
    tokens = P("section", CTX, None)
    layer = P("section", None, None)
    return jax.shard_map(
        per_device,
        mesh=split,
        in_specs=(
            tokens,
            layer,
            layer,
            tokens,
            tokens,
            P("section", None),
            P("section", None),
            P("section", None, None, None),
            layer,
        ),
        out_specs=tokens,
        check_vma=False,
    )
```

time: 944 us -> 169 us (0.18)
  the two profiles are of different devices: /device:TPU:231 before, /device:TPU:1 now
where the time goes in v1:
time: 169 us
  waiting for transfers between devices  107 us (63%)
  Pallas kernels  24.7 us (15%)
  starting transfers between devices  23.5 us (14%)
  local copies, waits for them, and re-layouts  12.2 us (7%)
    ppermute x1, waiting for transfers between devices, per_device(): handed = lax.ppermute(rows, 'section', [(i, (i + 1) % 4) for i in range(4)])  47.4 us
    all_to_all x1, waiting for transfers between devices, per_device(): got = lax.all_to_all(pay, CTX, 0, 0)  31.6 us
    all_to_all x1, waiting for transfers between devices, per_device(): starts = lax.all_to_all(back, CTX, 0, 0)  27.8 us
    pallas_call x1, Pallas kernels, per_device(): pl.pallas_call(last_kernel, grid=(GROUPS,), out_shape=jax.ShapeDtypeStruc...  11.1 us
    all_to_all x1, starting transfers between devices, per_device(): got = lax.all_to_all(pay, CTX, 0, 0)  11.1 us
    pallas_call x1, Pallas kernels, per_device(): pl.pallas_call(first_kernel, out_shape=(jax.ShapeDtypeStruct((TOK, CH), B...  10.6 us
    unnamed x11, local copies, waits for them, and re-layouts  6.6 us
    all_to_all x1, starting transfers between devices, per_device(): starts = lax.all_to_all(back, CTX, 0, 0)  6.16 us
  transfers between devices with their start and end apart: 4, of which 3 were waited for; matrix products, arithmetic and copies ran while one was open for 5% of the time, Pallas kernels for 0%

profile of v1, /device:TPU:1, one launch (start us, length us, event | category | flops | bytes accessed | tf_op | source)
XLA Modules:
  0.0 168.7 jit_solution(5528495702913817131)
XLA Ops:
  0.0 0.0 copy-start
  0.0 1.1 slice_bitcast_fusion
  1.1 4.9 %collective-permute-start = (bf16[16,4096]{1,0:T(8,128)(2,1)S(1)}, bf16[16,4096]{1,0:T(8,128)(2,1)S(1)}, u32[]{:S(2)}, u32[]{:S(2)}) collective-permute-start(bf16[16,4096]{1,0:T(8,128)(2,1)S(1)} %slice_bitcast_fusion), channel_id=1, source_target_pairs={{0,1},{1,2},{2,3},{3,4},{4,5},{5,6},{6,7},{7,8},{8,9},{9,10},{10,1... | collective-permute-start | bytes 393224 | tf_op jit(solution)/shard_map/ppermute | solution.py:176
  6.0 1.6 copy.12
  7.6 1.6 copy.13
  9.2 1.3 pad_slice_fusion.carried_bc
  10.5 0.0 collective-permute-done
  10.5 1.4 fusion.halo
  11.9 10.6 %first.1 = (bf16[256,4096]{1,0:T(8,128)(2,1)}, bf16[256,256]{1,0:T(8,128)(2,1)}, f32[256,128]{1,0:T(8,128)}, f32[64,256]{1,0:T(8,128)}, bf16[256,128]{1,0:T(8,128)(2,1)}, /*index=5*/bf16[64,16,640]{2,1,0:T(8,128)(2,1)}) custom-call(s32[1]{0:T(128)} %bitcast.1.first, bf16[256,4096]{1,0:T(8,128)(2,1)} %bitcast.17, bf16[16,4096]{1,0:T(8,128)(2,1)} %fusion.halo, ...), custom_call_target="tpu_custom_call" | custom-call | tf_op jit(solution)/shard_map/first/pallas_call | solution.py:180
  22.5 11.1 %all-to-all-start = ((bf16[64,16,640]{2,1,0:T(8,128)(2,1)}), bf16[64,16,640]{2,1,0:T(8,128)(2,1)S(1)}, u32[]{:S(2)}, u32[]{:S(2)}) async-start(bf16[64,16,640]{2,1,0:T(8,128)(2,1)} %get-tuple-element.16), calls=%async_computation | async-start | bytes 2621440 | tf_op jit(solution)/shard_map/all_to_all | solution.py:205
  33.6 0.9 constant_dynamic-slice_fusion
  34.5 1.7 copy.18.start
  36.1 31.6 %all-to-all-done.got = bf16[64,16,640]{2,1,0:T(8,128)(2,1)S(1)} async-done(((bf16[64,16,640]{2,1,0:T(8,128)(2,1)}), bf16[64,16,640]{2,1,0:T(8,128)(2,1)S(1)}, u32[]{:S(2)}, u32[]{:S(2)}) %all-to-all-start) | async-done | bytes 1310752 | tf_op jit(solution)/shard_map/all_to_all | solution.py:205
  67.8 1.1 copy-done.1
  68.9 3.0 %scan.1 = bf16[64,16,512]{2,1,0:T(8,128)(2,1)} custom-call(bf16[64,16,640]{2,1,0:T(8,128)(2,1)} %copy-done.1, f32[16,512]{1,0:T(8,128)} %copy.18.start), custom_call_target="tpu_custom_call" | custom-call | tf_op jit(solution)/shard_map/scan/pallas_call | solution.py:209
  71.8 6.2 %all-to-all-start.1 = ((bf16[64,16,512]{2,1,0:T(8,128)(2,1)}), bf16[64,16,512]{2,1,0:T(8,128)(2,1)S(1)}, u32[]{:S(2)}, u32[]{:S(2)}) async-start(bf16[64,16,512]{2,1,0:T(8,128)(2,1)} %scan.1), calls=%async_computation.1 | async-start | bytes 2097152 | tf_op jit(solution)/shard_map/all_to_all | solution.py:217
  78.0 0.1 broadcast_in_dim.16
  78.1 0.7 broadcast_in_dim.17.skip
  78.8 27.8 %all-to-all-done.1.starts = bf16[64,16,512]{2,1,0:T(8,128)(2,1)S(1)} async-done(((bf16[64,16,512]{2,1,0:T(8,128)(2,1)}), bf16[64,16,512]{2,1,0:T(8,128)(2,1)S(1)}, u32[]{:S(2)}, u32[]{:S(2)}) %all-to-all-start.1) | async-done | bytes 1048608 | tf_op jit(solution)/shard_map/all_to_all | solution.py:217
  106.6 1.0 copy-done.2
  107.6 11.1 %last.1 = bf16[256,4096]{1,0:T(8,128)(2,1)} custom-call(bf16[256,4096]{1,0:T(8,128)(2,1)} %bitcast.18, bf16[256,4096]{1,0:T(8,128)(2,1)} %get-tuple-element.11.vals, bf16[256,256]{1,0:T(8,128)(2,1)} %get-tuple-element.12.bc, f32[256,128]{1,0:T(8,128)} %get-tuple-element.13.log_col, f32[64,256]{1,0:T(8,128)} %get-tuple-element.14.log_row, ...), custom_call_target="tpu_custom_call" | custom-call | tf_op jit(solution)/shard_map/last/pallas_call | solution.py:220
  118.7 1.3 collective-permute-start.1
  120.0 47.4 %collective-permute-done.1 = bf16[256,4096]{1,0:T(8,128)(2,1)S(1)} collective-permute-done((bf16[256,4096]{1,0:T(8,128)(2,1)}, bf16[256,4096]{1,0:T(8,128)(2,1)S(1)}, u32[]{:S(2)}, u32[]{:S(2)}) %collective-permute-start.1) | collective-permute-done | bytes 2097184 | tf_op jit(solution)/shard_map/ppermute | solution.py:240
  167.4 1.3 copy.20
  (5 shorter events, 0.0 us)
Async XLA Ops:
  0.0 33.6 %copy-start = (f32[1,64,128,64]{2,3,1,0:T(8,128)S(1)}, f32[1,64,128,64]{2,3,1,0:T(8,128)}, u32[]{:S(2)}) copy-start(f32[1,64,128,64]{2,3,1,0:T(8,128)} %param.16) | copy-start | bytes 6291460
  1.1 9.4 %collective-permute-start = (bf16[16,4096]{1,0:T(8,128)(2,1)S(1)}, bf16[16,4096]{1,0:T(8,128)(2,1)S(1)}, u32[]{:S(2)}, u32[]{:S(2)}) collective-permute-start(bf16[16,4096]{1,0:T(8,128)(2,1)S(1)} %slice_bitcast_fusion), channel_id=1, source_target_pairs={{0,1},{1,2},{2,3},{3,4},{4,5},{5,6},{6,7},{7,8},{8,9},{9,10},{10,1... | collective-permute-start | bytes 393224 | tf_op jit(solution)/shard_map/ppermute | solution.py:176
  22.5 45.2 %all-to-all-start = ((bf16[64,16,640]{2,1,0:T(8,128)(2,1)}), bf16[64,16,640]{2,1,0:T(8,128)(2,1)S(1)}, u32[]{:S(2)}, u32[]{:S(2)}) async-start(bf16[64,16,640]{2,1,0:T(8,128)(2,1)} %get-tuple-element.16), calls=%async_computation | async-start | bytes 2621440 | tf_op jit(solution)/shard_map/all_to_all | solution.py:205
  36.1 41.9 %copy-start.3 = (f32[1,64]{1,0:T(1,128)S(1)}, f32[1,64]{1,0:T(1,128)}, u32[]{:S(2)}) copy-start(f32[1,64]{1,0:T(1,128)} %param.14) | copy-start | bytes 772
  67.8 1.1 copy-start.1
  71.8 34.7 %all-to-all-start.1 = ((bf16[64,16,512]{2,1,0:T(8,128)(2,1)}), bf16[64,16,512]{2,1,0:T(8,128)(2,1)S(1)}, u32[]{:S(2)}, u32[]{:S(2)}) async-start(bf16[64,16,512]{2,1,0:T(8,128)(2,1)} %scan.1), calls=%async_computation.1 | async-start | bytes 2097152 | tf_op jit(solution)/shard_map/all_to_all | solution.py:217
  106.6 1.0 copy-start.2
  118.7 48.7 %collective-permute-start.1 = (bf16[256,4096]{1,0:T(8,128)(2,1)}, bf16[256,4096]{1,0:T(8,128)(2,1)S(1)}, u32[]{:S(2)}, u32[]{:S(2)}) collective-permute-start(bf16[256,4096]{1,0:T(8,128)(2,1)} %last.1), channel_id=1, source_target_pairs={{0,64},{64,128},{128,192},{192,0},{1,65},{65,129},{129,193},{193,1... | collective-permute-start | bytes 6291464 | tf_op jit(solution)/shard_map/ppermute | solution.py:240

commit v2 on v1

v2 whole, which is shorter than its diff:
```python
import functools

import jax
import jax.numpy as jnp
from jax import lax
from jax.experimental import pallas as pl
from jax.experimental.pallas import tpu as pltpu
from jax.sharding import Mesh
from jax.sharding import PartitionSpec as P

HEADS = 64
DIM = 64
STATE = 128
TOK = 256
CH = 4096
HALF = CH // 2
LANES = 512
GROUPS = 8
ROWS = 16
CHIPS = 32
LOG2E = 1.4426950408889634
F32 = jnp.float32
BF16 = jnp.bfloat16


def params(mib):
    return pltpu.CompilerParams(vmem_limit_bytes=mib * 2**20)


def cost(flops, moved, exps=0):
    return pl.CostEstimate(flops=int(flops), bytes_accessed=int(moved), transcendentals=int(exps))


def dot(a, b):
    return jnp.dot(a, b, preferred_element_type=F32)


def parts(x, count):
    out = []
    for _ in range(count):
        piece = x.astype(BF16)
        out.append(piece)
        x = x - piece.astype(F32)
    return out


def iota(shape, axis):
    return lax.broadcasted_iota(jnp.int32, shape, axis)


def two_parts(x):
    hi = x.astype(BF16).astype(F32)
    return jnp.where(iota(x.shape, 1) < HEADS, hi, x - hi).astype(BF16)


def spread_matrix(rows, group):
    head = iota((rows, LANES), 1) // DIM + group * (LANES // DIM)
    return (iota((rows, LANES), 0) % HEADS == head).astype(F32).astype(BF16)


def conv_silu(pad, x, halo, taps):
    pad[0:16, :] = halo.astype(F32)
    pad[16:272, :] = x.astype(F32)
    total = taps[0:1] * pad[13:269, :]
    for j in range(1, 4):
        total = total + taps[j : j + 1] * pad[13 + j : 269 + j, :]
    return (total / (1.0 + jnp.exp(-total))).astype(BF16)


def cumulated(rates):
    tri = (iota((TOK, TOK), 0) <= iota((TOK, TOK), 1)).astype(F32).astype(BF16)
    return sum(dot(piece, tri) for piece in parts(rates, 3))


def twice_turned(x):
    return jnp.concatenate([x, x], axis=0).T


def project_kernel(u, weight, rates, steps, projected, to_end, ends):
    projected[...] = dot(u[...], weight[...]).astype(BF16)
    cum = twice_turned(cumulated(rates[...]))
    last = cum[TOK - 1 : TOK]
    to_end[...] = two_parts(jnp.exp(last - cum) * twice_turned(steps[...]))
    hi, mid, lo = (piece.astype(F32) for piece in parts(jnp.exp(last), 3))
    kind = iota((ROWS, 128), 0) // 4
    tile = jnp.where(kind == 0, hi, jnp.where(kind == 1, mid, jnp.where(kind == 2, lo, 0.0)))
    ends[...] = jnp.where(iota((ROWS, 128), 1) < HEADS, tile, 0.0).astype(BF16)


def fresh_part(q, u, halo, taps, to_end, ends, turned, fresh, pad):
    spread = spread_matrix(2 * HEADS, q)
    scale = dot(to_end[...], spread)
    scaled = []
    for i in range(4):
        lane = slice(i * 128, (i + 1) * 128)
        act = conv_silu(pad.at[i], u[:, lane], halo[:, lane], taps[:, lane].astype(F32))
        scaled.append((act.astype(F32) * scale[:, lane]).astype(BF16))
    fresh[0:STATE, :] = dot(turned[...], jnp.concatenate(scaled, axis=1)).astype(BF16)
    fresh[STATE : STATE + ROWS, :] = dot(ends[...], spread).astype(BF16)


def send_kernel(
    flags, u, halo, taps, to_end, ends, all_halo, weight, projected, all_taps, carried_bc, par, fresh, turned, pack, pad
):
    step = pl.program_id(0)

    @pl.when(step == 0)
    def _():
        near = dot(all_halo[...], weight[...]).astype(BF16).astype(F32)
        near = jnp.where(flags[0] == 1, carried_bc[...].astype(F32), near)
        acts = []
        for i in range(2):
            lane = slice(i * 128, (i + 1) * 128)
            tap = all_taps[:, CH + i * 128 : CH + (i + 1) * 128].astype(F32)
            acts.append(conv_silu(pad.at[i], projected[:, lane], near[:, lane], tap))
        turned[...] = acts[0].astype(F32).T.astype(BF16)
        for s in range(16):
            for i in range(2):
                pack[s, :, i * 128 : (i + 1) * 128] = acts[i][s * 16 : (s + 1) * 16]
            lane = slice(s * 256, (s + 1) * 256)
            slab = jnp.where(
                iota((16, 256), 0) >= 13, all_halo[:, lane].astype(F32), par[:, lane].astype(F32)
            )
            pack[16 + s] = slab.astype(BF16)

    fresh_part(flags[1] * 4 + step, u, halo, taps, to_end, ends, turned, fresh, pad)


def keep_kernel(flags, u, halo, taps, to_end, ends, turned, fresh, pad):
    fresh_part(flags[2] * 4 + pl.program_id(0), u, halo, taps, to_end, ends, turned, fresh, pad)


def end_row(tail):
    tail = tail.astype(F32)
    return tail[0:1] + tail[4:5] + tail[8:9]


def join_kernel(flags, keep, got, pay, head_fresh):
    own, other = keep[0:STATE].astype(F32), got[0:STATE].astype(F32)
    own_end, other_end = end_row(keep[STATE:]), end_row(got[STATE:])
    lead = flags[2] == 0
    total = jnp.where(lead, other_end * own + other, own_end * other + own).astype(BF16)
    head_fresh[...] = jnp.where(lead, keep[...].astype(F32), got[...].astype(F32)).astype(BF16)
    pieces = [piece.astype(F32) for piece in parts(own_end * other_end, 3)]
    row = iota((ROWS, 128), 0)
    tail = jnp.zeros((ROWS, 128), F32)
    for p in range(3):
        for i in range(4):
            tail = jnp.where(row == 4 * p + i, pieces[p][:, i * 128 : (i + 1) * 128], tail)
    for g in range(8):
        pay[g, :, 0:LANES] = total[g * ROWS : (g + 1) * ROWS]
        pay[g, :, LANES : LANES + 128] = tail.astype(BF16)


def scan_kernel(got, start, out):
    def one(i, state):
        out[i] = state.astype(BF16)
        tail = got[i, :, LANES : LANES + 128].astype(F32)
        tail = tail[0:4] + tail[4:8] + tail[8:12]
        ends = jnp.concatenate([tail[i : i + 1] for i in range(4)], axis=1)
        return state * ends + got[i, :, 0:LANES].astype(F32)

    lax.fori_loop(0, CHIPS, one, start[...])


def start_kernel(flags, chip, head_fresh, mine, cross):
    state = jnp.concatenate([chip[g] for g in range(8)], axis=0).astype(F32)
    second = end_row(head_fresh[STATE:]) * state + head_fresh[0:STATE].astype(F32)
    lead = flags[2] == 0
    mine[...] = jnp.where(lead, state, second).astype(BF16)
    cross[...] = jnp.where(lead, second, state).astype(BF16)


def inner_kernel(u, pack, logs, partial, decay, scores, log_col, log_row, pad):
    q = pl.program_id(0)

    @pl.when(q == 0)
    def _():
        bc = pack[0:16].reshape(TOK, 256)
        scores[...] = lax.dot_general(
            bc[:, 128:256], bc[:, 0:128], (((1,), (1,)), ((), ())), preferred_element_type=F32
        )
        cum = cumulated(logs[0:HEADS])
        log_row[...] = cum * LOG2E - jnp.log2(logs[HEADS : 2 * HEADS])
        turned = twice_turned(cum)
        log_col[...] = turned * LOG2E
        decay[...] = two_parts(jnp.exp(turned))

    slab = jnp.concatenate([pack[16 + 2 * q], pack[17 + 2 * q]], axis=1).astype(F32)
    skip = slab[5:6] + slab[6:7] + slab[7:8]
    cols = pltpu.roll(log_col[...], (128 - 8 * q) % 128, 1)
    rows = log_row[pl.ds(pl.multiple_of(q * 8, 8), 8), :]
    half = TOK // 2
    causal = iota((half, half), 0) >= iota((half, half), 1)
    left = iota((TOK, 128), 1) < DIM
    for i in range(4):
        lane = slice(i * 128, (i + 1) * 128)
        value = conv_silu(pad.at[i], u[:, lane], slab[:, lane], slab[0:4, lane])
        both = []
        for h in (2 * i, 2 * i + 1):
            col = cols[:, h : h + 1]
            row = rows[h : h + 1]
            top = jnp.exp2(jnp.where(causal, col[:half] - row[:, :half], -jnp.inf)) * scores[:half, :half]
            low_left = jnp.exp2(col[half:] - row[:, :half]) * scores[half:, :half]
            low_right = jnp.exp2(jnp.where(causal, col[half:] - row[:, half:], -jnp.inf)) * scores[half:, half:]
            low = jnp.concatenate([low_left.astype(BF16), low_right.astype(BF16)], axis=1)
            both.append(jnp.concatenate([dot(top.astype(BF16), value[:half]), dot(low, value)], axis=0))
        partial[:, lane] = jnp.where(left, both[0], both[1]) + skip[:, lane] * value.astype(F32)


def outer_part(q, u, partial, starts, pack, decay, out):
    queries = pack[0:16].reshape(TOK, 256)[:, 128:256]
    carried = dot(queries, starts[...]) * dot(decay[...], spread_matrix(2 * HEADS, q))
    gain = jnp.concatenate([pack[16 + 2 * q], pack[17 + 2 * q]], axis=1).astype(F32)[4:5]
    same = (iota((128, 128), 0) // DIM == iota((128, 128), 1) // DIM).astype(F32).astype(BF16)
    for i in range(4):
        lane = slice(i * 128, (i + 1) * 128)
        result = partial[:, lane] + carried[:, lane]
        mean_sq = dot((result * result).astype(BF16), same) * (1.0 / DIM)
        normed = result * lax.rsqrt(mean_sq + 1e-05)
        out[:, lane] = (u[:, lane].astype(F32) + gain[:, lane] * normed).astype(BF16)


def outer_mine_kernel(flags, u, partial, starts, pack, decay, out):
    outer_part(flags[2] * 4 + pl.program_id(0), u, partial, starts, pack, decay, out)


def outer_other_kernel(flags, u, partial, starts, pack, decay, done, out):
    outer_part(flags[1] * 4 + pl.program_id(0), u, partial, starts, pack, decay, out)


def array(shape, dtype=BF16):
    return jax.ShapeDtypeStruct(shape, dtype)


def whole(*shape):
    return pl.BlockSpec(shape, lambda *_: (0,) * len(shape))


def half_columns(rows, which):
    return pl.BlockSpec((rows, LANES), lambda i, flags: (0, flags[which] * 4 + i))


def columns(rows):
    return pl.BlockSpec((rows, LANES), lambda i, *_: (0, i))


def call(kernel, name, out, grid, ins, outs, scratch=(), mib=16, prefetch=1, estimate=None, alias=None):
    return pl.pallas_call(
        kernel,
        out_shape=out,
        grid_spec=pltpu.PrefetchScalarGridSpec(
            num_scalar_prefetch=prefetch, grid=grid, in_specs=ins, out_specs=outs, scratch_shapes=list(scratch)
        ),
        compiler_params=params(mib),
        cost_estimate=estimate,
        input_output_aliases=alias or {},
        name=name,
    )


def exact(x):
    return lax.reduce_precision(x, 8, 7)


def per_device(
    section_in, proj_weight, conv_weight, log_decay, step_size, skip_gain, norm_gain, carry_state, carry_rows
):
    u = section_in[0]
    ctx = ("x", "z", "core")
    core = lax.axis_index("core")
    first = lax.axis_index(ctx) == 0
    flags = jnp.stack([first.astype(jnp.int32), 1 - core, core])

    def onward(value):
        return lax.ppermute(value, "section", [(i, (i + 1) % 4) for i in range(4)])

    def swapped(value):
        return lax.ppermute(value, "core", [(0, 1), (1, 0)])

    behind = lax.ppermute(u[TOK - 16 :], ctx, [(i, i + 1) for i in range(63)])
    next_u = onward(u)
    rates, steps = log_decay[0].T, step_size[0].T
    next_logs = onward(jnp.concatenate([rates, steps], axis=0))
    before = jnp.concatenate([jnp.zeros((13, CH + 256), BF16), carry_rows[0]], axis=0)
    halo = jnp.where(first, before[:, :CH], behind)
    skip = jnp.repeat(skip_gain, DIM, axis=1)
    skip_hi = exact(skip)
    skip_mid = exact(skip - skip_hi)
    skip_lo = skip - skip_hi - skip_mid
    par = jnp.concatenate(
        [conv_weight[0, :, :CH], norm_gain]
        + [piece.astype(BF16) for piece in (skip_hi, skip_mid, skip_lo)]
        + [jnp.zeros((8, CH), BF16)],
        axis=0,
    )
    vmem = pl.BlockSpec(memory_space=pltpu.VMEM)
    projected, to_end, ends = pl.pallas_call(
        project_kernel,
        out_shape=(array((TOK, 256)), array((TOK, 128)), array((ROWS, 128))),
        in_specs=[vmem] * 4,
        out_specs=[vmem] * 3,
        compiler_params=params(16),
        cost_estimate=cost(6e8, 4.5e6),
        name="project",
    )(u, proj_weight[0], rates, steps)

    pad = pltpu.VMEM((4, 272, 128), F32)
    ends_pad = whole(ROWS, 128)
    fresh_out = array((STATE + ROWS, HALF))
    send, turned, pack = call(
        send_kernel,
        "send",
        (fresh_out, array((STATE, TOK)), array((32, 16, 256))),
        (4,),
        [half_columns(TOK, 1), half_columns(16, 1), half_columns(4, 1), whole(TOK, 128), ends_pad]
        + [whole(16, CH), whole(CH, 256), whole(TOK, 256), whole(4, CH + 256), whole(16, 256), whole(16, CH)],
        [columns(STATE + ROWS), whole(STATE, TOK), whole(32, 16, 256)],
        [pad],
        mib=20,
        estimate=cost(6e8, 4.5e6, 5e5),
    )(
        flags, u, halo, conv_weight[0], to_end, ends, halo, proj_weight[0], projected, conv_weight[0],
        before[:, CH:], par,
    )
    got = swapped(send)
    keep = call(
        keep_kernel,
        "keep",
        fresh_out,
        (4,),
        [half_columns(TOK, 2), half_columns(16, 2), half_columns(4, 2), whole(TOK, 128), ends_pad, whole(STATE, TOK)],
        columns(STATE + ROWS),
        [pad],
        estimate=cost(6e8, 4.5e6, 5e5),
    )(flags, u, halo, conv_weight[0], to_end, ends, turned)
    pay, head_fresh = call(
        join_kernel,
        "join",
        (array((CHIPS, ROWS, LANES + 128)), fresh_out),
        (4,),
        [columns(STATE + ROWS)] * 2,
        [pl.BlockSpec((8, ROWS, LANES + 128), lambda i, *_: (i, 0, 0)), columns(STATE + ROWS)],
        estimate=cost(1e6, 2.5e6),
    )(flags, keep, got)
    shares = lax.all_to_all(pay, ("x", "z"), 0, 0)
    next_pack = onward(pack)
    next_fresh = onward(head_fresh)
    head = (core * 4 + lax.axis_index("x")) * 8
    start = lax.dynamic_slice(carry_state[0], (head, lax.axis_index("z") * ROWS, 0), (8, ROWS, DIM))
    start = start.transpose(1, 0, 2).reshape(ROWS, LANES)
    back = pl.pallas_call(
        scan_kernel,
        out_shape=array((CHIPS, ROWS, LANES)),
        in_specs=[vmem] * 2,
        out_specs=vmem,
        compiler_params=params(8),
        name="scan",
    )(shares, start)
    chip = lax.all_to_all(back, ("x", "z"), 0, 0)
    partial, decay = call(
        inner_kernel,
        "inner",
        (array((TOK, CH), F32), array((TOK, 128))),
        (GROUPS,),
        [columns(TOK), whole(32, 16, 256), whole(128, TOK)],
        [columns(TOK), whole(TOK, 128)],
        [pltpu.VMEM((TOK, TOK), F32), pltpu.VMEM((TOK, 128), F32), pltpu.VMEM((HEADS, TOK), F32), pad],
        mib=20,
        prefetch=0,
        estimate=cost(6e9, 9e6, 4e6),
    )(next_u, next_pack, next_logs)
    next_chip = onward(chip)
    state_half = array((STATE, HALF))
    mine, cross = call(
        start_kernel,
        "start",
        (state_half, state_half),
        (4,),
        [pl.BlockSpec((8, ROWS, LANES), lambda i, *_: (i, 0, 0)), columns(STATE + ROWS)],
        [columns(STATE)] * 2,
    )(flags, next_chip, next_fresh)
    other = swapped(cross)
    outer_in = [columns(STATE), whole(32, 16, 256), whole(TOK, 128)]
    rows = call(
        outer_mine_kernel,
        "outer_mine",
        array((TOK, CH)),
        (4,),
        [half_columns(TOK, 2), half_columns(TOK, 2)] + outer_in,
        half_columns(TOK, 2),
        estimate=cost(6e8, 5e6),
    )(flags, next_u, partial, mine, next_pack, decay)
    rows = call(
        outer_other_kernel,
        "outer_other",
        array((TOK, CH)),
        (4,),
        [half_columns(TOK, 1), half_columns(TOK, 1)] + outer_in + [pl.BlockSpec(memory_space=pl.ANY)],
        half_columns(TOK, 1),
        estimate=cost(6e8, 5e6),
        alias={6: 0},
    )(flags, next_u, partial, other, next_pack, decay, rows)
    return rows[None]


def solution(mesh):
    split = Mesh(mesh.devices.reshape(4, 4, 8, 2), ("section", "x", "z", "core"))
    tokens = P("section", ("x", "z", "core"), None)
    layer = P("section", None, None)
    return jax.shard_map(
        per_device,
        mesh=split,
        in_specs=(
            tokens,
            layer,
            layer,
            tokens,
            tokens,
            P("section", None),
            P("section", None),
            P("section", None, None, None),
            layer,
        ),
        out_specs=tokens,
        check_vma=False,
    )
```

time: 169 us -> 136 us (0.80)
  waiting for transfers between devices: 107 us -> 58.7 us
  starting transfers between devices: 23.5 us -> 32.8 us
  Pallas kernels: 24.7 us -> 30.6 us
    all_to_all x2, waiting for transfers between devices: 59.4 us -> 26.3 us  [the longest x1 13.6 us: per_device(): shares = lax.all_to_all(pay, ('x', 'z'), 0, 0)]
    ppermute x2 -> x8, waiting for transfers between devices: 47.4 us -> 32.4 us  [the longest x5 32.4 us: onward(): return lax.ppermute(value, 'section', [(i, (i + 1) % 4) for i in range(4)])]
    ppermute x2 -> x8, starting transfers between devices: 6.25 us -> 14.3 us  [the longest x5 6.42 us: onward(): return lax.ppermute(value, 'section', [(i, (i + 1) % 4) for i in range(4)])]
    pallas_call x3 -> x9, Pallas kernels: 24.7 us -> 30.6 us  [the longest x1 8.69 us: per_device(): call(inner_kernel, 'inner', (array((TOK, CH), F32), array((TOK, 128))), (...]
    unnamed x11 -> x26, local copies, waits for them, and re-layouts: 6.6 us -> 8.06 us
  transfers between devices with their start and end apart: 4 -> 10, of which waited for: 3 -> 5; matrix products, arithmetic and copies ran while one was open for 5% -> 3% of each run, Pallas kernels for 0% -> 15%
where the time goes in v2:
time: 136 us; the launch traced here: 135 us
  waiting for transfers between devices  58.7 us (43%)
  starting transfers between devices  32.8 us (24%)
  Pallas kernels  30.6 us (22%)
  local copies, waits for them, and re-layouts  12.7 us (9%)
    ppermute x5, waiting for transfers between devices, onward(): return lax.ppermute(value, 'section', [(i, (i + 1) % 4) for i in range(4)])  32.4 us
    all_to_all x1, waiting for transfers between devices, per_device(): shares = lax.all_to_all(pay, ('x', 'z'), 0, 0)  13.6 us
    all_to_all x1, waiting for transfers between devices, per_device(): chip = lax.all_to_all(back, ('x', 'z'), 0, 0)  12.7 us
    all_to_all x1, starting transfers between devices, per_device(): shares = lax.all_to_all(pay, ('x', 'z'), 0, 0)  10.3 us
    pallas_call x1, Pallas kernels, per_device(): call(inner_kernel, 'inner', (array((TOK, CH), F32), array((TOK, 128))), (...  8.69 us
    all_to_all x1, starting transfers between devices, per_device(): chip = lax.all_to_all(back, ('x', 'z'), 0, 0)  8.23 us
    unnamed x26, local copies, waits for them, and re-layouts  8.06 us
    ppermute x5, starting transfers between devices, onward(): return lax.ppermute(value, 'section', [(i, (i + 1) % 4) for i in range(4)])  6.42 us
  transfers between devices with their start and end apart: 10, of which 5 were waited for; matrix products, arithmetic and copies ran while one was open for 3% of the time, Pallas kernels for 15%

profile of v2, /device:TPU:1, one launch (start us, length us, event | category | flops | bytes accessed | tf_op | source)
XLA Modules:
  0.0 135.2 jit_solution(18374691149777551285)
XLA Ops:
  1.1 4.9 %collective-permute-start.1 = (bf16[16,4096]{1,0:T(8,128)(2,1)S(1)}, bf16[16,4096]{1,0:T(8,128)(2,1)S(1)}, u32[]{:S(2)}, u32[]{:S(2)}) collective-permute-start(bf16[16,4096]{1,0:T(8,128)(2,1)S(1)} %slice_bitcast_fusion), channel_id=1, source_target_pairs={{0,1},{1,2},{2,3},{3,4},{4,5},{5,6},{6,7},{7,8},{8,9},{9,10},{10,1... | collective-permute-start | bytes 393224 | tf_op jit(solution)/shard_map/ppermute | solution.py:281
  7.8 1.6 %copy-done.1 = bf16[1,256,4096]{2,1,0:T(8,128)(2,1)S(1)} copy-done((bf16[1,256,4096]{2,1,0:T(8,128)(2,1)S(1)}, bf16[1,256,4096]{2,1,0:T(8,128)(2,1)}, u32[]{:S(2)}) %copy-start.1) | copy-done | bytes 2097176
  9.4 1.6 %copy-done.3 = bf16[1,4096,256]{2,1,0:T(8,128)(2,1)S(1)} copy-done((bf16[1,4096,256]{2,1,0:T(8,128)(2,1)S(1)}, bf16[1,4096,256]{2,1,0:T(8,128)(2,1)}, u32[]{:S(2)}) %copy-start.3) | copy-done | bytes 2097176
  13.8 1.6 %copy-done.2 = bf16[1,256,4096]{2,1,0:T(8,128)(2,1)S(1)} copy-done((bf16[1,256,4096]{2,1,0:T(8,128)(2,1)S(1)}, bf16[1,256,4096]{2,1,0:T(8,128)(2,1)}, u32[]{:S(2)}) %copy-start.2) | copy-done | bytes 2097176
  15.4 1.6 %copy-done.4 = bf16[1,4096,256]{2,1,0:T(8,128)(2,1)S(1)} copy-done((bf16[1,4096,256]{2,1,0:T(8,128)(2,1)S(1)}, bf16[1,4096,256]{2,1,0:T(8,128)(2,1)}, u32[]{:S(2)}) %copy-start.4) | copy-done | bytes 2097176
  17.0 3.7 %send.1 = (bf16[144,2048]{1,0:T(8,128)(2,1)S(1)}, bf16[128,256]{1,0:T(8,128)(2,1)S(1)}, bf16[32,16,256]{2,1,0:T(8,128)(2,1)S(1)}) custom-call(s32[3]{0:T(128)S(1)} %pad_add_fusion.flags, bf16[256,4096]{1,0:T(8,128)(2,1)S(1)} %bitcast.27, bf16[16,4096]{1,0:T(8,128)(2,1)S(1)} %fusion.halo.all_halo, bf16[4,4352]{1,0:T(4,128)(2,1)S(1)} %bitcast.31, ...), custom_call_target="tpu_custom_call" | custom-call | flops 600000000 | bytes 4500000 | tf_op jit(solution)/shard_map/send/pallas_call | solution.py:311
  20.8 3.1 %keep.1 = bf16[144,2048]{1,0:T(8,128)(2,1)S(1)} custom-call(s32[3]{0:T(128)S(1)} %pad_add_fusion.flags, bf16[256,4096]{1,0:T(8,128)(2,1)S(1)} %bitcast.28, bf16[16,4096]{1,0:T(8,128)(2,1)S(1)} %fusion.halo.all_halo, bf16[4,4352]{1,0:T(4,128)(2,1)S(1)} %bitcast.33, bf16[256,128]{1,0:T(8,128)(2,1)S(1)} %get-tuple-element.17.to_end, ...), custom_call_target="tpu_custom_call" | custom-call | flops 600000000 | bytes 4500000 | tf_op jit(solution)/shard_map/keep/pallas_call | solution.py:327
  23.9 2.3 %join.1 = (bf16[32,16,640]{2,1,0:T(8,128)(2,1)}, bf16[144,2048]{1,0:T(8,128)(2,1)S(1)}) custom-call(s32[3]{0:T(128)S(1)} %pad_add_fusion.flags, bf16[144,2048]{1,0:T(8,128)(2,1)S(1)} %keep.1, bf16[144,2048]{1,0:T(8,128)(2,1)S(1)} %collective-permute-done.4.got), custom_call_target="tpu_custom_call" | custom-call | flops 1000000 | bytes 2500000 | tf_op jit(solution)/shard_map/join/pallas_call | solution.py:337
  26.2 10.3 %all-to-all-start = ((bf16[32,16,640]{2,1,0:T(8,128)(2,1)}), bf16[32,16,640]{2,1,0:T(8,128)(2,1)S(1)}, u32[]{:S(2)}, u32[]{:S(2)}) async-start(bf16[32,16,640]{2,1,0:T(8,128)(2,1)} %get-tuple-element.24), calls=%async_computation | async-start | bytes 1310720 | tf_op jit(solution)/shard_map/all_to_all | solution.py:346
  36.5 1.4 %collective-permute-start = (bf16[256,4096]{1,0:T(8,128)(2,1)}, bf16[256,4096]{1,0:T(8,128)(2,1)}, u32[]{:S(2)}, u32[]{:S(2)}) collective-permute-start(bf16[256,4096]{1,0:T(8,128)(2,1)} %bitcast.25), channel_id=1, source_target_pairs={{0,64},{64,128},{128,192},{192,0},{1,65},{65,129},{129,193},{193,1... | collective-permute-start | bytes 6291464 | tf_op jit(solution)/shard_map/ppermute | solution.py:276
  39.7 13.6 %all-to-all-done.got = bf16[32,16,640]{2,1,0:T(8,128)(2,1)S(1)} async-done(((bf16[32,16,640]{2,1,0:T(8,128)(2,1)}), bf16[32,16,640]{2,1,0:T(8,128)(2,1)S(1)}, u32[]{:S(2)}, u32[]{:S(2)}) %all-to-all-start) | async-done | bytes 655392 | tf_op jit(solution)/shard_map/all_to_all | solution.py:346
  53.3 1.1 scan.1
  54.5 8.2 %all-to-all-start.1 = ((bf16[32,16,512]{2,1,0:T(8,128)(2,1)}), bf16[32,16,512]{2,1,0:T(8,128)(2,1)}, u32[]{:S(2)}, u32[]{:S(2)}) async-start(bf16[32,16,512]{2,1,0:T(8,128)(2,1)} %scan.1), calls=%async_computation.1 | async-start | bytes 1048576 | tf_op jit(solution)/shard_map/all_to_all | solution.py:360
  62.7 1.4 %collective-permute-start.6 = (bf16[144,2048]{1,0:T(8,128)(2,1)S(1)}, bf16[144,2048]{1,0:T(8,128)(2,1)S(1)}, u32[]{:S(2)}, u32[]{:S(2)}) collective-permute-start(bf16[144,2048]{1,0:T(8,128)(2,1)S(1)} %get-tuple-element.25), channel_id=1, source_target_pairs={{0,64},{64,128},{128,192},{192,0},{1,65},{65,129},{129,193},{193,1... | collective-permute-start | bytes 1769480 | tf_op jit(solution)/shard_map/ppermute | solution.py:276
  64.1 12.7 %all-to-all-done.1 = bf16[32,16,512]{2,1,0:T(8,128)(2,1)} async-done(((bf16[32,16,512]{2,1,0:T(8,128)(2,1)}), bf16[32,16,512]{2,1,0:T(8,128)(2,1)}, u32[]{:S(2)}, u32[]{:S(2)}) %all-to-all-start.1) | async-done | bytes 524320 | tf_op jit(solution)/shard_map/all_to_all | solution.py:360
  76.8 1.3 collective-permute-start.5
  78.1 1.3 collective-permute-start.2
  80.5 16.6 %collective-permute-done.6.head_fresh = bf16[144,2048]{1,0:T(8,128)(2,1)S(1)} collective-permute-done((bf16[144,2048]{1,0:T(8,128)(2,1)S(1)}, bf16[144,2048]{1,0:T(8,128)(2,1)S(1)}, u32[]{:S(2)}, u32[]{:S(2)}) %collective-permute-start.6) | collective-permute-done | bytes 589856 | tf_op jit(solution)/shard_map/ppermute | solution.py:276
  97.1 11.2 %collective-permute-done.5.chip = bf16[32,16,512]{2,1,0:T(8,128)(2,1)S(1)} collective-permute-done((bf16[32,16,512]{2,1,0:T(8,128)(2,1)}, bf16[32,16,512]{2,1,0:T(8,128)(2,1)S(1)}, u32[]{:S(2)}, u32[]{:S(2)}) %collective-permute-start.5) | collective-permute-done | bytes 524320 | tf_op jit(solution)/shard_map/ppermute | solution.py:276
  109.4 2.9 %collective-permute-start.7 = (bf16[128,2048]{1,0:T(8,128)(2,1)S(1)}, bf16[128,2048]{1,0:T(8,128)(2,1)S(1)}, u32[]{:S(2)}, u32[]{:S(2)}) collective-permute-start(bf16[128,2048]{1,0:T(8,128)(2,1)S(1)} %get-tuple-element.26), channel_id=1, source_target_pairs={{0,1},{1,0},{2,3},{3,2},{4,5},{5,4},{6,7},{7,6},{8,9},{9,8},{10,11... | collective-permute-start | bytes 1572872 | tf_op jit(solution)/shard_map/ppermute | solution.py:279
  112.3 4.5 %collective-permute-done.3.logs = f32[128,256]{1,0:T(8,128)S(1)} collective-permute-done((f32[128,256]{1,0:T(8,128)S(1)}, f32[128,256]{1,0:T(8,128)S(1)}, u32[]{:S(2)}, u32[]{:S(2)}) %collective-permute-start.3) | collective-permute-done | bytes 131104 | tf_op jit(solution)/shard_map/ppermute | solution.py:276
  116.8 8.7 %inner.1 = (f32[256,4096]{1,0:T(8,128)S(1)}, bf16[256,128]{1,0:T(8,128)(2,1)S(1)}) custom-call(bf16[256,4096]{1,0:T(8,128)(2,1)} %collective-permute-done.u, bf16[32,16,256]{2,1,0:T(8,128)(2,1)S(1)} %collective-permute-done.2.pack, f32[128,256]{1,0:T(8,128)S(1)} %collective-permute-done.3.logs), custom_call_target="tpu_custom_call" | custom-call | flops 6000000000 | bytes 9000000 | tf_op jit(solution)/shard_map/inner/pallas_call | solution.py:361
  125.5 4.9 %outer_mine.1.done = bf16[256,4096]{1,0:T(8,128)(2,1)} custom-call(s32[3]{0:T(128)S(1)} %pad_add_fusion.flags, bf16[256,4096]{1,0:T(8,128)(2,1)} %collective-permute-done.u, f32[256,4096]{1,0:T(8,128)S(1)} %get-tuple-element.21.partial, bf16[128,2048]{1,0:T(8,128)(2,1)S(1)} %get-tuple-element.28.starts, ...), custom_call_target="tpu_custom_call" | custom-call | flops 600000000 | bytes 5000000 | tf_op jit(solution)/shard_map/outer_mine/pallas_call | solution.py:385
  130.4 4.9 %outer_other.1 = bf16[256,4096]{1,0:T(8,128)(2,1)} custom-call(s32[3]{0:T(128)S(1)} %pad_add_fusion.flags, bf16[256,4096]{1,0:T(8,128)(2,1)} %collective-permute-done.u, f32[256,4096]{1,0:T(8,128)S(1)} %get-tuple-element.21.partial, bf16[128,2048]{1,0:T(8,128)(2,1)S(1)} %collective-permute-done.7.starts, ...), custom_call_target="tpu_custom_call", output_to_operand_aliasing={{}: (6, {})} | custom-call | flops 600000000 | bytes 5000000 | tf_op jit(solution)/shard_map/outer_other/pallas_call | solution.py:394
  (44 shorter events, 9.7 us)
Async XLA Ops:
  0.0 37.8 %copy-start = (f32[1,64,128,64]{2,3,1,0:T(8,128)S(1)}, f32[1,64,128,64]{2,3,1,0:T(8,128)}, u32[]{:S(2)}) copy-start(f32[1,64,128,64]{2,3,1,0:T(8,128)} %param.16) | copy-start | bytes 6291460
  1.1 12.6 %collective-permute-start.1 = (bf16[16,4096]{1,0:T(8,128)(2,1)S(1)}, bf16[16,4096]{1,0:T(8,128)(2,1)S(1)}, u32[]{:S(2)}, u32[]{:S(2)}) collective-permute-start(bf16[16,4096]{1,0:T(8,128)(2,1)S(1)} %slice_bitcast_fusion), channel_id=1, source_target_pairs={{0,1},{1,2},{2,3},{3,4},{4,5},{5,6},{6,7},{7,8},{8,9},{9,10},{10,1... | collective-permute-start | bytes 393224 | tf_op jit(solution)/shard_map/ppermute | solution.py:281
  7.8 1.6 %copy-start.1 = (bf16[1,256,4096]{2,1,0:T(8,128)(2,1)S(1)}, bf16[1,256,4096]{2,1,0:T(8,128)(2,1)}, u32[]{:S(2)}) copy-start(bf16[1,256,4096]{2,1,0:T(8,128)(2,1)} %param.9) | copy-start | bytes 6291460
  9.4 1.6 %copy-start.3 = (bf16[1,4096,256]{2,1,0:T(8,128)(2,1)S(1)}, bf16[1,4096,256]{2,1,0:T(8,128)(2,1)}, u32[]{:S(2)}) copy-start(bf16[1,4096,256]{2,1,0:T(8,128)(2,1)} %param.10) | copy-start | bytes 6291460
  10.9 0.8 copy-start.6
  11.8 0.8 copy-start.8
  12.6 0.9 copy-start.12
  12.6 1.1 copy-start.11
  12.6 1.1 copy-start.5
  13.8 1.6 %copy-start.2 = (bf16[1,256,4096]{2,1,0:T(8,128)(2,1)S(1)}, bf16[1,256,4096]{2,1,0:T(8,128)(2,1)}, u32[]{:S(2)}) copy-start(bf16[1,256,4096]{2,1,0:T(8,128)(2,1)} %param.9) | copy-start | bytes 6291460
  15.4 1.6 %copy-start.4 = (bf16[1,4096,256]{2,1,0:T(8,128)(2,1)S(1)}, bf16[1,4096,256]{2,1,0:T(8,128)(2,1)}, u32[]{:S(2)}) copy-start(bf16[1,4096,256]{2,1,0:T(8,128)(2,1)} %param.10) | copy-start | bytes 6291460
  20.7 5.5 %copy-start.10 = (bf16[32,16,256]{2,1,0:T(8,128)(2,1)}, bf16[32,16,256]{2,1,0:T(8,128)(2,1)S(1)}, u32[]{:S(2)}) copy-start(bf16[32,16,256]{2,1,0:T(8,128)(2,1)S(1)} %get-tuple-element.20) | copy-start | bytes 786436
  20.7 3.2 %collective-permute-start.4 = (bf16[144,2048]{1,0:T(8,128)(2,1)S(1)}, bf16[144,2048]{1,0:T(8,128)(2,1)S(1)}, u32[]{:S(2)}, u32[]{:S(2)}) collective-permute-start(bf16[144,2048]{1,0:T(8,128)(2,1)S(1)} %get-tuple-element.23), channel_id=1, source_target_pairs={{0,1},{1,0},{2,3},{3,2},{4,5},{5,4},{6,7},{7,6},{8,9},{9,8},{10,11... | collective-permute-start | bytes 1769480 | tf_op jit(solution)/shard_map/ppermute | solution.py:279
  26.2 53.2 %copy-start.7 = (f32[1,256,64]{1,2,0:T(8,128)S(1)}, f32[1,256,64]{1,2,0:T(8,128)}, u32[]{:S(2)}) copy-start(f32[1,256,64]{1,2,0:T(8,128)} %param.12) | copy-start | bytes 196612
  26.2 53.2 %copy-start.9 = (f32[1,256,64]{1,2,0:T(8,128)S(1)}, f32[1,256,64]{1,2,0:T(8,128)}, u32[]{:S(2)}) copy-start(f32[1,256,64]{1,2,0:T(8,128)} %param.13) | copy-start | bytes 196612
  26.2 27.2 %all-to-all-start = ((bf16[32,16,640]{2,1,0:T(8,128)(2,1)}), bf16[32,16,640]{2,1,0:T(8,128)(2,1)S(1)}, u32[]{:S(2)}, u32[]{:S(2)}) async-start(bf16[32,16,640]{2,1,0:T(8,128)(2,1)} %get-tuple-element.24), calls=%async_computation | async-start | bytes 1310720 | tf_op jit(solution)/shard_map/all_to_all | solution.py:346
  36.5 80.3 %collective-permute-start = (bf16[256,4096]{1,0:T(8,128)(2,1)}, bf16[256,4096]{1,0:T(8,128)(2,1)}, u32[]{:S(2)}, u32[]{:S(2)}) collective-permute-start(bf16[256,4096]{1,0:T(8,128)(2,1)} %bitcast.25), channel_id=1, source_target_pairs={{0,64},{64,128},{128,192},{192,0},{1,65},{65,129},{129,193},{193,1... | collective-permute-start | bytes 6291464 | tf_op jit(solution)/shard_map/ppermute | solution.py:276
  54.5 22.3 %all-to-all-start.1 = ((bf16[32,16,512]{2,1,0:T(8,128)(2,1)}), bf16[32,16,512]{2,1,0:T(8,128)(2,1)}, u32[]{:S(2)}, u32[]{:S(2)}) async-start(bf16[32,16,512]{2,1,0:T(8,128)(2,1)} %scan.1), calls=%async_computation.1 | async-start | bytes 1048576 | tf_op jit(solution)/shard_map/all_to_all | solution.py:360
  62.7 34.4 %collective-permute-start.6 = (bf16[144,2048]{1,0:T(8,128)(2,1)S(1)}, bf16[144,2048]{1,0:T(8,128)(2,1)S(1)}, u32[]{:S(2)}, u32[]{:S(2)}) collective-permute-start(bf16[144,2048]{1,0:T(8,128)(2,1)S(1)} %get-tuple-element.25), channel_id=1, source_target_pairs={{0,64},{64,128},{128,192},{192,0},{1,65},{65,129},{129,193},{193,1... | collective-permute-start | bytes 1769480 | tf_op jit(solution)/shard_map/ppermute | solution.py:276
  76.8 31.6 %collective-permute-start.5 = (bf16[32,16,512]{2,1,0:T(8,128)(2,1)}, bf16[32,16,512]{2,1,0:T(8,128)(2,1)S(1)}, u32[]{:S(2)}, u32[]{:S(2)}) collective-permute-start(bf16[32,16,512]{2,1,0:T(8,128)(2,1)} %all-to-all-done.1), channel_id=1, source_target_pairs={{0,64},{64,128},{128,192},{192,0},{1,65},{65,129},{129,193},{193,1... | collective-permute-start | bytes 1572872 | tf_op jit(solution)/shard_map/ppermute | solution.py:276
  78.1 38.7 %collective-permute-start.2 = (bf16[32,16,256]{2,1,0:T(8,128)(2,1)}, bf16[32,16,256]{2,1,0:T(8,128)(2,1)S(1)}, u32[]{:S(2)}, u32[]{:S(2)}) collective-permute-start(bf16[32,16,256]{2,1,0:T(8,128)(2,1)} %copy-done.10), channel_id=1, source_target_pairs={{0,64},{64,128},{128,192},{192,0},{1,65},{65,129},{129,193},{193,1... | collective-permute-start | bytes 786440 | tf_op jit(solution)/shard_map/ppermute | solution.py:276
  79.4 37.4 %collective-permute-start.3 = (f32[128,256]{1,0:T(8,128)S(1)}, f32[128,256]{1,0:T(8,128)S(1)}, u32[]{:S(2)}, u32[]{:S(2)}) collective-permute-start(f32[128,256]{1,0:T(8,128)S(1)} %pad_maximum_fusion), channel_id=1, source_target_pairs={{0,64},{64,128},{128,192},{192,0},{1,65},{65,129},{129,193},{193,1... | collective-permute-start | bytes 393224 | tf_op jit(solution)/shard_map/ppermute | solution.py:276
  109.4 21.0 %collective-permute-start.7 = (bf16[128,2048]{1,0:T(8,128)(2,1)S(1)}, bf16[128,2048]{1,0:T(8,128)(2,1)S(1)}, u32[]{:S(2)}, u32[]{:S(2)}) collective-permute-start(bf16[128,2048]{1,0:T(8,128)(2,1)S(1)} %get-tuple-element.26), channel_id=1, source_target_pairs={{0,1},{1,0},{2,3},{3,2},{4,5},{5,4},{6,7},{7,6},{8,9},{9,8},{10,11... | collective-permute-start | bytes 1572872 | tf_op jit(solution)/shard_map/ppermute | solution.py:279

commit v3 on v2

--- a/solution.py
+++ b/solution.py
@@ -14,6 +14,7 @@
 TOK = 256
 CH = 4096
 HALF = CH // 2
+WIDE = 1024
 LANES = 512
 GROUPS = 8
 ROWS = 16
@@ -64,7 +65,8 @@
     total = taps[0:1] * pad[13:269, :]
     for j in range(1, 4):
         total = total + taps[j : j + 1] * pad[13 + j : 269 + j, :]
-    return (total / (1.0 + jnp.exp(-total))).astype(BF16)
+    half = 0.5 * total
+    return (half + half * jnp.tanh(half)).astype(BF16)
 
 
 def cumulated(rates):
@@ -76,20 +78,37 @@
     return jnp.concatenate([x, x], axis=0).T
 
 
-def project_kernel(u, weight, rates, steps, projected, to_end, ends):
-    projected[...] = dot(u[...], weight[...]).astype(BF16)
-    cum = twice_turned(cumulated(rates[...]))
+def end_factors(cum, steps):
     last = cum[TOK - 1 : TOK]
-    to_end[...] = two_parts(jnp.exp(last - cum) * twice_turned(steps[...]))
     hi, mid, lo = (piece.astype(F32) for piece in parts(jnp.exp(last), 3))
     kind = iota((ROWS, 128), 0) // 4
     tile = jnp.where(kind == 0, hi, jnp.where(kind == 1, mid, jnp.where(kind == 2, lo, 0.0)))
-    ends[...] = jnp.where(iota((ROWS, 128), 1) < HEADS, tile, 0.0).astype(BF16)
-
-
-def fresh_part(q, u, halo, taps, to_end, ends, turned, fresh, pad):
+    ends = jnp.where(iota((ROWS, 128), 1) < HEADS, tile, 0.0).astype(BF16)
+    return two_parts(jnp.exp(last - cum) * steps), ends
+
+
+def project_kernel(u, weight, rates, steps, projected, to_end, ends, edge, total):
+    step = pl.program_id(0)
+
+    @pl.when(step == 0)
+    def _():
+        total[...] = jnp.zeros_like(total)
+        to_end[...], ends[...] = end_factors(twice_turned(cumulated(rates[...])), twice_turned(steps[...]))
+
+    edge[:, pl.ds(pl.multiple_of(step * 1024, 1024), 1024)] = u[TOK - 16 : TOK]
+    total[...] += dot(u[...], weight[...])
+
+    @pl.when(step == 3)
+    def _():
+        rounded = total[...].astype(BF16)
+        projected[...] = rounded
+        edge[:, CH:] = rounded[TOK - 16 : TOK]
+
+
+def fresh_part(q, first, u, behind, before, taps, to_end, ends, turned, fresh, pad):
     spread = spread_matrix(2 * HEADS, q)
     scale = dot(to_end[...], spread)
+    halo = jnp.where(first == 1, before[...].astype(F32), behind[...].astype(F32))
     scaled = []
     for i in range(4):
         lane = slice(i * 128, (i + 1) * 128)
@@ -100,34 +119,32 @@
 
 
 def send_kernel(
-    flags, u, halo, taps, to_end, ends, all_halo, weight, projected, all_taps, carried_bc, par, fresh, turned, pack, pad
+    flags, u, behind, before, taps, to_end, ends, all_behind, all_before, projected, all_taps, par, fresh, turned, pack, pad
 ):
     step = pl.program_id(0)
 
     @pl.when(step == 0)
     def _():
-        near = dot(all_halo[...], weight[...]).astype(BF16).astype(F32)
-        near = jnp.where(flags[0] == 1, carried_bc[...].astype(F32), near)
+        near = jnp.where(flags[0] == 1, all_before[...].astype(F32), all_behind[...].astype(F32))
         acts = []
         for i in range(2):
-            lane = slice(i * 128, (i + 1) * 128)
-            tap = all_taps[:, CH + i * 128 : CH + (i + 1) * 128].astype(F32)
-            acts.append(conv_silu(pad.at[i], projected[:, lane], near[:, lane], tap))
+            lane = slice(CH + i * 128, CH + (i + 1) * 128)
+            value = projected[:, i * 128 : (i + 1) * 128]
+            acts.append(conv_silu(pad.at[i], value, near[:, lane], all_taps[:, lane].astype(F32)))
         turned[...] = acts[0].astype(F32).T.astype(BF16)
         for s in range(16):
             for i in range(2):
                 pack[s, :, i * 128 : (i + 1) * 128] = acts[i][s * 16 : (s + 1) * 16]
             lane = slice(s * 256, (s + 1) * 256)
-            slab = jnp.where(
-                iota((16, 256), 0) >= 13, all_halo[:, lane].astype(F32), par[:, lane].astype(F32)
-            )
+            slab = jnp.where(iota((16, 256), 0) >= 13, near[:, lane], par[:, lane].astype(F32))
             pack[16 + s] = slab.astype(BF16)
 
-    fresh_part(flags[1] * 4 + step, u, halo, taps, to_end, ends, turned, fresh, pad)
-
-
-def keep_kernel(flags, u, halo, taps, to_end, ends, turned, fresh, pad):
-    fresh_part(flags[2] * 4 + pl.program_id(0), u, halo, taps, to_end, ends, turned, fresh, pad)
+    fresh_part(flags[1] * 4 + step, flags[0], u, behind, before, taps, to_end, ends, turned, fresh, pad)
+
+
+def keep_kernel(flags, u, behind, before, taps, to_end, ends, turned, fresh, pad):
+    q = flags[2] * 4 + pl.program_id(0)
+    fresh_part(q, flags[0], u, behind, before, taps, to_end, ends, turned, fresh, pad)
 
 
 def end_row(tail):
@@ -135,12 +152,11 @@
     return tail[0:1] + tail[4:5] + tail[8:9]
 
 
-def join_kernel(flags, keep, got, pay, head_fresh):
+def join_kernel(flags, keep, got, pay):
     own, other = keep[0:STATE].astype(F32), got[0:STATE].astype(F32)
     own_end, other_end = end_row(keep[STATE:]), end_row(got[STATE:])
     lead = flags[2] == 0
     total = jnp.where(lead, other_end * own + other, own_end * other + own).astype(BF16)
-    head_fresh[...] = jnp.where(lead, keep[...].astype(F32), got[...].astype(F32)).astype(BF16)
     pieces = [piece.astype(F32) for piece in parts(own_end * other_end, 3)]
     row = iota((ROWS, 128), 0)
     tail = jnp.zeros((ROWS, 128), F32)
@@ -163,15 +179,18 @@
     lax.fori_loop(0, CHIPS, one, start[...])
 
 
-def start_kernel(flags, chip, head_fresh, mine, cross):
+def start_kernel(flags, chip, low_fresh, lead_fresh, mine, cross):
     state = jnp.concatenate([chip[g] for g in range(8)], axis=0).astype(F32)
-    second = end_row(head_fresh[STATE:]) * state + head_fresh[0:STATE].astype(F32)
     lead = flags[2] == 0
+    fresh = jnp.where(lead, low_fresh[...].astype(F32), lead_fresh[...].astype(F32))
+    second = end_row(fresh[STATE:]) * state + fresh[0:STATE]
     mine[...] = jnp.where(lead, state, second).astype(BF16)
     cross[...] = jnp.where(lead, second, state).astype(BF16)
 
 
-def inner_kernel(u, pack, logs, partial, decay, scores, log_col, log_row, pad):
+def inner_kernel(
+    u, pack, logs, partial, decay, low_fresh, high_fresh, scores, log_col, log_row, turned_keys, to_end, ends, pad
+):
     q = pl.program_id(0)
 
     @pl.when(q == 0)
@@ -185,9 +204,14 @@
         turned = twice_turned(cum)
         log_col[...] = turned * LOG2E
         decay[...] = two_parts(jnp.exp(turned))
+        turned_keys[...] = bc[:, 0:128].astype(F32).T.astype(BF16)
+        to_end[...], ends[...] = end_factors(turned, twice_turned(logs[HEADS : 2 * HEADS]))
 
     slab = jnp.concatenate([pack[16 + 2 * q], pack[17 + 2 * q]], axis=1).astype(F32)
     skip = slab[5:6] + slab[6:7] + slab[7:8]
+    spread = spread_matrix(2 * HEADS, q)
+    scale = dot(to_end[...], spread)
+    scaled = []
     cols = pltpu.roll(log_col[...], (128 - 8 * q) % 128, 1)
     rows = log_row[pl.ds(pl.multiple_of(q * 8, 8), 8), :]
     half = TOK // 2
@@ -196,6 +220,7 @@
     for i in range(4):
         lane = slice(i * 128, (i + 1) * 128)
         value = conv_silu(pad.at[i], u[:, lane], slab[:, lane], slab[0:4, lane])
+        scaled.append((value.astype(F32) * scale[:, lane]).astype(BF16))
         both = []
         for h in (2 * i, 2 * i + 1):
             col = cols[:, h : h + 1]
@@ -206,14 +231,34 @@
             low = jnp.concatenate([low_left.astype(BF16), low_right.astype(BF16)], axis=1)
             both.append(jnp.concatenate([dot(top.astype(BF16), value[:half]), dot(low, value)], axis=0))
         partial[:, lane] = jnp.where(left, both[0], both[1]) + skip[:, lane] * value.astype(F32)
-
-
-def outer_part(q, u, partial, starts, pack, decay, out):
+    fresh = dot(turned_keys[...], jnp.concatenate(scaled, axis=1)).astype(BF16)
+    end_rows = dot(ends[...], spread).astype(BF16)
+
+    @pl.when(q < 4)
+    def _():
+        low_fresh[0:STATE, :] = fresh
+        low_fresh[STATE:, :] = end_rows
+
+    @pl.when(q >= 4)
+    def _():
+        high_fresh[0:STATE, :] = fresh
+        high_fresh[STATE:, :] = end_rows
+
+
+def mark_kernel(*refs):
+    pass
+
+
+def outer_part(half, u, partial, starts, pack, decay, out):
+    step = pl.program_id(0)
     queries = pack[0:16].reshape(TOK, 256)[:, 128:256]
-    carried = dot(queries, starts[...]) * dot(decay[...], spread_matrix(2 * HEADS, q))
-    gain = jnp.concatenate([pack[16 + 2 * q], pack[17 + 2 * q]], axis=1).astype(F32)[4:5]
+    head = iota((2 * HEADS, WIDE), 1) // DIM + (half * 2 + step) * (WIDE // DIM)
+    spread = (iota((2 * HEADS, WIDE), 0) % HEADS == head).astype(F32).astype(BF16)
+    carried = dot(queries, starts[...]) * dot(decay[...], spread)
+    slabs = [pack[16 + half * 8 + step * 4 + i] for i in range(4)]
+    gain = jnp.concatenate(slabs, axis=1).astype(F32)[4:5]
     same = (iota((128, 128), 0) // DIM == iota((128, 128), 1) // DIM).astype(F32).astype(BF16)
-    for i in range(4):
+    for i in range(WIDE // 128):
         lane = slice(i * 128, (i + 1) * 128)
         result = partial[:, lane] + carried[:, lane]
         mean_sq = dot((result * result).astype(BF16), same) * (1.0 / DIM)
@@ -222,11 +267,11 @@
 
 
 def outer_mine_kernel(flags, u, partial, starts, pack, decay, out):
-    outer_part(flags[2] * 4 + pl.program_id(0), u, partial, starts, pack, decay, out)
+    outer_part(flags[2], u, partial, starts, pack, decay, out)
 
 
 def outer_other_kernel(flags, u, partial, starts, pack, decay, done, out):
-    outer_part(flags[1] * 4 + pl.program_id(0), u, partial, starts, pack, decay, out)
+    outer_part(flags[1], u, partial, starts, pack, decay, out)
 
 
 def array(shape, dtype=BF16):
@@ -239,6 +284,10 @@
 
 def half_columns(rows, which):
     return pl.BlockSpec((rows, LANES), lambda i, flags: (0, flags[which] * 4 + i))
+
+
+def wide_columns(rows, which):
+    return pl.BlockSpec((rows, WIDE), lambda i, flags: (0, flags[which] * 2 + i))
 
 
 def columns(rows):
@@ -259,6 +308,20 @@
     )
 
 
+def mark(value, *others):
+    place = pl.BlockSpec(memory_space=pl.ANY)
+    return pl.pallas_call(
+        mark_kernel,
+        out_shape=array(value.shape, value.dtype),
+        in_specs=[place] * (1 + len(others)),
+        out_specs=place,
+        input_output_aliases={0: 0},
+        cost_estimate=cost(6e9, 9e6, 4e6),
+        compiler_params=params(2),
+        name="mark",
+    )(value, *others)
+
+
 def exact(x):
     return lax.reduce_precision(x, 8, 7)
 
@@ -278,12 +341,37 @@
     def swapped(value):
         return lax.ppermute(value, "core", [(0, 1), (1, 0)])
 
-    behind = lax.ppermute(u[TOK - 16 :], ctx, [(i, i + 1) for i in range(63)])
+    rates, steps = log_decay[0].T, step_size[0].T
+    projected, to_end, ends, edge = pl.pallas_call(
+        project_kernel,
+        grid=(4,),
+        out_shape=(
+            array((TOK, 256)),
+            array((TOK, 128)),
+            array((ROWS, 128)),
+            array((16, CH + 256)),
+        ),
+        in_specs=[
+            pl.BlockSpec((TOK, 1024), lambda i: (0, i)),
+            pl.BlockSpec((1024, 256), lambda i: (i, 0)),
+            whole(HEADS, TOK),
+            whole(HEADS, TOK),
+        ],
+        out_specs=[
+            whole(TOK, 256),
+            whole(TOK, 128),
+            whole(ROWS, 128),
+            whole(16, CH + 256),
+        ],
+        scratch_shapes=[pltpu.VMEM((TOK, 256), F32)],
+        compiler_params=params(16),
+        cost_estimate=cost(6e8, 4.5e6),
+        name="project",
+    )(u, proj_weight[0], rates, steps)
+    behind = lax.ppermute(edge, ctx, [(i, i + 1) for i in range(63)])
     next_u = onward(u)
-    rates, steps = log_decay[0].T, step_size[0].T
     next_logs = onward(jnp.concatenate([rates, steps], axis=0))
     before = jnp.concatenate([jnp.zeros((13, CH + 256), BF16), carry_rows[0]], axis=0)
-    halo = jnp.where(first, before[:, :CH], behind)
     skip = jnp.repeat(skip_gain, DIM, axis=1)
     skip_hi = exact(skip)
     skip_mid = exact(skip - skip_hi)
@@ -294,58 +382,52 @@
         + [jnp.zeros((8, CH), BF16)],
         axis=0,
     )
+    behind, before, par = lax.optimization_barrier((behind, before, par))
     vmem = pl.BlockSpec(memory_space=pltpu.VMEM)
-    projected, to_end, ends = pl.pallas_call(
-        project_kernel,
-        out_shape=(array((TOK, 256)), array((TOK, 128)), array((ROWS, 128))),
-        in_specs=[vmem] * 4,
-        out_specs=[vmem] * 3,
-        compiler_params=params(16),
-        cost_estimate=cost(6e8, 4.5e6),
-        name="project",
-    )(u, proj_weight[0], rates, steps)
 
     pad = pltpu.VMEM((4, 272, 128), F32)
-    ends_pad = whole(ROWS, 128)
     fresh_out = array((STATE + ROWS, HALF))
+
+    def columns_of(which):
+        return [half_columns(rows, which) for rows in (TOK, 16, 16, 4)] + [whole(TOK, 128), whole(ROWS, 128)]
+
     send, turned, pack = call(
         send_kernel,
         "send",
         (fresh_out, array((STATE, TOK)), array((32, 16, 256))),
         (4,),
-        [half_columns(TOK, 1), half_columns(16, 1), half_columns(4, 1), whole(TOK, 128), ends_pad]
-        + [whole(16, CH), whole(CH, 256), whole(TOK, 256), whole(4, CH + 256), whole(16, 256), whole(16, CH)],
+        columns_of(1)
+        + [whole(16, CH + 256), whole(16, CH + 256), whole(TOK, 256), whole(4, CH + 256), whole(16, CH)],
         [columns(STATE + ROWS), whole(STATE, TOK), whole(32, 16, 256)],
         [pad],
-        mib=20,
+        mib=16,
         estimate=cost(6e8, 4.5e6, 5e5),
     )(
-        flags, u, halo, conv_weight[0], to_end, ends, halo, proj_weight[0], projected, conv_weight[0],
-        before[:, CH:], par,
+        flags, u, behind, before, conv_weight[0], to_end, ends, behind, before, projected, conv_weight[0], par
     )
+    next_pack = onward(pack)
     got = swapped(send)
     keep = call(
         keep_kernel,
         "keep",
         fresh_out,
         (4,),
-        [half_columns(TOK, 2), half_columns(16, 2), half_columns(4, 2), whole(TOK, 128), ends_pad, whole(STATE, TOK)],
+        columns_of(2) + [whole(STATE, TOK)],
         columns(STATE + ROWS),
         [pad],
+        mib=16,
         estimate=cost(6e8, 4.5e6, 5e5),
-    )(flags, u, halo, conv_weight[0], to_end, ends, turned)
-    pay, head_fresh = call(
+    )(flags, u, behind, before, conv_weight[0], to_end, ends, turned)
+    pay = call(
         join_kernel,
         "join",
-        (array((CHIPS, ROWS, LANES + 128)), fresh_out),
+        array((CHIPS, ROWS, LANES + 128)),
         (4,),
         [columns(STATE + ROWS)] * 2,
-        [pl.BlockSpec((8, ROWS, LANES + 128), lambda i, *_: (i, 0, 0)), columns(STATE + ROWS)],
+        pl.BlockSpec((8, ROWS, LANES + 128), lambda i, *_: (i, 0, 0)),
         estimate=cost(1e6, 2.5e6),
     )(flags, keep, got)
     shares = lax.all_to_all(pay, ("x", "z"), 0, 0)
-    next_pack = onward(pack)
-    next_fresh = onward(head_fresh)
     head = (core * 4 + lax.axis_index("x")) * 8
     start = lax.dynamic_slice(carry_state[0], (head, lax.axis_index("z") * ROWS, 0), (8, ROWS, DIM))
     start = start.transpose(1, 0, 2).reshape(ROWS, LANES)
@@ -358,46 +440,63 @@
         name="scan",
     )(shares, start)
     chip = lax.all_to_all(back, ("x", "z"), 0, 0)
-    partial, decay = call(
+    next_u = mark(next_u, next_pack, next_logs)
+    chip, next_u, next_pack, next_logs = lax.optimization_barrier((chip, next_u, next_pack, next_logs))
+    next_chip = onward(chip)
+    next_chip = mark(next_chip)
+    partial, decay, low_fresh, high_fresh = call(
         inner_kernel,
         "inner",
-        (array((TOK, CH), F32), array((TOK, 128))),
+        (array((TOK, CH), F32), array((TOK, 128)), fresh_out, fresh_out),
         (GROUPS,),
         [columns(TOK), whole(32, 16, 256), whole(128, TOK)],
-        [columns(TOK), whole(TOK, 128)],
-        [pltpu.VMEM((TOK, TOK), F32), pltpu.VMEM((TOK, 128), F32), pltpu.VMEM((HEADS, TOK), F32), pad],
+        [
+            columns(TOK),
+            whole(TOK, 128),
+            pl.BlockSpec((STATE + ROWS, LANES), lambda q: (0, jnp.minimum(q, 3))),
+            pl.BlockSpec((STATE + ROWS, LANES), lambda q: (0, jnp.maximum(q - 4, 0))),
+        ],
+        [
+            pltpu.VMEM((TOK, TOK), F32),
+            pltpu.VMEM((TOK, 128), F32),
+            pltpu.VMEM((HEADS, TOK), F32),
+            pltpu.VMEM((STATE, TOK), BF16),
+            pltpu.VMEM((TOK, 128), BF16),
+            pltpu.VMEM((ROWS, 128), BF16),
+            pad,
+        ],
         mib=20,
         prefetch=0,
-        estimate=cost(6e9, 9e6, 4e6),
+        estimate=cost(1, 1),
     )(next_u, next_pack, next_logs)
-    next_chip = onward(chip)
+    lead_fresh = lax.ppermute(high_fresh, "core", [(0, 1)])
     state_half = array((STATE, HALF))
     mine, cross = call(
         start_kernel,
         "start",
         (state_half, state_half),
         (4,),
-        [pl.BlockSpec((8, ROWS, LANES), lambda i, *_: (i, 0, 0)), columns(STATE + ROWS)],
+        [pl.BlockSpec((8, ROWS, LANES), lambda i, *_: (i, 0, 0)), columns(STATE + ROWS), columns(STATE + ROWS)],
         [columns(STATE)] * 2,
-    )(flags, next_chip, next_fresh)
+    )(flags, next_chip, low_fresh, lead_fresh)
     other = swapped(cross)
-    outer_in = [columns(STATE), whole(32, 16, 256), whole(TOK, 128)]
+    outer_in = [pl.BlockSpec((STATE, WIDE), lambda i, *_: (0, i)), whole(32, 16, 256), whole(TOK, 128)]
     rows = call(
         outer_mine_kernel,
         "outer_mine",
         array((TOK, CH)),
-        (4,),
-        [half_columns(TOK, 2), half_columns(TOK, 2)] + outer_in,
-        half_columns(TOK, 2),
+        (2,),
+        [wide_columns(TOK, 2), wide_columns(TOK, 2)] + outer_in,
+        wide_columns(TOK, 2),
         estimate=cost(6e8, 5e6),
     )(flags, next_u, partial, mine, next_pack, decay)
     rows = call(
         outer_other_kernel,
         "outer_other",
         array((TOK, CH)),
-        (4,),
-        [half_columns(TOK, 1), half_columns(TOK, 1)] + outer_in + [pl.BlockSpec(memory_space=pl.ANY)],
-        half_columns(TOK, 1),
+        (2,),
+        [wide_columns(TOK, 1), wide_columns(TOK, 1)] + outer_in + [pl.BlockSpec(memory_space=pl.ANY)],
+        wide_columns(TOK, 1),
         estimate=cost(6e8, 5e6),
         alias={6: 0},
     )(flags, next_u, partial, other, next_pack, decay, rows)

time: 136 us -> 108 us (0.79)
  waiting for transfers between devices: 58.7 us -> 35.5 us
  local copies, waits for them, and re-layouts: 12.7 us -> 4.01 us
  Pallas kernels: 30.6 us -> 34.3 us
    ppermute x5 -> x4, waiting for transfers between devices: 32.4 us -> 8.28 us  [onward(): return lax.ppermute(value, 'section', [(i, (i + 1) % 4) for i in range(4)])]
    all_to_all x1, waiting for transfers between devices: 12.7 us -> 3.32 us  [per_device(): chip = lax.all_to_all(back, ('x', 'z'), 0, 0)]
    ppermute x1 -> x2, waiting for transfers between devices: 0.01 us -> 7.31 us  [the longest x1 5.86 us: per_device(): lead_fresh = lax.ppermute(high_fresh, 'core', [(0, 1)])]
    unnamed x26 -> x20, local copies, waits for them, and re-layouts: 8.06 us -> 3.44 us
    all_to_all x1, waiting for transfers between devices: 13.6 us -> 16.6 us  [per_device(): shares = lax.all_to_all(pay, ('x', 'z'), 0, 0)]
    all_to_all x1, starting transfers between devices: 10.3 us -> 13.2 us  [per_device(): shares = lax.all_to_all(pay, ('x', 'z'), 0, 0)]
    pallas_call x6 -> x8, Pallas kernels: 24.7 us -> 27.4 us  [the longest x1 9.55 us: per_device(): call(inner_kernel, 'inner', (array((TOK, CH), F32), array((TOK, 128)), fr...]
    ppermute x2, starting transfers between devices: 2.96 us -> 0.32 us  [swapped(): return lax.ppermute(value, 'core', [(0, 1), (1, 0)])]
  transfers between devices with their start and end apart: 10 -> 10, of which waited for: 5 -> 5; matrix products, arithmetic and copies ran while one was open for 3% -> 1% of each run, Pallas kernels for 15% -> 20%
where the time goes in v3:
time: 108 us; the launch traced here: 107 us
  waiting for transfers between devices  35.5 us (33%)
  Pallas kernels  34.3 us (32%)
  starting transfers between devices  33.2 us (31%)
  local copies, waits for them, and re-layouts  4.01 us (4%)
    all_to_all x1, waiting for transfers between devices, per_device(): shares = lax.all_to_all(pay, ('x', 'z'), 0, 0)  16.6 us
    all_to_all x1, starting transfers between devices, per_device(): shares = lax.all_to_all(pay, ('x', 'z'), 0, 0)  13.2 us
    pallas_call x1, Pallas kernels, per_device(): call(inner_kernel, 'inner', (array((TOK, CH), F32), array((TOK, 128)), fr...  9.55 us
    ppermute x4, waiting for transfers between devices, onward(): return lax.ppermute(value, 'section', [(i, (i + 1) % 4) for i in range(4)])  8.28 us
    all_to_all x1, starting transfers between devices, per_device(): chip = lax.all_to_all(back, ('x', 'z'), 0, 0)  8.27 us
    ppermute x1, waiting for transfers between devices, per_device(): lead_fresh = lax.ppermute(high_fresh, 'core', [(0, 1)])  5.86 us
    ppermute x4, starting transfers between devices, onward(): return lax.ppermute(value, 'section', [(i, (i + 1) % 4) for i in range(4)])  5.12 us
    ppermute x1, starting transfers between devices, per_device(): behind = lax.ppermute(edge, ctx, [(i, i + 1) for i in range(63)])  4.94 us
  transfers between devices with their start and end apart: 10, of which 5 were waited for; matrix products, arithmetic and copies ran while one was open for 1% of the time, Pallas kernels for 20%

profile of v3, /device:TPU:1, one launch (start us, length us, event | category | flops | bytes accessed | tf_op | source)
XLA Modules:
  0.0 107.3 jit_solution(4176002154492757792)
XLA Ops:
  0.0 1.7 %copy-done.1 = bf16[1,4096,256]{2,1,0:T(8,128)(2,1)S(1)} copy-done((bf16[1,4096,256]{2,1,0:T(8,128)(2,1)S(1)}, bf16[1,4096,256]{2,1,0:T(8,128)(2,1)}, u32[]{:S(2)}) %copy-start.1) | copy-done | bytes 2097176
  1.7 0.8 copy-done.3
  3.4 3.5 %project.1 = (bf16[256,256]{1,0:T(8,128)(2,1)S(1)}, bf16[256,128]{1,0:T(8,128)(2,1)S(1)}, bf16[16,128]{1,0:T(8,128)(2,1)S(1)}, bf16[16,4352]{1,0:T(8,128)(2,1)S(1)}) custom-call(bf16[256,4096]{1,0:T(8,128)(2,1)} %bitcast.3.u, bf16[4096,256]{1,0:T(8,128)(2,1)S(1)} %bitcast.23, f32[64,256]{1,0:T(8,128)S(1)} %bitcast.27, f32[64,256]{1,0:T(8,128)S(1)} %bitcast.29), custom_call_target="tpu_custom_call" | custom-call | flops 600000000 | bytes 4500000 | tf_op jit(solution)/shard_map/project/pallas_call | solution.py:345
  6.9 4.9 %collective-permute-start = (bf16[16,4352]{1,0:T(8,128)(2,1)S(1)}, bf16[16,4352]{1,0:T(8,128)(2,1)S(1)}, u32[]{:S(2)}, u32[]{:S(2)}) collective-permute-start(bf16[16,4352]{1,0:T(8,128)(2,1)S(1)} %get-tuple-element.25), channel_id=1, source_target_pairs={{0,1},{1,2},{2,3},{3,4},{4,5},{5,6},{6,7},{7,8},{8,9},{9,10},{10,1... | collective-permute-start | bytes 417800 | tf_op jit(solution)/shard_map/ppermute | solution.py:371
  12.4 1.5 %collective-permute-done.behind.all_behind = bf16[16,4352]{1,0:T(8,128)(2,1)S(1)} collective-permute-done((bf16[16,4352]{1,0:T(8,128)(2,1)S(1)}, bf16[16,4352]{1,0:T(8,128)(2,1)S(1)}, u32[]{:S(2)}, u32[]{:S(2)}) %collective-permute-start) | collective-permute-done | bytes 139296 | tf_op jit(solution)/shard_map/ppermute | solution.py:371
  13.9 4.6 %send.1 = (bf16[144,2048]{1,0:T(8,128)(2,1)S(1)}, bf16[128,256]{1,0:T(8,128)(2,1)S(1)}, bf16[32,16,256]{2,1,0:T(8,128)(2,1)S(1)}) custom-call(s32[3]{0:T(128)S(1)} %pad_add_fusion.flags, bf16[256,4096]{1,0:T(8,128)(2,1)} %bitcast.3.u, bf16[16,4352]{1,0:T(8,128)(2,1)S(1)} %collective-permute-done.behind.all_behind, ...), custom_call_target="tpu_custom_call" | custom-call | flops 600000000 | bytes 4500000 | tf_op jit(solution)/shard_map/send/pallas_call | solution.py:394
  18.6 1.4 %collective-permute-start.2 = (bf16[256,4096]{1,0:T(8,128)(2,1)}, bf16[256,4096]{1,0:T(8,128)(2,1)}, u32[]{:S(2)}, u32[]{:S(2)}) collective-permute-start(bf16[256,4096]{1,0:T(8,128)(2,1)} %bitcast.3.u), channel_id=1, source_target_pairs={{0,64},{64,128},{128,192},{192,0},{1,65},{65,129},{129,193},{193,1... | collective-permute-start | bytes 6291464 | tf_op jit(solution)/shard_map/ppermute | solution.py:339
  20.0 4.3 %keep.1 = bf16[144,2048]{1,0:T(8,128)(2,1)S(1)} custom-call(s32[3]{0:T(128)S(1)} %pad_add_fusion.flags, bf16[256,4096]{1,0:T(8,128)(2,1)} %bitcast.3.u, bf16[16,4352]{1,0:T(8,128)(2,1)S(1)} %collective-permute-done.behind.all_behind, bf16[16,4352]{1,0:T(8,128)(2,1)S(1)} %concatenate.9.before.all_before, bf16[4,4352]{1,0:T(4,128)(2,1)S(1)} %bitcast.26, ...), custom_call_target="tpu_custom_call" | custom-call | flops 600000000 | bytes 4500000 | tf_op jit(solution)/shard_map/keep/pallas_call | solution.py:410
  24.3 2.2 %join.1 = bf16[32,16,640]{2,1,0:T(8,128)(2,1)} custom-call(s32[3]{0:T(128)S(1)} %pad_add_fusion.flags, bf16[144,2048]{1,0:T(8,128)(2,1)S(1)} %keep.1, bf16[144,2048]{1,0:T(8,128)(2,1)S(1)} %collective-permute-done.1.got), custom_call_target="tpu_custom_call" | custom-call | flops 1000000 | bytes 2500000 | tf_op jit(solution)/shard_map/join/pallas_call | solution.py:421
  26.6 13.2 %all-to-all-start = ((bf16[32,16,640]{2,1,0:T(8,128)(2,1)}), bf16[32,16,640]{2,1,0:T(8,128)(2,1)S(1)}, u32[]{:S(2)}, u32[]{:S(2)}) async-start(bf16[32,16,640]{2,1,0:T(8,128)(2,1)} %join.1), calls=%async_computation | async-start | bytes 1310720 | tf_op jit(solution)/shard_map/all_to_all | solution.py:430
  40.1 16.6 %all-to-all-done.got = bf16[32,16,640]{2,1,0:T(8,128)(2,1)S(1)} async-done(((bf16[32,16,640]{2,1,0:T(8,128)(2,1)}), bf16[32,16,640]{2,1,0:T(8,128)(2,1)S(1)}, u32[]{:S(2)}, u32[]{:S(2)}) %all-to-all-start) | async-done | bytes 655392 | tf_op jit(solution)/shard_map/all_to_all | solution.py:430
  56.7 1.1 %scan.1 = bf16[32,16,512]{2,1,0:T(8,128)(2,1)} custom-call(bf16[32,16,640]{2,1,0:T(8,128)(2,1)S(1)} %all-to-all-done.got, f32[16,512]{1,0:T(8,128)S(1)} %copy.17.start), custom_call_target="tpu_custom_call" | custom-call | tf_op jit(solution)/shard_map/scan/pallas_call | solution.py:434
  57.8 8.3 %all-to-all-start.1 = ((bf16[32,16,512]{2,1,0:T(8,128)(2,1)}), bf16[32,16,512]{2,1,0:T(8,128)(2,1)}, u32[]{:S(2)}, u32[]{:S(2)}) async-start(bf16[32,16,512]{2,1,0:T(8,128)(2,1)} %scan.1), calls=%async_computation.1 | async-start | bytes 1048576 | tf_op jit(solution)/shard_map/all_to_all | solution.py:442
  66.1 1.4 %collective-permute-start.3 = (bf16[32,16,256]{2,1,0:T(8,128)(2,1)S(1)}, bf16[32,16,256]{2,1,0:T(8,128)(2,1)S(1)}, u32[]{:S(2)}, u32[]{:S(2)}) collective-permute-start(bf16[32,16,256]{2,1,0:T(8,128)(2,1)S(1)} %get-tuple-element.34), channel_id=1, source_target_pairs={{0,64},{64,128},{128,192},{192,0},{1,65},{65,129},{129,193},{193,1... | collective-permute-start | bytes 786440 | tf_op jit(solution)/shard_map/ppermute | solution.py:339
  67.5 1.1 %collective-permute-start.4 = (f32[128,256]{1,0:T(8,128)S(1)}, f32[128,256]{1,0:T(8,128)S(1)}, u32[]{:S(2)}, u32[]{:S(2)}) collective-permute-start(f32[128,256]{1,0:T(8,128)S(1)} %pad_maximum_fusion), channel_id=1, source_target_pairs={{0,64},{64,128},{128,192},{192,0},{1,65},{65,129},{129,193},{193,1... | collective-permute-start | bytes 393224 | tf_op jit(solution)/shard_map/ppermute | solution.py:339
  68.5 8.3 %collective-permute-done.4.refs_2_.logs = f32[128,256]{1,0:T(8,128)S(1)} collective-permute-done((f32[128,256]{1,0:T(8,128)S(1)}, f32[128,256]{1,0:T(8,128)S(1)}, u32[]{:S(2)}, u32[]{:S(2)}) %collective-permute-start.4) | collective-permute-done | bytes 131104 | tf_op jit(solution)/shard_map/ppermute | solution.py:339
  76.8 3.3 %all-to-all-done.1 = bf16[32,16,512]{2,1,0:T(8,128)(2,1)} async-done(((bf16[32,16,512]{2,1,0:T(8,128)(2,1)}), bf16[32,16,512]{2,1,0:T(8,128)(2,1)}, u32[]{:S(2)}, u32[]{:S(2)}) %all-to-all-start.1) | async-done | bytes 524320 | tf_op jit(solution)/shard_map/all_to_all | solution.py:442
  80.2 1.3 %collective-permute-start.5 = (bf16[32,16,512]{2,1,0:T(8,128)(2,1)}, bf16[32,16,512]{2,1,0:T(8,128)(2,1)S(1)}, u32[]{:S(2)}, u32[]{:S(2)}) collective-permute-start(bf16[32,16,512]{2,1,0:T(8,128)(2,1)} %all-to-all-done.1), channel_id=1, source_target_pairs={{0,64},{64,128},{128,192},{192,0},{1,65},{65,129},{129,193},{193,1... | collective-permute-start | bytes 1572872 | tf_op jit(solution)/shard_map/ppermute | solution.py:339
  81.4 9.5 %inner.1 = (f32[256,4096]{1,0:T(8,128)S(1)}, bf16[256,128]{1,0:T(8,128)(2,1)S(1)}, bf16[144,2048]{1,0:T(8,128)(2,1)S(1)}, bf16[144,2048]{1,0:T(8,128)(2,1)S(1)}) custom-call(bf16[256,4096]{1,0:T(8,128)(2,1)} %mark.2.u, bf16[32,16,256]{2,1,0:T(8,128)(2,1)S(1)} %collective-permute-done.3.refs_1_.pack, f32[128,256]{1,0:T(8,128)S(1)} %collective-permute-done.4.refs_2_.logs), custom_call_target="tpu_custom_call" | custom-call | flops 1 | bytes 1 | tf_op jit(solution)/shard_map/inner/pallas_call | solution.py:447
  91.0 1.3 %collective-permute-start.6 = (bf16[144,2048]{1,0:T(8,128)(2,1)S(1)}, bf16[144,2048]{1,0:T(8,128)(2,1)S(1)}, u32[]{:S(2)}, u32[]{:S(2)}) collective-permute-start(bf16[144,2048]{1,0:T(8,128)(2,1)S(1)} %get-tuple-element.41), channel_id=1, source_target_pairs={{0,1},{2,3},{4,5},{6,7},{8,9},{10,11},{12,13},{14,15},{16,17},{18,... | collective-permute-start | bytes 1769480 | tf_op jit(solution)/shard_map/ppermute | solution.py:472
  92.3 5.9 %collective-permute-done.6.lead_fresh = bf16[144,2048]{1,0:T(8,128)(2,1)S(1)} collective-permute-done((bf16[144,2048]{1,0:T(8,128)(2,1)S(1)}, bf16[144,2048]{1,0:T(8,128)(2,1)S(1)}, u32[]{:S(2)}, u32[]{:S(2)}) %collective-permute-start.6) | collective-permute-done | bytes 589856 | tf_op jit(solution)/shard_map/ppermute | solution.py:472
  98.2 1.1 %start.1 = (bf16[128,2048]{1,0:T(8,128)(2,1)S(1)}, bf16[128,2048]{1,0:T(8,128)(2,1)S(1)}) custom-call(s32[3]{0:T(128)S(1)} %pad_add_fusion.flags, bf16[32,16,512]{2,1,0:T(8,128)(2,1)S(1)} %mark.3.chip, bf16[144,2048]{1,0:T(8,128)(2,1)S(1)} %get-tuple-element.40.low_fresh, bf16[144,2048]{1,0:T(8,128)(2,1)S(1)} %collective-permute-done.6.lead_fresh), custom_call_target="tpu_custom_call" | custom-call | tf_op jit(solution)/shard_map/start/pallas_call | solution.py:474
  99.6 3.9 %outer_mine.1.done = bf16[256,4096]{1,0:T(8,128)(2,1)} custom-call(s32[3]{0:T(128)S(1)} %pad_add_fusion.flags, bf16[256,4096]{1,0:T(8,128)(2,1)} %mark.2.u, f32[256,4096]{1,0:T(8,128)S(1)} %get-tuple-element.38.partial, bf16[128,2048]{1,0:T(8,128)(2,1)S(1)} %get-tuple-element.44.starts, bf16[32,16,256]{2,1,0:T(8,128)(2,1)S(1)} %collective-permute-done.3.refs_1_.pack, ...), custom_call_target="tpu_custom_call" | custom-call | flops 600000000 | bytes 5000000 | tf_op jit(solution)/shard_map/outer_mine/pallas_call | solution.py:484
  103.5 3.9 %outer_other.1 = bf16[256,4096]{1,0:T(8,128)(2,1)} custom-call(s32[3]{0:T(128)S(1)} %pad_add_fusion.flags, bf16[256,4096]{1,0:T(8,128)(2,1)} %mark.2.u, f32[256,4096]{1,0:T(8,128)S(1)} %get-tuple-element.38.partial, bf16[128,2048]{1,0:T(8,128)(2,1)S(1)} %collective-permute-done.7.starts, ...), custom_call_target="tpu_custom_call", output_to_operand_aliasing={{}: (6, {})} | custom-call | flops 600000000 | bytes 5000000 | tf_op jit(solution)/shard_map/outer_other/pallas_call | solution.py:493
  (38 shorter events, 1.9 us)
Async XLA Ops:
  0.0 39.8 %copy-start = (f32[1,64,128,64]{2,3,1,0:T(8,128)S(1)}, f32[1,64,128,64]{2,3,1,0:T(8,128)}, u32[]{:S(2)}) copy-start(f32[1,64,128,64]{2,3,1,0:T(8,128)} %param.16) | copy-start | bytes 6291460
  0.0 1.7 %copy-start.1 = (bf16[1,4096,256]{2,1,0:T(8,128)(2,1)S(1)}, bf16[1,4096,256]{2,1,0:T(8,128)(2,1)}, u32[]{:S(2)}) copy-start(bf16[1,4096,256]{2,1,0:T(8,128)(2,1)} %param.10) | copy-start | bytes 6291460
  1.7 0.8 copy-start.3
  2.6 0.8 copy-start.5
  3.4 8.5 %copy-start.9 = (f32[1,64]{1,0:T(1,128)S(1)}, f32[1,64]{1,0:T(1,128)}, u32[]{:S(2)}) copy-start(f32[1,64]{1,0:T(1,128)} %param.14) | copy-start | bytes 772
  3.4 8.6 %copy-start.2 = (bf16[1,4,4352]{2,1,0:T(4,128)(2,1)S(1)}, bf16[1,4,4352]{2,1,0:T(4,128)(2,1)}, u32[]{:S(2)}) copy-start(bf16[1,4,4352]{2,1,0:T(4,128)(2,1)} %param.11) | copy-start | bytes 104452
  3.4 8.7 %copy-start.7 = (bf16[1,3,4352]{2,1,0:T(4,128)(2,1)S(1)}, bf16[1,3,4352]{2,1,0:T(4,128)(2,1)}, u32[]{:S(2)}) copy-start(bf16[1,3,4352]{2,1,0:T(4,128)(2,1)} %param.17) | copy-start | bytes 78340
  3.4 8.8 %copy-start.8 = (bf16[1,4096]{1,0:T(2,128)(2,1)S(1)}, bf16[1,4096]{1,0:T(2,128)(2,1)}, u32[]{:S(2)}) copy-start(bf16[1,4096]{1,0:T(2,128)(2,1)} %param.15) | copy-start | bytes 24580
  6.9 6.9 %collective-permute-start = (bf16[16,4352]{1,0:T(8,128)(2,1)S(1)}, bf16[16,4352]{1,0:T(8,128)(2,1)S(1)}, u32[]{:S(2)}, u32[]{:S(2)}) collective-permute-start(bf16[16,4352]{1,0:T(8,128)(2,1)S(1)} %get-tuple-element.25), channel_id=1, source_target_pairs={{0,1},{1,2},{2,3},{3,4},{4,5},{5,6},{6,7},{7,8},{8,9},{9,10},{10,1... | collective-permute-start | bytes 417800 | tf_op jit(solution)/shard_map/ppermute | solution.py:371
  18.5 5.8 %collective-permute-start.1 = (bf16[144,2048]{1,0:T(8,128)(2,1)S(1)}, bf16[144,2048]{1,0:T(8,128)(2,1)S(1)}, u32[]{:S(2)}, u32[]{:S(2)}) collective-permute-start(bf16[144,2048]{1,0:T(8,128)(2,1)S(1)} %get-tuple-element.33), channel_id=1, source_target_pairs={{0,1},{1,0},{2,3},{3,2},{4,5},{5,4},{6,7},{7,6},{8,9},{9,8},{10,11... | collective-permute-start | bytes 1769480 | tf_op jit(solution)/shard_map/ppermute | solution.py:342
  18.6 58.2 %collective-permute-start.2 = (bf16[256,4096]{1,0:T(8,128)(2,1)}, bf16[256,4096]{1,0:T(8,128)(2,1)}, u32[]{:S(2)}, u32[]{:S(2)}) collective-permute-start(bf16[256,4096]{1,0:T(8,128)(2,1)} %bitcast.3.u), channel_id=1, source_target_pairs={{0,64},{64,128},{128,192},{192,0},{1,65},{65,129},{129,193},{193,1... | collective-permute-start | bytes 6291464 | tf_op jit(solution)/shard_map/ppermute | solution.py:339
  26.6 40.9 %copy-start.4 = (f32[1,256,64]{1,2,0:T(8,128)S(1)}, f32[1,256,64]{1,2,0:T(8,128)}, u32[]{:S(2)}) copy-start(f32[1,256,64]{1,2,0:T(8,128)} %param.12) | copy-start | bytes 196612
  26.6 40.9 %copy-start.6 = (f32[1,256,64]{1,2,0:T(8,128)S(1)}, f32[1,256,64]{1,2,0:T(8,128)}, u32[]{:S(2)}) copy-start(f32[1,256,64]{1,2,0:T(8,128)} %param.13) | copy-start | bytes 196612
  26.6 30.1 %all-to-all-start = ((bf16[32,16,640]{2,1,0:T(8,128)(2,1)}), bf16[32,16,640]{2,1,0:T(8,128)(2,1)S(1)}, u32[]{:S(2)}, u32[]{:S(2)}) async-start(bf16[32,16,640]{2,1,0:T(8,128)(2,1)} %join.1), calls=%async_computation | async-start | bytes 1310720 | tf_op jit(solution)/shard_map/all_to_all | solution.py:430
  57.8 22.4 %all-to-all-start.1 = ((bf16[32,16,512]{2,1,0:T(8,128)(2,1)}), bf16[32,16,512]{2,1,0:T(8,128)(2,1)}, u32[]{:S(2)}, u32[]{:S(2)}) async-start(bf16[32,16,512]{2,1,0:T(8,128)(2,1)} %scan.1), calls=%async_computation.1 | async-start | bytes 1048576 | tf_op jit(solution)/shard_map/all_to_all | solution.py:442
  66.1 10.7 %collective-permute-start.3 = (bf16[32,16,256]{2,1,0:T(8,128)(2,1)S(1)}, bf16[32,16,256]{2,1,0:T(8,128)(2,1)S(1)}, u32[]{:S(2)}, u32[]{:S(2)}) collective-permute-start(bf16[32,16,256]{2,1,0:T(8,128)(2,1)S(1)} %get-tuple-element.34), channel_id=1, source_target_pairs={{0,64},{64,128},{128,192},{192,0},{1,65},{65,129},{129,193},{193,1... | collective-permute-start | bytes 786440 | tf_op jit(solution)/shard_map/ppermute | solution.py:339
  67.5 9.4 %collective-permute-start.4 = (f32[128,256]{1,0:T(8,128)S(1)}, f32[128,256]{1,0:T(8,128)S(1)}, u32[]{:S(2)}, u32[]{:S(2)}) collective-permute-start(f32[128,256]{1,0:T(8,128)S(1)} %pad_maximum_fusion), channel_id=1, source_target_pairs={{0,64},{64,128},{128,192},{192,0},{1,65},{65,129},{129,193},{193,1... | collective-permute-start | bytes 393224 | tf_op jit(solution)/shard_map/ppermute | solution.py:339
  80.2 12.2 %collective-permute-start.5 = (bf16[32,16,512]{2,1,0:T(8,128)(2,1)}, bf16[32,16,512]{2,1,0:T(8,128)(2,1)S(1)}, u32[]{:S(2)}, u32[]{:S(2)}) collective-permute-start(bf16[32,16,512]{2,1,0:T(8,128)(2,1)} %all-to-all-done.1), channel_id=1, source_target_pairs={{0,64},{64,128},{128,192},{192,0},{1,65},{65,129},{129,193},{193,1... | collective-permute-start | bytes 1572872 | tf_op jit(solution)/shard_map/ppermute | solution.py:339
  91.0 7.2 %collective-permute-start.6 = (bf16[144,2048]{1,0:T(8,128)(2,1)S(1)}, bf16[144,2048]{1,0:T(8,128)(2,1)S(1)}, u32[]{:S(2)}, u32[]{:S(2)}) collective-permute-start(bf16[144,2048]{1,0:T(8,128)(2,1)S(1)} %get-tuple-element.41), channel_id=1, source_target_pairs={{0,1},{2,3},{4,5},{6,7},{8,9},{10,11},{12,13},{14,15},{16,17},{18,... | collective-permute-start | bytes 1769480 | tf_op jit(solution)/shard_map/ppermute | solution.py:472
  99.3 4.1 %collective-permute-start.7 = (bf16[128,2048]{1,0:T(8,128)(2,1)S(1)}, bf16[128,2048]{1,0:T(8,128)(2,1)S(1)}, u32[]{:S(2)}, u32[]{:S(2)}) collective-permute-start(bf16[128,2048]{1,0:T(8,128)(2,1)S(1)} %get-tuple-element.42), channel_id=1, source_target_pairs={{0,1},{1,0},{2,3},{3,2},{4,5},{5,4},{6,7},{7,6},{8,9},{9,8},{10,11... | collective-permute-start | bytes 1572872 | tf_op jit(solution)/shard_map/ppermute | solution.py:342

commit v4 on v3

v4 whole, which is shorter than its diff:
```python
import functools

import jax
import jax.numpy as jnp
from jax import lax
from jax.experimental import pallas as pl
from jax.experimental.pallas import tpu as pltpu
from jax.sharding import Mesh
from jax.sharding import PartitionSpec as P

HEADS = 64
DIM = 64
STATE = 128
TOK = 256
CH = 4096
HALF = CH // 2
LANES = 512
GROUPS = 8
ROWS = 16
CHIPS = 32
LOG2E = 1.4426950408889634
F32 = jnp.float32
BF16 = jnp.bfloat16


def params(mib):
    return pltpu.CompilerParams(vmem_limit_bytes=mib * 2**20)


def cost(flops, moved, exps=0):
    return pl.CostEstimate(flops=int(flops), bytes_accessed=int(moved), transcendentals=int(exps))


def dot(a, b):
    return jnp.dot(a, b, preferred_element_type=F32)


def parts(x, count):
    out = []
    for _ in range(count):
        piece = x.astype(BF16)
        out.append(piece)
        x = x - piece.astype(F32)
    return out


def iota(shape, axis):
    return lax.broadcasted_iota(jnp.int32, shape, axis)


def two_parts(x):
    hi = x.astype(BF16).astype(F32)
    return jnp.where(iota(x.shape, 1) < HEADS, hi, x - hi).astype(BF16)


def spread_matrix(rows, group):
    head = iota((rows, LANES), 1) // DIM + group * (LANES // DIM)
    return (iota((rows, LANES), 0) % HEADS == head).astype(F32).astype(BF16)


def conv_silu(pad, x, halo, taps, first=None, carried=None):
    pad[0:16, :] = halo.astype(F32)
    if carried is not None:
        pad[13:16, :] = jnp.where(first == 1, carried.astype(F32), halo.astype(F32)[13:16])
    pad[16:272, :] = x.astype(F32)
    total = taps[0:1] * pad[13:269, :]
    for j in range(1, 4):
        total = total + taps[j : j + 1] * pad[13 + j : 269 + j, :]
    half = 0.5 * total
    return (half + half * jnp.tanh(half)).astype(BF16)


def cumulated(rates):
    tri = (iota((TOK, TOK), 0) <= iota((TOK, TOK), 1)).astype(F32).astype(BF16)
    return sum(dot(piece, tri) for piece in parts(rates, 3))


def twice_turned(x):
    return jnp.concatenate([x, x], axis=0).T


def end_factors(cum, steps):
    last = cum[TOK - 1 : TOK]
    hi, mid, lo = (piece.astype(F32) for piece in parts(jnp.exp(last), 3))
    kind = iota((ROWS, 128), 0) // 4
    tile = jnp.where(kind == 0, hi, jnp.where(kind == 1, mid, jnp.where(kind == 2, lo, 0.0)))
    ends = jnp.where(iota((ROWS, 128), 1) < HEADS, tile, 0.0).astype(BF16)
    return two_parts(jnp.exp(last - cum) * steps), ends


def fresh_half(half, first, u, behind, carried, taps, to_end, ends, turned, fresh, pad):
    for q in range(4):
        spread = spread_matrix(2 * HEADS, half * 4 + q)
        scale = dot(to_end[...], spread)
        scaled = []
        for i in range(4):
            lane = pl.ds(pl.multiple_of(half * HALF + q * LANES + i * 128, 128), 128)
            act = conv_silu(
                pad.at[i], u[:, lane], behind[:, lane], taps[:, lane].astype(F32), first, carried[:, lane]
            )
            scaled.append((act.astype(F32) * scale[:, i * 128 : (i + 1) * 128]).astype(BF16))
        cols = slice(q * LANES, (q + 1) * LANES)
        fresh[0:STATE, cols] = dot(turned[...], jnp.concatenate(scaled, axis=1)).astype(BF16)
        fresh[STATE : STATE + ROWS, cols] = dot(ends[...], spread).astype(BF16)


def fetch_kernel(u, weight, near_u, near_weight, sems):
    copies = []
    for i in range(4):
        rows, depth = pl.ds(i * 64, 64), pl.ds(i * 1024, 1024)
        copies.append(pltpu.make_async_copy(u.at[rows], near_u.at[rows], sems.at[2 * i]))
        copies.append(pltpu.make_async_copy(weight.at[depth], near_weight.at[depth], sems.at[2 * i + 1]))
    for copy in copies:
        copy.start()
    for copy in copies:
        copy.wait()


def send_kernel(
    flags, u, weight, logs, behind, carried, taps, fresh, turned, pack, to_end, ends, pad
):
    first = flags[0]
    to_end[...], ends[...] = end_factors(
        twice_turned(cumulated(logs[0:HEADS])), twice_turned(logs[HEADS : 2 * HEADS])
    )
    projected = dot(u[...], weight[...]).astype(BF16)
    rim_bc = dot(behind[...], weight[...]).astype(BF16).astype(F32)
    acts = []
    for i in range(2):
        lane = slice(CH + i * 128, CH + (i + 1) * 128)
        value, rim = projected[:, i * 128 : (i + 1) * 128], rim_bc[:, i * 128 : (i + 1) * 128]
        acts.append(conv_silu(pad.at[i], value, rim, taps[:, lane].astype(F32), first, carried[:, lane]))
    turned[...] = acts[0].astype(F32).T.astype(BF16)
    for s in range(16):
        for i in range(2):
            pack[s, :, i * 128 : (i + 1) * 128] = acts[i][s * 16 : (s + 1) * 16]
    fresh_half(flags[1], first, u, behind, carried, taps, to_end, ends, turned, fresh, pad)


def keep_kernel(flags, u, behind, carried, taps, to_end, ends, turned, fresh, pad):
    fresh_half(flags[2], flags[0], u, behind, carried, taps, to_end, ends, turned, fresh, pad)


def end_row(tail):
    tail = tail.astype(F32)
    return tail[0:1] + tail[4:5] + tail[8:9]


def join_kernel(flags, keep, got, pay):
    lead = flags[2] == 0
    row = iota((ROWS, 128), 0)
    for q in range(4):
        cols = slice(q * LANES, (q + 1) * LANES)
        own, other = keep[0:STATE, cols].astype(F32), got[0:STATE, cols].astype(F32)
        own_end, other_end = end_row(keep[STATE:, cols]), end_row(got[STATE:, cols])
        total = jnp.where(lead, other_end * own + other, own_end * other + own).astype(BF16)
        pieces = [piece.astype(F32) for piece in parts(own_end * other_end, 3)]
        tail = jnp.zeros((ROWS, 128), F32)
        for p in range(3):
            for i in range(4):
                tail = jnp.where(row == 4 * p + i, pieces[p][:, i * 128 : (i + 1) * 128], tail)
        tail = tail.astype(BF16)
        for g in range(8):
            pay[q * 8 + g, :, 0:LANES] = total[g * ROWS : (g + 1) * ROWS]
            pay[q * 8 + g, :, LANES : LANES + 128] = tail


def scan_kernel(got, start, out):
    def one(i, state):
        out[i] = state.astype(BF16)
        tail = got[i, :, LANES : LANES + 128].astype(F32)
        tail = tail[0:4] + tail[4:8] + tail[8:12]
        ends = jnp.concatenate([tail[i : i + 1] for i in range(4)], axis=1)
        return state * ends + got[i, :, 0:LANES].astype(F32)

    lax.fori_loop(0, CHIPS, one, start[...])


def start_kernel(flags, chip, low_fresh, lead_fresh, mine, cross):
    lead = flags[2] == 0
    for q in range(4):
        cols = slice(q * LANES, (q + 1) * LANES)
        state = jnp.concatenate([chip[q * 8 + g] for g in range(8)], axis=0).astype(F32)
        fresh = jnp.where(lead, low_fresh[:, cols].astype(F32), lead_fresh[:, cols].astype(F32))
        second = end_row(fresh[STATE:]) * state + fresh[0:STATE]
        mine[:, cols] = jnp.where(lead, state, second).astype(BF16)
        cross[:, cols] = jnp.where(lead, second, state).astype(BF16)


def inner_kernel(
    u, pack, par, logs, partial, decay, far_u, low_fresh, high_fresh, scores, log_col, log_row, turned_keys, to_end, ends, pad
):
    q = pl.program_id(0)

    @pl.when(q == 0)
    def _():
        bc = pack[...].reshape(TOK, 256)
        scores[...] = lax.dot_general(
            bc[:, 128:256], bc[:, 0:128], (((1,), (1,)), ((), ())), preferred_element_type=F32
        )
        cum = cumulated(logs[0:HEADS])
        log_row[...] = cum * LOG2E - jnp.log2(logs[HEADS : 2 * HEADS])
        turned = twice_turned(cum)
        log_col[...] = turned * LOG2E
        decay[...] = two_parts(jnp.exp(turned))
        turned_keys[...] = bc[:, 0:128].astype(F32).T.astype(BF16)
        to_end[...], ends[...] = end_factors(turned, twice_turned(logs[HEADS : 2 * HEADS]))

    far_u[...] = u[...]
    slab = par[...].astype(F32)
    skip = slab[5:6] + slab[6:7] + slab[7:8]
    spread = spread_matrix(2 * HEADS, q)
    scale = dot(to_end[...], spread)
    scaled = []
    cols = pltpu.roll(log_col[...], (128 - 8 * q) % 128, 1)
    rows = log_row[pl.ds(pl.multiple_of(q * 8, 8), 8), :]
    half = TOK // 2
    causal = iota((half, half), 0) >= iota((half, half), 1)
    left = iota((TOK, 128), 1) < DIM
    for i in range(4):
        lane = slice(i * 128, (i + 1) * 128)
        value = conv_silu(pad.at[i], u[:, lane], slab[:, lane], slab[0:4, lane])
        scaled.append((value.astype(F32) * scale[:, lane]).astype(BF16))
        both = []
        for h in (2 * i, 2 * i + 1):
            col = cols[:, h : h + 1]
            row = rows[h : h + 1]
            top = jnp.exp2(jnp.where(causal, col[:half] - row[:, :half], -jnp.inf)) * scores[:half, :half]
            low_left = jnp.exp2(col[half:] - row[:, :half]) * scores[half:, :half]
            low_right = jnp.exp2(jnp.where(causal, col[half:] - row[:, half:], -jnp.inf)) * scores[half:, half:]
            low = jnp.concatenate([low_left.astype(BF16), low_right.astype(BF16)], axis=1)
            both.append(jnp.concatenate([dot(top.astype(BF16), value[:half]), dot(low, value)], axis=0))
        partial[:, lane] = jnp.where(left, both[0], both[1]) + skip[:, lane] * value.astype(F32)
    fresh = dot(turned_keys[...], jnp.concatenate(scaled, axis=1)).astype(BF16)
    end_rows = dot(ends[...], spread).astype(BF16)

    @pl.when(q < 4)
    def _():
        low_fresh[0:STATE, :] = fresh
        low_fresh[STATE:, :] = end_rows

    @pl.when(q >= 4)
    def _():
        high_fresh[0:STATE, :] = fresh
        high_fresh[STATE:, :] = end_rows


def mark_kernel(*refs):
    pass


def outer_half(half, u, partial, starts, pack, par, decay, out, buf, sems):
    queries = pack[...].reshape(TOK, 256)[:, 128:256]
    same = (iota((128, 128), 0) // DIM == iota((128, 128), 1) // DIM).astype(F32).astype(BF16)
    copies = []
    for q in range(4):
        spread = spread_matrix(2 * HEADS, half * 4 + q)
        carried = dot(queries, starts[:, q * LANES : (q + 1) * LANES]) * dot(decay[...], spread)
        base = half * HALF + q * LANES
        for i in range(4):
            lane = slice(i * 128, (i + 1) * 128)
            here = pl.ds(pl.multiple_of(base + i * 128, 128), 128)
            result = partial[:, here] + carried[:, lane]
            mean_sq = dot((result * result).astype(BF16), same) * (1.0 / DIM)
            normed = result * lax.rsqrt(mean_sq + 1e-05)
            buf[q, :, lane] = (u[:, here].astype(F32) + par[:, here].astype(F32)[4:5] * normed).astype(BF16)
        target = out.at[:, pl.ds(pl.multiple_of(base, LANES), LANES)]
        copies.append(pltpu.make_async_copy(buf.at[q], target, sems.at[q]))
        copies[-1].start()
    for copy in copies:
        copy.wait()


def outer_mine_kernel(flags, u, partial, starts, pack, par, decay, out, buf, sems):
    outer_half(flags[2], u, partial, starts, pack, par, decay, out, buf, sems)


def outer_other_kernel(flags, u, partial, starts, pack, par, decay, done, out, buf, sems):
    outer_half(flags[1], u, partial, starts, pack, par, decay, out, buf, sems)


def array(shape, dtype=BF16):
    return jax.ShapeDtypeStruct(shape, dtype)


def whole(*shape):
    return pl.BlockSpec(shape, lambda *_: (0,) * len(shape))


def columns(rows):
    return pl.BlockSpec((rows, LANES), lambda i, *_: (0, i))


def call(kernel, name, out, ins, outs, scratch=(), mib=16, estimate=None):
    return pl.pallas_call(
        kernel,
        out_shape=out,
        in_specs=[pl.BlockSpec(memory_space=pltpu.SMEM)] + ins,
        out_specs=outs,
        scratch_shapes=list(scratch),
        compiler_params=params(mib),
        cost_estimate=estimate,
        name=name,
    )


def mark(value, *others):
    place = pl.BlockSpec(memory_space=pl.ANY)
    return pl.pallas_call(
        mark_kernel,
        out_shape=array(value.shape, value.dtype),
        in_specs=[place] * (1 + len(others)),
        out_specs=place,
        input_output_aliases={0: 0},
        cost_estimate=cost(6e9, 9e6, 4e6),
        compiler_params=params(1),
        name="mark",
    )(value, *others)


def exact(x):
    return lax.reduce_precision(x, 8, 7)


def per_device(
    section_in, proj_weight, conv_weight, log_decay, step_size, skip_gain, norm_gain, carry_state, carry_rows
):
    u = section_in[0]
    ctx = ("x", "z", "core")
    core = lax.axis_index("core")
    first = lax.axis_index(ctx) == 0
    flags = jnp.stack([first.astype(jnp.int32), 1 - core, core])

    def onward(value):
        return lax.ppermute(value, "section", [(i, (i + 1) % 4) for i in range(4)])

    def swapped(value):
        return lax.ppermute(value, "core", [(0, 1), (1, 0)])

    logs = jnp.concatenate([log_decay[0].T, step_size[0].T], axis=0)
    vmem, anywhere = pl.BlockSpec(memory_space=pltpu.VMEM), pl.BlockSpec(memory_space=pl.ANY)
    behind = lax.ppermute(u[TOK - 16 :], ctx, [(i, i + 1) for i in range(63)])
    near_u, near_weight = pl.pallas_call(
        fetch_kernel,
        out_shape=(array((TOK, CH)), array((CH, 256))),
        in_specs=[anywhere] * 2,
        out_specs=[vmem] * 2,
        scratch_shapes=[pltpu.SemaphoreType.DMA((8,))],
        compiler_params=params(46),
        cost_estimate=cost(1e9, 1e7),
        name="fetch",
    )(u, proj_weight[0])
    next_u = onward(u)
    next_logs = onward(logs)
    skip = jnp.repeat(skip_gain, DIM, axis=1)
    skip_hi = exact(skip)
    skip_mid = exact(skip - skip_hi)
    skip_lo = skip - skip_hi - skip_mid
    par = jnp.concatenate(
        [conv_weight[0, :, :CH], norm_gain]
        + [piece.astype(BF16) for piece in (skip_hi, skip_mid, skip_lo)]
        + [jnp.zeros((5, CH), BF16), jnp.where(first, carry_rows[0, :, :CH], behind[13:])],
        axis=0,
    )
    next_par = onward(par)
    pad = pltpu.VMEM((4, 272, 128), F32)
    fresh_out = array((STATE + ROWS, HALF))
    send, turned, pack, to_end, ends = call(
        send_kernel,
        "send",
        (
            fresh_out,
            array((STATE, TOK)),
            array((16, 16, 256)),
            array((TOK, 128)),
            array((ROWS, 128)),
        ),
        [vmem] * 6,
        [vmem] * 5,
        [pad],
        estimate=cost(6e8, 4.5e6, 5e5),
    )(flags, near_u, near_weight, logs, behind, carry_rows[0], conv_weight[0])
    next_pack = onward(pack)
    got = swapped(send)
    keep = call(
        keep_kernel,
        "keep",
        fresh_out,
        [vmem] * 7,
        vmem,
        [pad],
        estimate=cost(6e8, 4.5e6, 5e5),
    )(flags, near_u, behind, carry_rows[0], conv_weight[0], to_end, ends, turned)
    pay = call(join_kernel, "join", array((CHIPS, ROWS, LANES + 128)), [vmem] * 2, vmem, estimate=cost(1e6, 2.5e6))(
        flags, keep, got
    )
    shares = lax.all_to_all(pay, ("x", "z"), 0, 0)
    head = (core * 4 + lax.axis_index("x")) * 8
    start = lax.dynamic_slice(carry_state[0], (head, lax.axis_index("z") * ROWS, 0), (8, ROWS, DIM))
    start = start.transpose(1, 0, 2).reshape(ROWS, LANES)
    back = pl.pallas_call(
        scan_kernel,
        out_shape=array((CHIPS, ROWS, LANES)),
        in_specs=[vmem] * 2,
        out_specs=vmem,
        compiler_params=params(8),
        name="scan",
    )(shares, start)
    chip = lax.all_to_all(back, ("x", "z"), 0, 0)
    next_u = mark(next_u, next_pack, next_logs, next_par)
    chip, next_u, next_pack, next_logs, next_par = lax.optimization_barrier(
        (chip, next_u, next_pack, next_logs, next_par)
    )
    next_chip = onward(chip)
    next_chip = mark(next_chip)
    partial, decay, far_u, low_fresh, high_fresh = pl.pallas_call(
        inner_kernel,
        grid=(GROUPS,),
        out_shape=(array((TOK, CH), F32), array((TOK, 128)), array((TOK, CH)), fresh_out, fresh_out),
        in_specs=[columns(TOK), whole(16, 16, 256), columns(16), whole(128, TOK)],
        out_specs=[
            columns(TOK),
            whole(TOK, 128),
            columns(TOK),
            pl.BlockSpec((STATE + ROWS, LANES), lambda q: (0, jnp.minimum(q, 3))),
            pl.BlockSpec((STATE + ROWS, LANES), lambda q: (0, jnp.maximum(q - 4, 0))),
        ],
        scratch_shapes=[
            pltpu.VMEM((TOK, TOK), F32),
            pltpu.VMEM((TOK, 128), F32),
            pltpu.VMEM((HEADS, TOK), F32),
            pltpu.VMEM((STATE, TOK), BF16),
            pltpu.VMEM((TOK, 128), BF16),
            pltpu.VMEM((ROWS, 128), BF16),
            pad,
        ],
        compiler_params=params(20),
        cost_estimate=cost(1, 1),
        name="inner",
    )(next_u, next_pack, next_par, next_logs)
    lead_fresh = lax.ppermute(high_fresh, "core", [(0, 1)])
    state_half = array((STATE, HALF))
    mine, cross = call(start_kernel, "start", (state_half, state_half), [vmem] * 3, [vmem] * 2)(
        flags, next_chip, low_fresh, lead_fresh
    )
    other = swapped(cross)
    scratch = [pltpu.VMEM((4, TOK, LANES), BF16), pltpu.SemaphoreType.DMA((4,))]
    inputs = [pl.BlockSpec(memory_space=pltpu.SMEM)] + [vmem] * 6
    rows = pl.pallas_call(
        outer_mine_kernel,
        out_shape=array((TOK, CH)),
        in_specs=inputs,
        out_specs=anywhere,
        scratch_shapes=scratch,
        compiler_params=params(16),
        cost_estimate=cost(6e8, 5e6),
        name="outer_mine",
    )(flags, far_u, partial, mine, next_pack, next_par, decay)
    rows = pl.pallas_call(
        outer_other_kernel,
        out_shape=array((TOK, CH)),
        in_specs=inputs + [anywhere],
        out_specs=anywhere,
        scratch_shapes=scratch,
        compiler_params=params(16),
        cost_estimate=cost(6e8, 5e6),
        input_output_aliases={7: 0},
        name="outer_other",
    )(flags, far_u, partial, other, next_pack, next_par, decay, rows)
    return rows[None]


def solution(mesh):
    split = Mesh(mesh.devices.reshape(4, 4, 8, 2), ("section", "x", "z", "core"))
    tokens = P("section", ("x", "z", "core"), None)
    layer = P("section", None, None)
    return jax.shard_map(
        per_device,
        mesh=split,
        in_specs=(
            tokens,
            layer,
            layer,
            tokens,
            tokens,
            P("section", None),
            P("section", None),
            P("section", None, None, None),
            layer,
        ),
        out_specs=tokens,
        check_vma=False,
    )
```

time: 108 us -> 97.3 us (0.901)
  Pallas kernels: 34.3 us -> 27.6 us
  waiting for transfers between devices: 35.5 us -> 32.5 us
    pallas_call x8, Pallas kernels: 33.1 us -> 26.5 us  [the longest x1 9.77 us: per_device(): pl.pallas_call(inner_kernel, grid=(GROUPS,), out_shape=(array((TOK, CH),...]
    unnamed x20 -> x14, local copies, waits for them, and re-layouts: 3.44 us -> 0.03 us
    all_to_all x1, waiting for transfers between devices: 16.6 us -> 14.2 us  [per_device(): shares = lax.all_to_all(pay, ('x', 'z'), 0, 0)]
    ppermute x1, waiting for transfers between devices: 1.45 us -> 0.01 us  [per_device(): behind = lax.ppermute(u[TOK - 16:], ctx, [(i, i + 1) for i in range(63)])]
    ppermute x4 -> x5, waiting for transfers between devices: 8.28 us -> 9.6 us  [onward(): return lax.ppermute(value, 'section', [(i, (i + 1) % 4) for i in range(4)])]
    ppermute x4 -> x5, starting transfers between devices: 5.12 us -> 4.95 us  [onward(): return lax.ppermute(value, 'section', [(i, (i + 1) % 4) for i in range(4)])]
  transfers between devices with their start and end apart: 10 -> 11, of which waited for: 5 -> 5; matrix products, arithmetic and copies ran while one was open for 1% -> 2% of each run, Pallas kernels for 20% -> 21%
where the time goes in v4:
time: 97.3 us; the launch traced here: 96.9 us
  starting transfers between devices  32.8 us (34%)
  waiting for transfers between devices  32.5 us (33%)
  Pallas kernels  27.6 us (28%)
  local copies, waits for them, and re-layouts  3.32 us (3%)
    all_to_all x1, waiting for transfers between devices, per_device(): shares = lax.all_to_all(pay, ('x', 'z'), 0, 0)  14.2 us
    all_to_all x1, starting transfers between devices, per_device(): shares = lax.all_to_all(pay, ('x', 'z'), 0, 0)  12.7 us
    pallas_call x1, Pallas kernels, per_device(): pl.pallas_call(inner_kernel, grid=(GROUPS,), out_shape=(array((TOK, CH),...  9.77 us
    ppermute x5, waiting for transfers between devices, onward(): return lax.ppermute(value, 'section', [(i, (i + 1) % 4) for i in range(4)])  9.6 us
    all_to_all x1, starting transfers between devices, per_device(): chip = lax.all_to_all(back, ('x', 'z'), 0, 0)  8.43 us
    ppermute x1, waiting for transfers between devices, per_device(): lead_fresh = lax.ppermute(high_fresh, 'core', [(0, 1)])  6.09 us
    ppermute x5, starting transfers between devices, onward(): return lax.ppermute(value, 'section', [(i, (i + 1) % 4) for i in range(4)])  4.95 us
    ppermute x1, starting transfers between devices, per_device(): behind = lax.ppermute(u[TOK - 16:], ctx, [(i, i + 1) for i in range(63)])  4.94 us
  transfers between devices with their start and end apart: 11, of which 5 were waited for; matrix products, arithmetic and copies ran while one was open for 2% of the time, Pallas kernels for 21%

profile of v4, /device:TPU:1, one launch (start us, length us, event | category | flops | bytes accessed | tf_op | source)
XLA Modules:
  0.0 96.9 jit_solution(17732337164904028587)
XLA Ops:
  0.0 1.1 %slice_bitcast_fusion = bf16[16,4096]{1,0:T(8,128)(2,1)S(1)} fusion(bf16[1,256,4096]{2,1,0:T(8,128)(2,1)} %param.9), kind=kLoop, calls=%fused_computation.1 | loop fusion | bytes 262144 | tf_op jit(solution)/shard_map/slice | solution.py:342
  1.1 4.9 %collective-permute-start = (bf16[16,4096]{1,0:T(8,128)(2,1)S(1)}, bf16[16,4096]{1,0:T(8,128)(2,1)S(1)}, u32[]{:S(2)}, u32[]{:S(2)}) collective-permute-start(bf16[16,4096]{1,0:T(8,128)(2,1)S(1)} %slice_bitcast_fusion), channel_id=1, source_target_pairs={{0,1},{1,2},{2,3},{3,4},{4,5},{5,6},{6,7},{7,8},{8,9},{9,10},{10,1... | collective-permute-start | bytes 393224 | tf_op jit(solution)/shard_map/ppermute | solution.py:342
  6.1 2.3 %fetch.1 = (bf16[256,4096]{1,0:T(8,128)(2,1)S(1)}, bf16[4096,256]{1,0:T(8,128)(2,1)S(1)}) custom-call(bf16[256,4096]{1,0:T(8,128)(2,1)} %bitcast.3.u, bf16[4096,256]{1,0:T(8,128)(2,1)} %bitcast.31), custom_call_target="tpu_custom_call" | custom-call | flops 1000000000 | bytes 10000000 | tf_op jit(solution)/shard_map/fetch/pallas_call | solution.py:343
  8.4 3.7 %send.1 = (bf16[144,2048]{1,0:T(8,128)(2,1)S(1)}, bf16[128,256]{1,0:T(8,128)(2,1)S(1)}, bf16[16,16,256]{2,1,0:T(8,128)(2,1)S(1)}, bf16[256,128]{1,0:T(8,128)(2,1)S(1)}, bf16[16,128]{1,0:T(8,128)(2,1)S(1)}) custom-call(s32[3]{0:T(128)S(1)} %pad_add_fusion.flags, bf16[256,4096]{1,0:T(8,128)(2,1)S(1)} %get-tuple-element.24.u, ...), custom_call_target="tpu_custom_call" | custom-call | flops 600000000 | bytes 4500000 | tf_op jit(solution)/shard_map/send/pallas_call | solution.py:368
  12.3 1.4 %collective-permute-start.4 = (f32[128,256]{1,0:T(8,128)S(1)}, f32[128,256]{1,0:T(8,128)S(1)}, u32[]{:S(2)}, u32[]{:S(2)}) collective-permute-start(f32[128,256]{1,0:T(8,128)S(1)} %pad_maximum_fusion.logs), channel_id=1, source_target_pairs={{0,64},{64,128},{128,192},{192,0},{1,65},{65,129},{129,193},{193,1... | collective-permute-start | bytes 393224 | tf_op jit(solution)/shard_map/ppermute | solution.py:335
  13.7 1.3 %collective-permute-start.2 = (bf16[256,4096]{1,0:T(8,128)(2,1)}, bf16[256,4096]{1,0:T(8,128)(2,1)}, u32[]{:S(2)}, u32[]{:S(2)}) collective-permute-start(bf16[256,4096]{1,0:T(8,128)(2,1)} %bitcast.3.u), channel_id=1, source_target_pairs={{0,64},{64,128},{128,192},{192,0},{1,65},{65,129},{129,193},{193,1... | collective-permute-start | bytes 6291464 | tf_op jit(solution)/shard_map/ppermute | solution.py:335
  14.9 2.5 %keep.1 = bf16[144,2048]{1,0:T(8,128)(2,1)S(1)} custom-call(s32[3]{0:T(128)S(1)} %pad_add_fusion.flags, bf16[256,4096]{1,0:T(8,128)(2,1)S(1)} %get-tuple-element.24.u, bf16[16,4096]{1,0:T(8,128)(2,1)S(1)} %collective-permute-done.behind, bf16[3,4352]{1,0:T(4,128)(2,1)S(1)} %bitcast.28, bf16[4,4352]{1,0:T(4,128)(2,1)S(1)} %bitcast.30, ...), custom_call_target="tpu_custom_call" | custom-call | flops 600000000 | bytes 4500000 | tf_op jit(solution)/shard_map/keep/pallas_call | solution.py:385
  17.5 1.7 %join.1 = bf16[32,16,640]{2,1,0:T(8,128)(2,1)} custom-call(s32[3]{0:T(128)S(1)} %pad_add_fusion.flags, bf16[144,2048]{1,0:T(8,128)(2,1)S(1)} %keep.1, bf16[144,2048]{1,0:T(8,128)(2,1)S(1)} %collective-permute-done.1.got), custom_call_target="tpu_custom_call" | custom-call | flops 1000000 | bytes 2500000 | tf_op jit(solution)/shard_map/join/pallas_call | solution.py:394
  19.2 12.7 %all-to-all-start = ((bf16[32,16,640]{2,1,0:T(8,128)(2,1)}), bf16[32,16,640]{2,1,0:T(8,128)(2,1)S(1)}, u32[]{:S(2)}, u32[]{:S(2)}) async-start(bf16[32,16,640]{2,1,0:T(8,128)(2,1)} %join.1), calls=%async_computation | async-start | bytes 1310720 | tf_op jit(solution)/shard_map/all_to_all | solution.py:397
  33.0 1.0 %copy.17.start = f32[16,512]{1,0:T(8,128)S(1)} copy(f32[16,512]{0,1:T(8,128)} %bitcast.32) | data formatting | bytes 65536 | tf_op jit(solution)/shard_map/reshape | solution.py:400
  34.0 14.2 %all-to-all-done.got = bf16[32,16,640]{2,1,0:T(8,128)(2,1)S(1)} async-done(((bf16[32,16,640]{2,1,0:T(8,128)(2,1)}), bf16[32,16,640]{2,1,0:T(8,128)(2,1)S(1)}, u32[]{:S(2)}, u32[]{:S(2)}) %all-to-all-start) | async-done | bytes 655392 | tf_op jit(solution)/shard_map/all_to_all | solution.py:397
  48.2 1.1 %scan.1 = bf16[32,16,512]{2,1,0:T(8,128)(2,1)} custom-call(bf16[32,16,640]{2,1,0:T(8,128)(2,1)S(1)} %all-to-all-done.got, f32[16,512]{1,0:T(8,128)S(1)} %copy.17.start), custom_call_target="tpu_custom_call" | custom-call | tf_op jit(solution)/shard_map/scan/pallas_call | solution.py:401
  49.4 8.4 %all-to-all-start.1 = ((bf16[32,16,512]{2,1,0:T(8,128)(2,1)}), bf16[32,16,512]{2,1,0:T(8,128)(2,1)S(1)}, u32[]{:S(2)}, u32[]{:S(2)}) async-start(bf16[32,16,512]{2,1,0:T(8,128)(2,1)} %scan.1), calls=%async_computation.1 | async-start | bytes 1048576 | tf_op jit(solution)/shard_map/all_to_all | solution.py:409
  58.0 1.1 %collective-permute-start.5 = (bf16[16,4096]{1,0:T(8,128)(2,1)S(1)}, bf16[16,4096]{1,0:T(8,128)(2,1)S(1)}, u32[]{:S(2)}, u32[]{:S(2)}) collective-permute-start(bf16[16,4096]{1,0:T(8,128)(2,1)S(1)} %concatenate.7), channel_id=1, source_target_pairs={{0,64},{64,128},{128,192},{192,0},{1,65},{65,129},{129,193},{193,1... | collective-permute-start | bytes 393224 | tf_op jit(solution)/shard_map/ppermute | solution.py:335
  59.3 6.8 %collective-permute-done.5.refs_3_.par = bf16[16,4096]{1,0:T(8,128)(2,1)S(1)} collective-permute-done((bf16[16,4096]{1,0:T(8,128)(2,1)S(1)}, bf16[16,4096]{1,0:T(8,128)(2,1)S(1)}, u32[]{:S(2)}, u32[]{:S(2)}) %collective-permute-start.5) | collective-permute-done | bytes 131104 | tf_op jit(solution)/shard_map/ppermute | solution.py:335
  66.1 2.8 %collective-permute-done.3.refs_1_.pack = bf16[16,16,256]{2,1,0:T(8,128)(2,1)S(1)} collective-permute-done((bf16[16,16,256]{2,1,0:T(8,128)(2,1)S(1)}, bf16[16,16,256]{2,1,0:T(8,128)(2,1)S(1)}, u32[]{:S(2)}, u32[]{:S(2)}) %collective-permute-start.3) | collective-permute-done | bytes 131104 | tf_op jit(solution)/shard_map/ppermute | solution.py:335
  68.9 2.6 %all-to-all-done.1 = bf16[32,16,512]{2,1,0:T(8,128)(2,1)S(1)} async-done(((bf16[32,16,512]{2,1,0:T(8,128)(2,1)}), bf16[32,16,512]{2,1,0:T(8,128)(2,1)S(1)}, u32[]{:S(2)}, u32[]{:S(2)}) %all-to-all-start.1) | async-done | bytes 524320 | tf_op jit(solution)/shard_map/all_to_all | solution.py:409
  71.6 1.0 %collective-permute-start.6 = (bf16[32,16,512]{2,1,0:T(8,128)(2,1)S(1)}, bf16[32,16,512]{2,1,0:T(8,128)(2,1)S(1)}, u32[]{:S(2)}, u32[]{:S(2)}) collective-permute-start(bf16[32,16,512]{2,1,0:T(8,128)(2,1)S(1)} %all-to-all-done.1), channel_id=1, source_target_pairs={{0,64},{64,128},{128,192},{192,0},{1,65},{65,129},{129,193},{193,1... | collective-permute-start | bytes 1572872 | tf_op jit(solution)/shard_map/ppermute | solution.py:335
  72.6 9.8 %inner.1 = (f32[256,4096]{1,0:T(8,128)S(1)}, bf16[256,128]{1,0:T(8,128)(2,1)S(1)}, bf16[256,4096]{1,0:T(8,128)(2,1)S(1)}, bf16[144,2048]{1,0:T(8,128)(2,1)S(1)}, bf16[144,2048]{1,0:T(8,128)(2,1)S(1)}) custom-call(bf16[256,4096]{1,0:T(8,128)(2,1)} %mark.2.u, bf16[16,16,256]{2,1,0:T(8,128)(2,1)S(1)} %collective-permute-done.3.refs_1_.pack, ...), custom_call_target="tpu_custom_call" | custom-call | flops 1 | bytes 1 | tf_op jit(solution)/shard_map/inner/pallas_call | solution.py:416
  82.3 1.5 %collective-permute-start.7 = (bf16[144,2048]{1,0:T(8,128)(2,1)S(1)}, bf16[144,2048]{1,0:T(8,128)(2,1)S(1)}, u32[]{:S(2)}, u32[]{:S(2)}) collective-permute-start(bf16[144,2048]{1,0:T(8,128)(2,1)S(1)} %get-tuple-element.39), channel_id=1, source_target_pairs={{0,1},{2,3},{4,5},{6,7},{8,9},{10,11},{12,13},{14,15},{16,17},{18,... | collective-permute-start | bytes 1769480 | tf_op jit(solution)/shard_map/ppermute | solution.py:441
  83.8 6.1 %collective-permute-done.7.lead_fresh = bf16[144,2048]{1,0:T(8,128)(2,1)S(1)} collective-permute-done((bf16[144,2048]{1,0:T(8,128)(2,1)S(1)}, bf16[144,2048]{1,0:T(8,128)(2,1)S(1)}, u32[]{:S(2)}, u32[]{:S(2)}) %collective-permute-start.7) | collective-permute-done | bytes 589856 | tf_op jit(solution)/shard_map/ppermute | solution.py:441
  89.9 0.9 start.1
  91.0 2.8 %outer_mine.1.done = bf16[256,4096]{1,0:T(8,128)(2,1)} custom-call(s32[3]{0:T(128)S(1)} %pad_add_fusion.flags, bf16[256,4096]{1,0:T(8,128)(2,1)S(1)} %get-tuple-element.35.u, f32[256,4096]{1,0:T(8,128)S(1)} %get-tuple-element.36.partial, bf16[128,2048]{1,0:T(8,128)(2,1)S(1)} %get-tuple-element.42.starts, ...), custom_call_target="tpu_custom_call" | custom-call | flops 600000000 | bytes 5000000 | tf_op jit(solution)/shard_map/outer_mine/pallas_call | solution.py:449
  93.9 2.8 %outer_other.1 = bf16[256,4096]{1,0:T(8,128)(2,1)} custom-call(s32[3]{0:T(128)S(1)} %pad_add_fusion.flags, bf16[256,4096]{1,0:T(8,128)(2,1)S(1)} %get-tuple-element.35.u, f32[256,4096]{1,0:T(8,128)S(1)} %get-tuple-element.36.partial, bf16[128,2048]{1,0:T(8,128)(2,1)S(1)} %collective-permute-done.8.starts, ...), custom_call_target="tpu_custom_call", output_to_operand_aliasing={{}: (7, {})} | custom-call | flops 600000000 | bytes 5000000 | tf_op jit(solution)/shard_map/outer_other/pallas_call | solution.py:459
  (35 shorter events, 1.9 us)
Async XLA Ops:
  0.0 32.1 %copy-start = (f32[1,64,128,64]{2,3,1,0:T(8,128)S(1)}, f32[1,64,128,64]{2,3,1,0:T(8,128)}, u32[]{:S(2)}) copy-start(f32[1,64,128,64]{2,3,1,0:T(8,128)} %param.16) | copy-start | bytes 6291460
  1.1 7.4 %collective-permute-start = (bf16[16,4096]{1,0:T(8,128)(2,1)S(1)}, bf16[16,4096]{1,0:T(8,128)(2,1)S(1)}, u32[]{:S(2)}, u32[]{:S(2)}) collective-permute-start(bf16[16,4096]{1,0:T(8,128)(2,1)S(1)} %slice_bitcast_fusion), channel_id=1, source_target_pairs={{0,1},{1,2},{2,3},{3,4},{4,5},{5,6},{6,7},{7,8},{8,9},{9,10},{10,1... | collective-permute-start | bytes 393224 | tf_op jit(solution)/shard_map/ppermute | solution.py:342
  6.1 2.3 %copy-start.3 = (f32[1,256,64]{1,2,0:T(8,128)S(1)}, f32[1,256,64]{1,2,0:T(8,128)}, u32[]{:S(2)}) copy-start(f32[1,256,64]{1,2,0:T(8,128)} %param.13) | copy-start | bytes 196612
  6.1 2.3 %copy-start.4 = (f32[1,256,64]{1,2,0:T(8,128)S(1)}, f32[1,256,64]{1,2,0:T(8,128)}, u32[]{:S(2)}) copy-start(f32[1,256,64]{1,2,0:T(8,128)} %param.12) | copy-start | bytes 196612
  6.1 2.3 %copy-start.1 = (bf16[1,3,4352]{2,1,0:T(4,128)(2,1)S(1)}, bf16[1,3,4352]{2,1,0:T(4,128)(2,1)}, u32[]{:S(2)}) copy-start(bf16[1,3,4352]{2,1,0:T(4,128)(2,1)} %param.17) | copy-start | bytes 78340
  6.1 2.3 %copy-start.2 = (bf16[1,4,4352]{2,1,0:T(4,128)(2,1)S(1)}, bf16[1,4,4352]{2,1,0:T(4,128)(2,1)}, u32[]{:S(2)}) copy-start(bf16[1,4,4352]{2,1,0:T(4,128)(2,1)} %param.11) | copy-start | bytes 104452
  12.2 5.3 %collective-permute-start.1 = (bf16[144,2048]{1,0:T(8,128)(2,1)S(1)}, bf16[144,2048]{1,0:T(8,128)(2,1)S(1)}, u32[]{:S(2)}, u32[]{:S(2)}) collective-permute-start(bf16[144,2048]{1,0:T(8,128)(2,1)S(1)} %get-tuple-element.29), channel_id=1, source_target_pairs={{0,1},{1,0},{2,3},{3,2},{4,5},{5,4},{6,7},{7,6},{8,9},{9,8},{10,11... | collective-permute-start | bytes 1769480 | tf_op jit(solution)/shard_map/ppermute | solution.py:338
  12.3 47.1 %collective-permute-start.4 = (f32[128,256]{1,0:T(8,128)S(1)}, f32[128,256]{1,0:T(8,128)S(1)}, u32[]{:S(2)}, u32[]{:S(2)}) collective-permute-start(f32[128,256]{1,0:T(8,128)S(1)} %pad_maximum_fusion.logs), channel_id=1, source_target_pairs={{0,64},{64,128},{128,192},{192,0},{1,65},{65,129},{129,193},{193,1... | collective-permute-start | bytes 393224 | tf_op jit(solution)/shard_map/ppermute | solution.py:335
  13.7 55.3 %collective-permute-start.2 = (bf16[256,4096]{1,0:T(8,128)(2,1)}, bf16[256,4096]{1,0:T(8,128)(2,1)}, u32[]{:S(2)}, u32[]{:S(2)}) collective-permute-start(bf16[256,4096]{1,0:T(8,128)(2,1)} %bitcast.3.u), channel_id=1, source_target_pairs={{0,64},{64,128},{128,192},{192,0},{1,65},{65,129},{129,193},{193,1... | collective-permute-start | bytes 6291464 | tf_op jit(solution)/shard_map/ppermute | solution.py:335
  17.4 14.5 %copy-start.6 = (f32[1,64]{1,0:T(1,128)S(1)}, f32[1,64]{1,0:T(1,128)}, u32[]{:S(2)}) copy-start(f32[1,64]{1,0:T(1,128)} %param.14) | copy-start | bytes 772
  19.2 38.7 %copy-start.5 = (bf16[1,4096]{1,0:T(2,128)(2,1)S(1)}, bf16[1,4096]{1,0:T(2,128)(2,1)}, u32[]{:S(2)}) copy-start(bf16[1,4096]{1,0:T(2,128)(2,1)} %param.15) | copy-start | bytes 24580
  19.2 29.1 %all-to-all-start = ((bf16[32,16,640]{2,1,0:T(8,128)(2,1)}), bf16[32,16,640]{2,1,0:T(8,128)(2,1)S(1)}, u32[]{:S(2)}, u32[]{:S(2)}) async-start(bf16[32,16,640]{2,1,0:T(8,128)(2,1)} %join.1), calls=%async_computation | async-start | bytes 1310720 | tf_op jit(solution)/shard_map/all_to_all | solution.py:397
  49.4 22.2 %all-to-all-start.1 = ((bf16[32,16,512]{2,1,0:T(8,128)(2,1)}), bf16[32,16,512]{2,1,0:T(8,128)(2,1)S(1)}, u32[]{:S(2)}, u32[]{:S(2)}) async-start(bf16[32,16,512]{2,1,0:T(8,128)(2,1)} %scan.1), calls=%async_computation.1 | async-start | bytes 1048576 | tf_op jit(solution)/shard_map/all_to_all | solution.py:409
  58.0 8.1 %collective-permute-start.5 = (bf16[16,4096]{1,0:T(8,128)(2,1)S(1)}, bf16[16,4096]{1,0:T(8,128)(2,1)S(1)}, u32[]{:S(2)}, u32[]{:S(2)}) collective-permute-start(bf16[16,4096]{1,0:T(8,128)(2,1)S(1)} %concatenate.7), channel_id=1, source_target_pairs={{0,64},{64,128},{128,192},{192,0},{1,65},{65,129},{129,193},{193,1... | collective-permute-start | bytes 393224 | tf_op jit(solution)/shard_map/ppermute | solution.py:335
  59.1 9.8 %collective-permute-start.3 = (bf16[16,16,256]{2,1,0:T(8,128)(2,1)S(1)}, bf16[16,16,256]{2,1,0:T(8,128)(2,1)S(1)}, u32[]{:S(2)}, u32[]{:S(2)}) collective-permute-start(bf16[16,16,256]{2,1,0:T(8,128)(2,1)S(1)} %get-tuple-element.30), channel_id=1, source_target_pairs={{0,64},{64,128},{128,192},{192,0},{1,65},{65,129},{129,193},{193,1... | collective-permute-start | bytes 393224 | tf_op jit(solution)/shard_map/ppermute | solution.py:335
  71.6 12.3 %collective-permute-start.6 = (bf16[32,16,512]{2,1,0:T(8,128)(2,1)S(1)}, bf16[32,16,512]{2,1,0:T(8,128)(2,1)S(1)}, u32[]{:S(2)}, u32[]{:S(2)}) collective-permute-start(bf16[32,16,512]{2,1,0:T(8,128)(2,1)S(1)} %all-to-all-done.1), channel_id=1, source_target_pairs={{0,64},{64,128},{128,192},{192,0},{1,65},{65,129},{129,193},{193,1... | collective-permute-start | bytes 1572872 | tf_op jit(solution)/shard_map/ppermute | solution.py:335
  82.3 7.6 %collective-permute-start.7 = (bf16[144,2048]{1,0:T(8,128)(2,1)S(1)}, bf16[144,2048]{1,0:T(8,128)(2,1)S(1)}, u32[]{:S(2)}, u32[]{:S(2)}) collective-permute-start(bf16[144,2048]{1,0:T(8,128)(2,1)S(1)} %get-tuple-element.39), channel_id=1, source_target_pairs={{0,1},{2,3},{4,5},{6,7},{8,9},{10,11},{12,13},{14,15},{16,17},{18,... | collective-permute-start | bytes 1769480 | tf_op jit(solution)/shard_map/ppermute | solution.py:441
  90.8 3.1 %collective-permute-start.8 = (bf16[128,2048]{1,0:T(8,128)(2,1)S(1)}, bf16[128,2048]{1,0:T(8,128)(2,1)S(1)}, u32[]{:S(2)}, u32[]{:S(2)}) collective-permute-start(bf16[128,2048]{1,0:T(8,128)(2,1)S(1)} %get-tuple-element.40), channel_id=1, source_target_pairs={{0,1},{1,0},{2,3},{3,2},{4,5},{5,4},{6,7},{7,6},{8,9},{9,8},{10,11... | collective-permute-start | bytes 1572872 | tf_op jit(solution)/shard_map/ppermute | solution.py:338

commit v5 on v4

--- a/solution.py
+++ b/solution.py
@@ -187,27 +187,12 @@
         cross[:, cols] = jnp.where(lead, second, state).astype(BF16)
 
 
-def inner_kernel(
-    u, pack, par, logs, partial, decay, far_u, low_fresh, high_fresh, scores, log_col, log_row, turned_keys, to_end, ends, pad
+def inner_group(
+    q, column, par, partial, u, fresh, decay_logs, scores, turned_keys, to_end, ends, pad
 ):
-    q = pl.program_id(0)
-
-    @pl.when(q == 0)
-    def _():
-        bc = pack[...].reshape(TOK, 256)
-        scores[...] = lax.dot_general(
-            bc[:, 128:256], bc[:, 0:128], (((1,), (1,)), ((), ())), preferred_element_type=F32
-        )
-        cum = cumulated(logs[0:HEADS])
-        log_row[...] = cum * LOG2E - jnp.log2(logs[HEADS : 2 * HEADS])
-        turned = twice_turned(cum)
-        log_col[...] = turned * LOG2E
-        decay[...] = two_parts(jnp.exp(turned))
-        turned_keys[...] = bc[:, 0:128].astype(F32).T.astype(BF16)
-        to_end[...], ends[...] = end_factors(turned, twice_turned(logs[HEADS : 2 * HEADS]))
-
-    far_u[...] = u[...]
-    slab = par[...].astype(F32)
+    log_col, log_row = decay_logs
+    base = q * LANES
+    slab = par[:, pl.ds(pl.multiple_of(base, LANES), LANES)].astype(F32)
     skip = slab[5:6] + slab[6:7] + slab[7:8]
     spread = spread_matrix(2 * HEADS, q)
     scale = dot(to_end[...], spread)
@@ -219,7 +204,8 @@
     left = iota((TOK, 128), 1) < DIM
     for i in range(4):
         lane = slice(i * 128, (i + 1) * 128)
-        value = conv_silu(pad.at[i], u[:, lane], slab[:, lane], slab[0:4, lane])
+        here = pl.ds(pl.multiple_of(base + i * 128, 128), 128)
+        value = conv_silu(pad.at[i], u[:, here], slab[:, lane], slab[0:4, lane])
         scaled.append((value.astype(F32) * scale[:, lane]).astype(BF16))
         both = []
         for h in (2 * i, 2 * i + 1):
@@ -230,19 +216,46 @@
             low_right = jnp.exp2(jnp.where(causal, col[half:] - row[:, half:], -jnp.inf)) * scores[half:, half:]
             low = jnp.concatenate([low_left.astype(BF16), low_right.astype(BF16)], axis=1)
             both.append(jnp.concatenate([dot(top.astype(BF16), value[:half]), dot(low, value)], axis=0))
-        partial[:, lane] = jnp.where(left, both[0], both[1]) + skip[:, lane] * value.astype(F32)
-    fresh = dot(turned_keys[...], jnp.concatenate(scaled, axis=1)).astype(BF16)
-    end_rows = dot(ends[...], spread).astype(BF16)
-
-    @pl.when(q < 4)
-    def _():
-        low_fresh[0:STATE, :] = fresh
-        low_fresh[STATE:, :] = end_rows
-
-    @pl.when(q >= 4)
-    def _():
-        high_fresh[0:STATE, :] = fresh
-        high_fresh[STATE:, :] = end_rows
+        partial[:, here] = jnp.where(left, both[0], both[1]) + skip[:, lane] * value.astype(F32)
+    there = pl.ds(pl.multiple_of(column, LANES), LANES)
+    fresh[0:STATE, there] = dot(turned_keys[...], jnp.concatenate(scaled, axis=1)).astype(BF16)
+    fresh[STATE : STATE + ROWS, there] = dot(ends[...], spread).astype(BF16)
+
+
+def inner_kernel(
+    far, pack, par, logs, partial, decay, u, low_fresh, high_fresh,
+    scores, log_col, log_row, turned_keys, to_end, ends, pad, sems,
+):
+    copies = []
+    for i in range(4):
+        rows = pl.ds(i * 64, 64)
+        copies.append(pltpu.make_async_copy(far.at[rows], u.at[rows], sems.at[i]))
+        copies[-1].start()
+    bc = pack[...].reshape(TOK, 256)
+    scores[...] = lax.dot_general(
+        bc[:, 128:256], bc[:, 0:128], (((1,), (1,)), ((), ())), preferred_element_type=F32
+    )
+    cum = cumulated(logs[0:HEADS])
+    log_row[...] = cum * LOG2E - jnp.log2(logs[HEADS : 2 * HEADS])
+    turned = twice_turned(cum)
+    log_col[...] = turned * LOG2E
+    decay[...] = two_parts(jnp.exp(turned))
+    turned_keys[...] = bc[:, 0:128].astype(F32).T.astype(BF16)
+    to_end[...], ends[...] = end_factors(turned, twice_turned(logs[HEADS : 2 * HEADS]))
+    for copy in copies:
+        copy.wait()
+    rest = ((log_col, log_row), scores, turned_keys, to_end, ends, pad)
+
+    def low(q, _):
+        inner_group(q, q * LANES, par, partial, u, low_fresh, *rest)
+        return 0
+
+    def high(q, _):
+        inner_group(q, (q - 4) * LANES, par, partial, u, high_fresh, *rest)
+        return 0
+
+    lax.fori_loop(0, 4, low, 0)
+    lax.fori_loop(4, 8, high, 0)
 
 
 def mark_kernel(*refs):
@@ -351,7 +364,6 @@
         name="fetch",
     )(u, proj_weight[0])
     next_u = onward(u)
-    next_logs = onward(logs)
     skip = jnp.repeat(skip_gain, DIM, axis=1)
     skip_hi = exact(skip)
     skip_mid = exact(skip - skip_hi)
@@ -394,7 +406,10 @@
     pay = call(join_kernel, "join", array((CHIPS, ROWS, LANES + 128)), [vmem] * 2, vmem, estimate=cost(1e6, 2.5e6))(
         flags, keep, got
     )
+    pay, logs = lax.optimization_barrier((pay, logs))
+    next_logs = onward(logs)
     shares = lax.all_to_all(pay, ("x", "z"), 0, 0)
+    shares, next_par, next_pack, next_logs = lax.optimization_barrier((shares, next_par, next_pack, next_logs))
     head = (core * 4 + lax.axis_index("x")) * 8
     start = lax.dynamic_slice(carry_state[0], (head, lax.axis_index("z") * ROWS, 0), (8, ROWS, DIM))
     start = start.transpose(1, 0, 2).reshape(ROWS, LANES)
@@ -407,24 +422,15 @@
         name="scan",
     )(shares, start)
     chip = lax.all_to_all(back, ("x", "z"), 0, 0)
-    next_u = mark(next_u, next_pack, next_logs, next_par)
-    chip, next_u, next_pack, next_logs, next_par = lax.optimization_barrier(
-        (chip, next_u, next_pack, next_logs, next_par)
-    )
+    next_u = mark(next_u)
+    chip, next_u = lax.optimization_barrier((chip, next_u))
     next_chip = onward(chip)
     next_chip = mark(next_chip)
     partial, decay, far_u, low_fresh, high_fresh = pl.pallas_call(
         inner_kernel,
-        grid=(GROUPS,),
         out_shape=(array((TOK, CH), F32), array((TOK, 128)), array((TOK, CH)), fresh_out, fresh_out),
-        in_specs=[columns(TOK), whole(16, 16, 256), columns(16), whole(128, TOK)],
-        out_specs=[
-            columns(TOK),
-            whole(TOK, 128),
-            columns(TOK),
-            pl.BlockSpec((STATE + ROWS, LANES), lambda q: (0, jnp.minimum(q, 3))),
-            pl.BlockSpec((STATE + ROWS, LANES), lambda q: (0, jnp.maximum(q - 4, 0))),
-        ],
+        in_specs=[anywhere] + [vmem] * 3,
+        out_specs=[vmem] * 5,
         scratch_shapes=[
             pltpu.VMEM((TOK, TOK), F32),
             pltpu.VMEM((TOK, 128), F32),
@@ -433,6 +439,7 @@
             pltpu.VMEM((TOK, 128), BF16),
             pltpu.VMEM((ROWS, 128), BF16),
             pad,
+            pltpu.SemaphoreType.DMA((4,)),
         ],
         compiler_params=params(20),
         cost_estimate=cost(1, 1),

time: 97.3 us -> 113 us (1.16); the launches traced: 96.9 us -> 111 us
  waiting for transfers between devices: 32.5 us -> 42.3 us
  local copies, waits for them, and re-layouts: 3.32 us -> 11.9 us
  starting transfers between devices: 32.8 us -> 30.4 us
  Pallas kernels: 27.6 us -> 26.2 us
    ppermute x5, waiting for transfers between devices: 9.6 us -> 23.8 us  [onward(): return lax.ppermute(value, 'section', [(i, (i + 1) % 4) for i in range(4)])]
    all_to_all x1, waiting for transfers between devices: 14.2 us -> 0.01 us  [per_device(): shares = lax.all_to_all(pay, ('x', 'z'), 0, 0)]
    all_to_all x1, waiting for transfers between devices: 2.64 us -> 14.1 us  [per_device(): chip = lax.all_to_all(back, ('x', 'z'), 0, 0)]
    unnamed x14 -> x24, local copies, waits for them, and re-layouts: 0.03 us -> 7.42 us
    all_to_all x1, starting transfers between devices: 12.7 us -> 10.1 us  [per_device(): shares = lax.all_to_all(pay, ('x', 'z'), 0, 0)]
    ppermute x1, waiting for transfers between devices: 6.09 us -> 4.31 us  [per_device(): lead_fresh = lax.ppermute(high_fresh, 'core', [(0, 1)])]
    all_to_all x1, starting transfers between devices: 8.43 us -> 9.84 us  [per_device(): chip = lax.all_to_all(back, ('x', 'z'), 0, 0)]
    concatenate x1, local copies, waits for them, and re-layouts: 0.16 us -> 1.39 us  [per_device(): jnp.concatenate([conv_weight[0, :, :CH], norm_gain] + [piece.astype(BF16)...]
  transfers between devices with their start and end apart: 11 -> 11, of which waited for: 5 -> 6; matrix products, arithmetic and copies ran while one was open for 2% -> 3% of each run, Pallas kernels for 21% -> 17%
where the time goes in v5:
time: 113 us; the launch traced here: 111 us
  waiting for transfers between devices  42.3 us (37%)
  starting transfers between devices  30.4 us (27%)
  Pallas kernels  26.2 us (23%)
  local copies, waits for them, and re-layouts  11.9 us (11%)
    ppermute x5, waiting for transfers between devices, onward(): return lax.ppermute(value, 'section', [(i, (i + 1) % 4) for i in range(4)])  23.8 us
    all_to_all x1, waiting for transfers between devices, per_device(): chip = lax.all_to_all(back, ('x', 'z'), 0, 0)  14.1 us
    all_to_all x1, starting transfers between devices, per_device(): shares = lax.all_to_all(pay, ('x', 'z'), 0, 0)  10.1 us
    all_to_all x1, starting transfers between devices, per_device(): chip = lax.all_to_all(back, ('x', 'z'), 0, 0)  9.84 us
    pallas_call x1, Pallas kernels, per_device(): pl.pallas_call(inner_kernel, out_shape=(array((TOK, CH), F32), array((TOK...  8.95 us
    unnamed x24, local copies, waits for them, and re-layouts  7.42 us
    ppermute x1, starting transfers between devices, per_device(): behind = lax.ppermute(u[TOK - 16:], ctx, [(i, i + 1) for i in range(63)])  4.94 us
    ppermute x1, waiting for transfers between devices, per_device(): lead_fresh = lax.ppermute(high_fresh, 'core', [(0, 1)])  4.31 us
  transfers between devices with their start and end apart: 11, of which 6 were waited for; matrix products, arithmetic and copies ran while one was open for 3% of the time, Pallas kernels for 17%

profile of v5, /device:TPU:1, one launch (start us, length us, event | category | flops | bytes accessed | tf_op | source)
XLA Modules:
  0.0 111.4 jit_solution(17535505429210372104)
XLA Ops:
  1.1 4.9 %collective-permute-start = (bf16[16,4096]{1,0:T(8,128)(2,1)S(1)}, bf16[16,4096]{1,0:T(8,128)(2,1)S(1)}, u32[]{:S(2)}, u32[]{:S(2)}) collective-permute-start(bf16[16,4096]{1,0:T(8,128)(2,1)S(1)} %slice_bitcast_fusion), channel_id=1, source_target_pairs={{0,1},{1,2},{2,3},{3,4},{4,5},{5,6},{6,7},{7,8},{8,9},{9,10},{10,1... | collective-permute-start | bytes 393224 | tf_op jit(solution)/shard_map/ppermute | solution.py:355
  6.0 1.4 %collective-permute-start.5 = (bf16[256,4096]{1,0:T(8,128)(2,1)}, bf16[256,4096]{1,0:T(8,128)(2,1)}, u32[]{:S(2)}, u32[]{:S(2)}) collective-permute-start(bf16[256,4096]{1,0:T(8,128)(2,1)} %bitcast.27), channel_id=1, source_target_pairs={{0,64},{64,128},{128,192},{192,0},{1,65},{65,129},{129,193},{193,1... | collective-permute-start | bytes 6291464 | tf_op jit(solution)/shard_map/ppermute | solution.py:348
  7.5 1.6 %copy-done.3 = bf16[1,256,4096]{2,1,0:T(8,128)(2,1)S(1)} copy-done((bf16[1,256,4096]{2,1,0:T(8,128)(2,1)S(1)}, bf16[1,256,4096]{2,1,0:T(8,128)(2,1)}, u32[]{:S(2)}) %copy-start.3) | copy-done | bytes 2097176
  9.1 1.7 %fetch.1 = (bf16[256,4096]{1,0:T(8,128)(2,1)S(1)}, bf16[4096,256]{1,0:T(8,128)(2,1)S(1)}) custom-call(bf16[256,4096]{1,0:T(8,128)(2,1)S(1)} %bitcast.28, bf16[4096,256]{1,0:T(8,128)(2,1)} %bitcast.33), custom_call_target="tpu_custom_call" | custom-call | flops 1000000000 | bytes 10000000 | tf_op jit(solution)/shard_map/fetch/pallas_call | solution.py:356
  10.8 1.3 %copy-done.1 = bf16[256,4096]{1,0:T(8,128)(2,1)} copy-done((bf16[256,4096]{1,0:T(8,128)(2,1)}, bf16[256,4096]{1,0:T(8,128)(2,1)S(1)}, u32[]{:S(2)}) %copy-start.1) | copy-done | bytes 2097176
  12.1 1.3 %copy-done.4 = bf16[4096,256]{1,0:T(8,128)(2,1)} copy-done((bf16[4096,256]{1,0:T(8,128)(2,1)}, bf16[4096,256]{1,0:T(8,128)(2,1)S(1)}, u32[]{:S(2)}) %copy-start.4) | copy-done | bytes 2097176
  13.7 1.6 %copy-done.2 = bf16[256,4096]{1,0:T(8,128)(2,1)S(1)} copy-done((bf16[256,4096]{1,0:T(8,128)(2,1)S(1)}, bf16[256,4096]{1,0:T(8,128)(2,1)}, u32[]{:S(2)}) %copy-start.2) | copy-done | bytes 2097176
  15.2 1.6 %copy-done.5 = bf16[4096,256]{1,0:T(8,128)(2,1)S(1)} copy-done((bf16[4096,256]{1,0:T(8,128)(2,1)S(1)}, bf16[4096,256]{1,0:T(8,128)(2,1)}, u32[]{:S(2)}) %copy-start.5) | copy-done | bytes 2097176
  16.8 3.7 %send.1 = (bf16[144,2048]{1,0:T(8,128)(2,1)S(1)}, bf16[128,256]{1,0:T(8,128)(2,1)S(1)}, bf16[16,16,256]{2,1,0:T(8,128)(2,1)S(1)}, bf16[256,128]{1,0:T(8,128)(2,1)S(1)}, bf16[16,128]{1,0:T(8,128)(2,1)S(1)}) custom-call(s32[3]{0:T(128)S(1)} %pad_add_fusion.flags, bf16[256,4096]{1,0:T(8,128)(2,1)S(1)} %copy-done.2, bf16[4096,256]{1,0:T(8,128)(2,1)S(1)} %copy-done.5, ...), custom_call_target="tpu_custom_call" | custom-call | flops 600000000 | bytes 4500000 | tf_op jit(solution)/shard_map/send/pallas_call | solution.py:380
  20.7 2.5 %keep.1 = bf16[144,2048]{1,0:T(8,128)(2,1)S(1)} custom-call(s32[3]{0:T(128)S(1)} %pad_add_fusion.flags, bf16[256,4096]{1,0:T(8,128)(2,1)S(1)} %copy-done.2, bf16[16,4096]{1,0:T(8,128)(2,1)S(1)} %collective-permute-done.behind, bf16[3,4352]{1,0:T(4,128)(2,1)S(1)} %bitcast.30, bf16[4,4352]{1,0:T(4,128)(2,1)S(1)} %bitcast.32, ...), custom_call_target="tpu_custom_call" | custom-call | flops 600000000 | bytes 4500000 | tf_op jit(solution)/shard_map/keep/pallas_call | solution.py:397
  23.2 1.7 %join.1 = bf16[32,16,640]{2,1,0:T(8,128)(2,1)} custom-call(s32[3]{0:T(128)S(1)} %pad_add_fusion.flags, bf16[144,2048]{1,0:T(8,128)(2,1)S(1)} %keep.1, bf16[144,2048]{1,0:T(8,128)(2,1)S(1)} %collective-permute-done.1.got), custom_call_target="tpu_custom_call" | custom-call | flops 1000000 | bytes 2500000 | tf_op jit(solution)/shard_map/join/pallas_call | solution.py:406
  24.9 10.1 %all-to-all-start = ((bf16[32,16,640]{2,1,0:T(8,128)(2,1)}), bf16[32,16,640]{2,1,0:T(8,128)(2,1)S(1)}, u32[]{:S(2)}, u32[]{:S(2)}) async-start(bf16[32,16,640]{2,1,0:T(8,128)(2,1)} %join.1), calls=%async_computation | async-start | bytes 1310720 | tf_op jit(solution)/shard_map/all_to_all | solution.py:411
  35.1 1.4 %concatenate.7 = bf16[16,4096]{1,0:T(8,128)(2,1)} concatenate(bf16[4,4096]{1,0:T(4,128)(2,1)S(1)} %slice_bitcast_fusion.1, bf16[1,4096]{1,0:T(2,128)(2,1)S(1)} %copy-done.10, bf16[1,4096]{1,0:T(2,128)(2,1)S(1)} %get-tuple-element.51, bf16[1,4096]{1,0:T(2,128)(2,1)S(1)} %get-tuple-element.50, bf16[1,4096]{1,0:T(2,128)(2,1)S(1)} %get-tuple-element.49, ...), dimensions={0} | concatenate | bytes 262144 | tf_op jit(solution)/shard_map/concatenate | solution.py:371
  36.5 1.3 %collective-permute-start.2 = (bf16[16,4096]{1,0:T(8,128)(2,1)}, bf16[16,4096]{1,0:T(8,128)(2,1)S(1)}, u32[]{:S(2)}, u32[]{:S(2)}) collective-permute-start(bf16[16,4096]{1,0:T(8,128)(2,1)} %concatenate.7), channel_id=1, source_target_pairs={{0,64},{64,128},{128,192},{192,0},{1,65},{65,129},{129,193},{193,1... | collective-permute-start | bytes 393224 | tf_op jit(solution)/shard_map/ppermute | solution.py:348
  40.7 17.3 %collective-permute-done.2.par = bf16[16,4096]{1,0:T(8,128)(2,1)S(1)} collective-permute-done((bf16[16,4096]{1,0:T(8,128)(2,1)}, bf16[16,4096]{1,0:T(8,128)(2,1)S(1)}, u32[]{:S(2)}, u32[]{:S(2)}) %collective-permute-start.2) | collective-permute-done | bytes 131104 | tf_op jit(solution)/shard_map/ppermute | solution.py:348
  58.0 2.8 %collective-permute-done.3.pack = bf16[16,16,256]{2,1,0:T(8,128)(2,1)S(1)} collective-permute-done((bf16[16,16,256]{2,1,0:T(8,128)(2,1)S(1)}, bf16[16,16,256]{2,1,0:T(8,128)(2,1)S(1)}, u32[]{:S(2)}, u32[]{:S(2)}) %collective-permute-start.3) | collective-permute-done | bytes 131104 | tf_op jit(solution)/shard_map/ppermute | solution.py:348
  60.8 2.8 %collective-permute-done.4.logs = f32[128,256]{1,0:T(8,128)S(1)} collective-permute-done((f32[128,256]{1,0:T(8,128)S(1)}, f32[128,256]{1,0:T(8,128)S(1)}, u32[]{:S(2)}, u32[]{:S(2)}) %collective-permute-start.4) | collective-permute-done | bytes 131104 | tf_op jit(solution)/shard_map/ppermute | solution.py:348
  64.8 9.8 %all-to-all-start.1 = ((bf16[32,16,512]{2,1,0:T(8,128)(2,1)}), bf16[32,16,512]{2,1,0:T(8,128)(2,1)}, u32[]{:S(2)}, u32[]{:S(2)}) async-start(bf16[32,16,512]{2,1,0:T(8,128)(2,1)} %scan.1), calls=%async_computation.1 | async-start | bytes 1048576 | tf_op jit(solution)/shard_map/all_to_all | solution.py:424
  74.7 14.1 %all-to-all-done.1 = bf16[32,16,512]{2,1,0:T(8,128)(2,1)} async-done(((bf16[32,16,512]{2,1,0:T(8,128)(2,1)}), bf16[32,16,512]{2,1,0:T(8,128)(2,1)}, u32[]{:S(2)}, u32[]{:S(2)}) %all-to-all-start.1) | async-done | bytes 524320 | tf_op jit(solution)/shard_map/all_to_all | solution.py:424
  88.9 8.9 %inner.1 = (f32[256,4096]{1,0:T(8,128)S(1)}, bf16[256,128]{1,0:T(8,128)(2,1)S(1)}, bf16[256,4096]{1,0:T(8,128)(2,1)S(1)}, bf16[144,2048]{1,0:T(8,128)(2,1)S(1)}, bf16[144,2048]{1,0:T(8,128)(2,1)S(1)}) custom-call(bf16[256,4096]{1,0:T(8,128)(2,1)} %mark.2.far, bf16[16,16,256]{2,1,0:T(8,128)(2,1)S(1)} %collective-permute-done.3.pack, ...), custom_call_target="tpu_custom_call" | custom-call | flops 1 | bytes 1 | tf_op jit(solution)/shard_map/inner/pallas_call | solution.py:429
  97.9 1.3 %collective-permute-start.7 = (bf16[144,2048]{1,0:T(8,128)(2,1)S(1)}, bf16[144,2048]{1,0:T(8,128)(2,1)S(1)}, u32[]{:S(2)}, u32[]{:S(2)}) collective-permute-start(bf16[144,2048]{1,0:T(8,128)(2,1)S(1)} %get-tuple-element.45), channel_id=1, source_target_pairs={{0,1},{2,3},{4,5},{6,7},{8,9},{10,11},{12,13},{14,15},{16,17},{18,... | collective-permute-start | bytes 1769480 | tf_op jit(solution)/shard_map/ppermute | solution.py:448
  100.1 4.3 %collective-permute-done.7.lead_fresh = bf16[144,2048]{1,0:T(8,128)(2,1)S(1)} collective-permute-done((bf16[144,2048]{1,0:T(8,128)(2,1)S(1)}, bf16[144,2048]{1,0:T(8,128)(2,1)S(1)}, u32[]{:S(2)}, u32[]{:S(2)}) %collective-permute-start.7) | collective-permute-done | bytes 589856 | tf_op jit(solution)/shard_map/ppermute | solution.py:448
  105.5 2.8 %outer_mine.1.done = bf16[256,4096]{1,0:T(8,128)(2,1)} custom-call(s32[3]{0:T(128)S(1)} %pad_add_fusion.flags, bf16[256,4096]{1,0:T(8,128)(2,1)S(1)} %get-tuple-element.41.u, f32[256,4096]{1,0:T(8,128)S(1)} %get-tuple-element.42.partial, bf16[128,2048]{1,0:T(8,128)(2,1)S(1)} %get-tuple-element.48.starts, ...), custom_call_target="tpu_custom_call" | custom-call | flops 600000000 | bytes 5000000 | tf_op jit(solution)/shard_map/outer_mine/pallas_call | solution.py:456
  108.4 2.8 %outer_other.1 = bf16[256,4096]{1,0:T(8,128)(2,1)} custom-call(s32[3]{0:T(128)S(1)} %pad_add_fusion.flags, bf16[256,4096]{1,0:T(8,128)(2,1)S(1)} %get-tuple-element.41.u, f32[256,4096]{1,0:T(8,128)S(1)} %get-tuple-element.42.partial, bf16[128,2048]{1,0:T(8,128)(2,1)S(1)} %collective-permute-done.8.starts, ...), custom_call_target="tpu_custom_call", output_to_operand_aliasing={{}: (7, {})} | custom-call | flops 600000000 | bytes 5000000 | tf_op jit(solution)/shard_map/outer_other/pallas_call | solution.py:466
  (45 shorter events, 7.8 us)
Async XLA Ops:
  0.0 38.9 %copy-start = (f32[1,64,128,64]{2,3,1,0:T(8,128)S(1)}, f32[1,64,128,64]{2,3,1,0:T(8,128)}, u32[]{:S(2)}) copy-start(f32[1,64,128,64]{2,3,1,0:T(8,128)} %param.16) | copy-start | bytes 6291460
  1.1 12.5 %collective-permute-start = (bf16[16,4096]{1,0:T(8,128)(2,1)S(1)}, bf16[16,4096]{1,0:T(8,128)(2,1)S(1)}, u32[]{:S(2)}, u32[]{:S(2)}) collective-permute-start(bf16[16,4096]{1,0:T(8,128)(2,1)S(1)} %slice_bitcast_fusion), channel_id=1, source_target_pairs={{0,1},{1,2},{2,3},{3,4},{4,5},{5,6},{6,7},{7,8},{8,9},{9,10},{10,1... | collective-permute-start | bytes 393224 | tf_op jit(solution)/shard_map/ppermute | solution.py:355
  6.0 68.6 %collective-permute-start.5 = (bf16[256,4096]{1,0:T(8,128)(2,1)}, bf16[256,4096]{1,0:T(8,128)(2,1)}, u32[]{:S(2)}, u32[]{:S(2)}) collective-permute-start(bf16[256,4096]{1,0:T(8,128)(2,1)} %bitcast.27), channel_id=1, source_target_pairs={{0,64},{64,128},{128,192},{192,0},{1,65},{65,129},{129,193},{193,1... | collective-permute-start | bytes 6291464 | tf_op jit(solution)/shard_map/ppermute | solution.py:348
  7.5 1.6 %copy-start.3 = (bf16[1,256,4096]{2,1,0:T(8,128)(2,1)S(1)}, bf16[1,256,4096]{2,1,0:T(8,128)(2,1)}, u32[]{:S(2)}) copy-start(bf16[1,256,4096]{2,1,0:T(8,128)(2,1)} %param.9) | copy-start | bytes 6291460
  9.1 4.3 %copy-start.11 = (f32[1,64]{1,0:T(1,128)S(1)}, f32[1,64]{1,0:T(1,128)}, u32[]{:S(2)}) copy-start(f32[1,64]{1,0:T(1,128)} %param.14) | copy-start | bytes 772
  9.1 4.5 %copy-start.8 = (f32[1,256,64]{1,2,0:T(8,128)S(1)}, f32[1,256,64]{1,2,0:T(8,128)}, u32[]{:S(2)}) copy-start(f32[1,256,64]{1,2,0:T(8,128)} %param.13) | copy-start | bytes 196612
  9.1 4.5 %copy-start.9 = (f32[1,256,64]{1,2,0:T(8,128)S(1)}, f32[1,256,64]{1,2,0:T(8,128)}, u32[]{:S(2)}) copy-start(f32[1,256,64]{1,2,0:T(8,128)} %param.12) | copy-start | bytes 196612
  9.1 4.6 %copy-start.6 = (bf16[1,3,4352]{2,1,0:T(4,128)(2,1)S(1)}, bf16[1,3,4352]{2,1,0:T(4,128)(2,1)}, u32[]{:S(2)}) copy-start(bf16[1,3,4352]{2,1,0:T(4,128)(2,1)} %param.17) | copy-start | bytes 78340
  9.1 4.6 %copy-start.7 = (bf16[1,4,4352]{2,1,0:T(4,128)(2,1)S(1)}, bf16[1,4,4352]{2,1,0:T(4,128)(2,1)}, u32[]{:S(2)}) copy-start(bf16[1,4,4352]{2,1,0:T(4,128)(2,1)} %param.11) | copy-start | bytes 104452
  10.8 1.3 %copy-start.1 = (bf16[256,4096]{1,0:T(8,128)(2,1)}, bf16[256,4096]{1,0:T(8,128)(2,1)S(1)}, u32[]{:S(2)}) copy-start(bf16[256,4096]{1,0:T(8,128)(2,1)S(1)} %get-tuple-element.27.u) | copy-start | bytes 6291460
  12.1 1.3 %copy-start.4 = (bf16[4096,256]{1,0:T(8,128)(2,1)}, bf16[4096,256]{1,0:T(8,128)(2,1)S(1)}, u32[]{:S(2)}) copy-start(bf16[4096,256]{1,0:T(8,128)(2,1)S(1)} %get-tuple-element.28.weight) | copy-start | bytes 6291460
  13.6 1.6 %copy-start.2 = (bf16[256,4096]{1,0:T(8,128)(2,1)S(1)}, bf16[256,4096]{1,0:T(8,128)(2,1)}, u32[]{:S(2)}) copy-start(bf16[256,4096]{1,0:T(8,128)(2,1)} %copy-done.1) | copy-start | bytes 6291460
  15.2 1.6 %copy-start.5 = (bf16[4096,256]{1,0:T(8,128)(2,1)S(1)}, bf16[4096,256]{1,0:T(8,128)(2,1)}, u32[]{:S(2)}) copy-start(bf16[4096,256]{1,0:T(8,128)(2,1)} %copy-done.4) | copy-start | bytes 6291460
  20.5 2.6 %collective-permute-start.1 = (bf16[144,2048]{1,0:T(8,128)(2,1)S(1)}, bf16[144,2048]{1,0:T(8,128)(2,1)S(1)}, u32[]{:S(2)}, u32[]{:S(2)}) collective-permute-start(bf16[144,2048]{1,0:T(8,128)(2,1)S(1)} %get-tuple-element.32), channel_id=1, source_target_pairs={{0,1},{1,0},{2,3},{3,2},{4,5},{5,4},{6,7},{7,6},{8,9},{9,8},{10,11... | collective-permute-start | bytes 1769480 | tf_op jit(solution)/shard_map/ppermute | solution.py:351
  23.1 12.0 %copy-start.10 = (bf16[1,4096]{1,0:T(2,128)(2,1)S(1)}, bf16[1,4096]{1,0:T(2,128)(2,1)}, u32[]{:S(2)}) copy-start(bf16[1,4096]{1,0:T(2,128)(2,1)} %param.15) | copy-start | bytes 24580
  24.9 38.8 %all-to-all-start = ((bf16[32,16,640]{2,1,0:T(8,128)(2,1)}), bf16[32,16,640]{2,1,0:T(8,128)(2,1)S(1)}, u32[]{:S(2)}, u32[]{:S(2)}) async-start(bf16[32,16,640]{2,1,0:T(8,128)(2,1)} %join.1), calls=%async_computation | async-start | bytes 1310720 | tf_op jit(solution)/shard_map/all_to_all | solution.py:411
  36.5 21.5 %collective-permute-start.2 = (bf16[16,4096]{1,0:T(8,128)(2,1)}, bf16[16,4096]{1,0:T(8,128)(2,1)S(1)}, u32[]{:S(2)}, u32[]{:S(2)}) collective-permute-start(bf16[16,4096]{1,0:T(8,128)(2,1)} %concatenate.7), channel_id=1, source_target_pairs={{0,64},{64,128},{128,192},{192,0},{1,65},{65,129},{129,193},{193,1... | collective-permute-start | bytes 393224 | tf_op jit(solution)/shard_map/ppermute | solution.py:348
  37.8 23.0 %collective-permute-start.3 = (bf16[16,16,256]{2,1,0:T(8,128)(2,1)S(1)}, bf16[16,16,256]{2,1,0:T(8,128)(2,1)S(1)}, u32[]{:S(2)}, u32[]{:S(2)}) collective-permute-start(bf16[16,16,256]{2,1,0:T(8,128)(2,1)S(1)} %get-tuple-element.34), channel_id=1, source_target_pairs={{0,64},{64,128},{128,192},{192,0},{1,65},{65,129},{129,193},{193,1... | collective-permute-start | bytes 393224 | tf_op jit(solution)/shard_map/ppermute | solution.py:348
  38.8 24.8 %collective-permute-start.4 = (f32[128,256]{1,0:T(8,128)S(1)}, f32[128,256]{1,0:T(8,128)S(1)}, u32[]{:S(2)}, u32[]{:S(2)}) collective-permute-start(f32[128,256]{1,0:T(8,128)S(1)} %pad_maximum_fusion.logs), channel_id=1, source_target_pairs={{0,64},{64,128},{128,192},{192,0},{1,65},{65,129},{129,193},{193,1... | collective-permute-start | bytes 393224 | tf_op jit(solution)/shard_map/ppermute | solution.py:348
  64.8 24.0 %all-to-all-start.1 = ((bf16[32,16,512]{2,1,0:T(8,128)(2,1)}), bf16[32,16,512]{2,1,0:T(8,128)(2,1)}, u32[]{:S(2)}, u32[]{:S(2)}) async-start(bf16[32,16,512]{2,1,0:T(8,128)(2,1)} %scan.1), calls=%async_computation.1 | async-start | bytes 1048576 | tf_op jit(solution)/shard_map/all_to_all | solution.py:424
  88.8 11.3 %collective-permute-start.6 = (bf16[32,16,512]{2,1,0:T(8,128)(2,1)}, bf16[32,16,512]{2,1,0:T(8,128)(2,1)S(1)}, u32[]{:S(2)}, u32[]{:S(2)}) collective-permute-start(bf16[32,16,512]{2,1,0:T(8,128)(2,1)} %all-to-all-done.1), channel_id=1, source_target_pairs={{0,64},{64,128},{128,192},{192,0},{1,65},{65,129},{129,193},{193,1... | collective-permute-start | bytes 1572872 | tf_op jit(solution)/shard_map/ppermute | solution.py:348
  97.9 6.5 %collective-permute-start.7 = (bf16[144,2048]{1,0:T(8,128)(2,1)S(1)}, bf16[144,2048]{1,0:T(8,128)(2,1)S(1)}, u32[]{:S(2)}, u32[]{:S(2)}) collective-permute-start(bf16[144,2048]{1,0:T(8,128)(2,1)S(1)} %get-tuple-element.45), channel_id=1, source_target_pairs={{0,1},{2,3},{4,5},{6,7},{8,9},{10,11},{12,13},{14,15},{16,17},{18,... | collective-permute-start | bytes 1769480 | tf_op jit(solution)/shard_map/ppermute | solution.py:448
  105.3 3.0 %collective-permute-start.8 = (bf16[128,2048]{1,0:T(8,128)(2,1)S(1)}, bf16[128,2048]{1,0:T(8,128)(2,1)S(1)}, u32[]{:S(2)}, u32[]{:S(2)}) collective-permute-start(bf16[128,2048]{1,0:T(8,128)(2,1)S(1)} %get-tuple-element.46), channel_id=1, source_target_pairs={{0,1},{1,0},{2,3},{3,2},{4,5},{5,4},{6,7},{7,6},{8,9},{9,8},{10,11... | collective-permute-start | bytes 1572872 | tf_op jit(solution)/shard_map/ppermute | solution.py:351

commit v6 on v5

--- a/solution.py
+++ b/solution.py
@@ -409,7 +409,6 @@
     pay, logs = lax.optimization_barrier((pay, logs))
     next_logs = onward(logs)
     shares = lax.all_to_all(pay, ("x", "z"), 0, 0)
-    shares, next_par, next_pack, next_logs = lax.optimization_barrier((shares, next_par, next_pack, next_logs))
     head = (core * 4 + lax.axis_index("x")) * 8
     start = lax.dynamic_slice(carry_state[0], (head, lax.axis_index("z") * ROWS, 0), (8, ROWS, DIM))
     start = start.transpose(1, 0, 2).reshape(ROWS, LANES)
@@ -423,7 +422,9 @@
     )(shares, start)
     chip = lax.all_to_all(back, ("x", "z"), 0, 0)
     next_u = mark(next_u)
-    chip, next_u = lax.optimization_barrier((chip, next_u))
+    chip, next_u, next_pack, next_logs, next_par = lax.optimization_barrier(
+        (chip, next_u, next_pack, next_logs, next_par)
+    )
     next_chip = onward(chip)
     next_chip = mark(next_chip)
     partial, decay, far_u, low_fresh, high_fresh = pl.pallas_call(

time: 113 us -> 95.8 us (0.85)
  local copies, waits for them, and re-layouts: 11.9 us -> 1.67 us
  waiting for transfers between devices: 42.3 us -> 33.6 us
  starting transfers between devices: 30.4 us -> 32.7 us
    all_to_all x1, waiting for transfers between devices: 0.01 us -> 16.3 us  [per_device(): shares = lax.all_to_all(pay, ('x', 'z'), 0, 0)]
    ppermute x5, waiting for transfers between devices: 23.8 us -> 9.09 us  [onward(): return lax.ppermute(value, 'section', [(i, (i + 1) % 4) for i in range(4)])]
    all_to_all x1, waiting for transfers between devices: 14.1 us -> 2.28 us  [per_device(): chip = lax.all_to_all(back, ('x', 'z'), 0, 0)]
    unnamed x24 -> x14, local copies, waits for them, and re-layouts: 7.42 us -> 0.03 us
    all_to_all x1, starting transfers between devices: 10.1 us -> 12.7 us  [per_device(): shares = lax.all_to_all(pay, ('x', 'z'), 0, 0)]
    all_to_all x1, starting transfers between devices: 9.84 us -> 8.26 us  [per_device(): chip = lax.all_to_all(back, ('x', 'z'), 0, 0)]
    ppermute x1, waiting for transfers between devices: 4.31 us -> 5.86 us  [per_device(): lead_fresh = lax.ppermute(high_fresh, 'core', [(0, 1)])]
    ppermute x5, starting transfers between devices: 3.87 us -> 5.15 us  [onward(): return lax.ppermute(value, 'section', [(i, (i + 1) % 4) for i in range(4)])]
  transfers between devices with their start and end apart: 11 -> 11, of which waited for: 6 -> 7; matrix products, arithmetic and copies ran while one was open for 3% -> 1% of each run, Pallas kernels for 17% -> 20%
where the time goes in v6:
time: 95.8 us; the launch traced here: 95.3 us
  waiting for transfers between devices  33.6 us (35%)
  starting transfers between devices  32.7 us (34%)
  Pallas kernels  26.8 us (28%)
  local copies, waits for them, and re-layouts  1.67 us (2%)
    all_to_all x1, waiting for transfers between devices, per_device(): shares = lax.all_to_all(pay, ('x', 'z'), 0, 0)  16.3 us
    all_to_all x1, starting transfers between devices, per_device(): shares = lax.all_to_all(pay, ('x', 'z'), 0, 0)  12.7 us
    ppermute x5, waiting for transfers between devices, onward(): return lax.ppermute(value, 'section', [(i, (i + 1) % 4) for i in range(4)])  9.09 us
    pallas_call x1, Pallas kernels, per_device(): pl.pallas_call(inner_kernel, out_shape=(array((TOK, CH), F32), array((TOK...  8.95 us
    all_to_all x1, starting transfers between devices, per_device(): chip = lax.all_to_all(back, ('x', 'z'), 0, 0)  8.26 us
    ppermute x1, waiting for transfers between devices, per_device(): lead_fresh = lax.ppermute(high_fresh, 'core', [(0, 1)])  5.86 us
    ppermute x5, starting transfers between devices, onward(): return lax.ppermute(value, 'section', [(i, (i + 1) % 4) for i in range(4)])  5.15 us
    ppermute x1, starting transfers between devices, per_device(): behind = lax.ppermute(u[TOK - 16:], ctx, [(i, i + 1) for i in range(63)])  4.94 us
  transfers between devices with their start and end apart: 11, of which 7 were waited for; matrix products, arithmetic and copies ran while one was open for 1% of the time, Pallas kernels for 20%

profile of v6, /device:TPU:1, one launch (start us, length us, event | category | flops | bytes accessed | tf_op | source)
XLA Modules:
  0.0 95.3 jit_solution(3175955216134936905)
XLA Ops:
  0.0 1.1 %slice_bitcast_fusion = bf16[16,4096]{1,0:T(8,128)(2,1)S(1)} fusion(bf16[1,256,4096]{2,1,0:T(8,128)(2,1)} %param.9), kind=kLoop, calls=%fused_computation.1 | loop fusion | bytes 262144 | tf_op jit(solution)/shard_map/slice | solution.py:355
  1.1 4.9 %collective-permute-start = (bf16[16,4096]{1,0:T(8,128)(2,1)S(1)}, bf16[16,4096]{1,0:T(8,128)(2,1)S(1)}, u32[]{:S(2)}, u32[]{:S(2)}) collective-permute-start(bf16[16,4096]{1,0:T(8,128)(2,1)S(1)} %slice_bitcast_fusion), channel_id=1, source_target_pairs={{0,1},{1,2},{2,3},{3,4},{4,5},{5,6},{6,7},{7,8},{8,9},{9,10},{10,1... | collective-permute-start | bytes 393224 | tf_op jit(solution)/shard_map/ppermute | solution.py:355
  6.1 2.3 %fetch.1 = (bf16[256,4096]{1,0:T(8,128)(2,1)S(1)}, bf16[4096,256]{1,0:T(8,128)(2,1)S(1)}) custom-call(bf16[256,4096]{1,0:T(8,128)(2,1)} %bitcast.3.u, bf16[4096,256]{1,0:T(8,128)(2,1)} %bitcast.31), custom_call_target="tpu_custom_call" | custom-call | flops 1000000000 | bytes 10000000 | tf_op jit(solution)/shard_map/fetch/pallas_call | solution.py:356
  8.4 3.7 %send.1 = (bf16[144,2048]{1,0:T(8,128)(2,1)S(1)}, bf16[128,256]{1,0:T(8,128)(2,1)S(1)}, bf16[16,16,256]{2,1,0:T(8,128)(2,1)S(1)}, bf16[256,128]{1,0:T(8,128)(2,1)S(1)}, bf16[16,128]{1,0:T(8,128)(2,1)S(1)}) custom-call(s32[3]{0:T(128)S(1)} %pad_add_fusion.flags, bf16[256,4096]{1,0:T(8,128)(2,1)S(1)} %get-tuple-element.26.u, ...), custom_call_target="tpu_custom_call" | custom-call | flops 600000000 | bytes 4500000 | tf_op jit(solution)/shard_map/send/pallas_call | solution.py:380
  12.3 1.4 %collective-permute-start.2 = (bf16[256,4096]{1,0:T(8,128)(2,1)}, bf16[256,4096]{1,0:T(8,128)(2,1)}, u32[]{:S(2)}, u32[]{:S(2)}) collective-permute-start(bf16[256,4096]{1,0:T(8,128)(2,1)} %bitcast.3.u), channel_id=1, source_target_pairs={{0,64},{64,128},{128,192},{192,0},{1,65},{65,129},{129,193},{193,1... | collective-permute-start | bytes 6291464 | tf_op jit(solution)/shard_map/ppermute | solution.py:348
  13.6 2.5 %keep.1 = bf16[144,2048]{1,0:T(8,128)(2,1)S(1)} custom-call(s32[3]{0:T(128)S(1)} %pad_add_fusion.flags, bf16[256,4096]{1,0:T(8,128)(2,1)S(1)} %get-tuple-element.26.u, bf16[16,4096]{1,0:T(8,128)(2,1)S(1)} %collective-permute-done.behind, bf16[3,4352]{1,0:T(4,128)(2,1)S(1)} %bitcast.28, bf16[4,4352]{1,0:T(4,128)(2,1)S(1)} %bitcast.30, ...), custom_call_target="tpu_custom_call" | custom-call | flops 600000000 | bytes 4500000 | tf_op jit(solution)/shard_map/keep/pallas_call | solution.py:397
  16.2 1.7 %join.1 = bf16[32,16,640]{2,1,0:T(8,128)(2,1)} custom-call(s32[3]{0:T(128)S(1)} %pad_add_fusion.flags, bf16[144,2048]{1,0:T(8,128)(2,1)S(1)} %keep.1, bf16[144,2048]{1,0:T(8,128)(2,1)S(1)} %collective-permute-done.1.got), custom_call_target="tpu_custom_call" | custom-call | flops 1000000 | bytes 2500000 | tf_op jit(solution)/shard_map/join/pallas_call | solution.py:406
  17.9 12.7 %all-to-all-start = ((bf16[32,16,640]{2,1,0:T(8,128)(2,1)}), bf16[32,16,640]{2,1,0:T(8,128)(2,1)S(1)}, u32[]{:S(2)}, u32[]{:S(2)}) async-start(bf16[32,16,640]{2,1,0:T(8,128)(2,1)} %join.1), calls=%async_computation | async-start | bytes 1310720 | tf_op jit(solution)/shard_map/all_to_all | solution.py:411
  31.1 16.3 %all-to-all-done.got = bf16[32,16,640]{2,1,0:T(8,128)(2,1)S(1)} async-done(((bf16[32,16,640]{2,1,0:T(8,128)(2,1)}), bf16[32,16,640]{2,1,0:T(8,128)(2,1)S(1)}, u32[]{:S(2)}, u32[]{:S(2)}) %all-to-all-start) | async-done | bytes 655392 | tf_op jit(solution)/shard_map/all_to_all | solution.py:411
  47.4 1.1 %scan.1 = bf16[32,16,512]{2,1,0:T(8,128)(2,1)} custom-call(bf16[32,16,640]{2,1,0:T(8,128)(2,1)S(1)} %all-to-all-done.got, f32[16,512]{1,0:T(8,128)S(1)} %copy.17.start), custom_call_target="tpu_custom_call" | custom-call | tf_op jit(solution)/shard_map/scan/pallas_call | solution.py:415
  48.6 8.3 %all-to-all-start.1 = ((bf16[32,16,512]{2,1,0:T(8,128)(2,1)}), bf16[32,16,512]{2,1,0:T(8,128)(2,1)}, u32[]{:S(2)}, u32[]{:S(2)}) async-start(bf16[32,16,512]{2,1,0:T(8,128)(2,1)} %scan.1), calls=%async_computation.1 | async-start | bytes 1048576 | tf_op jit(solution)/shard_map/all_to_all | solution.py:423
  57.1 1.4 %collective-permute-start.5 = (bf16[16,4096]{1,0:T(8,128)(2,1)S(1)}, bf16[16,4096]{1,0:T(8,128)(2,1)S(1)}, u32[]{:S(2)}, u32[]{:S(2)}) collective-permute-start(bf16[16,4096]{1,0:T(8,128)(2,1)S(1)} %concatenate.7), channel_id=1, source_target_pairs={{0,64},{64,128},{128,192},{192,0},{1,65},{65,129},{129,193},{193,1... | collective-permute-start | bytes 393224 | tf_op jit(solution)/shard_map/ppermute | solution.py:348
  58.5 1.0 %collective-permute-start.3 = (bf16[16,16,256]{2,1,0:T(8,128)(2,1)S(1)}, bf16[16,16,256]{2,1,0:T(8,128)(2,1)S(1)}, u32[]{:S(2)}, u32[]{:S(2)}) collective-permute-start(bf16[16,16,256]{2,1,0:T(8,128)(2,1)S(1)} %get-tuple-element.33), channel_id=1, source_target_pairs={{0,64},{64,128},{128,192},{192,0},{1,65},{65,129},{129,193},{193,1... | collective-permute-start | bytes 393224 | tf_op jit(solution)/shard_map/ppermute | solution.py:348
  59.6 1.3 %collective-permute-done.2.refs_0_ = bf16[256,4096]{1,0:T(8,128)(2,1)} collective-permute-done((bf16[256,4096]{1,0:T(8,128)(2,1)}, bf16[256,4096]{1,0:T(8,128)(2,1)}, u32[]{:S(2)}, u32[]{:S(2)}) %collective-permute-start.2) | collective-permute-done | bytes 2097184 | tf_op jit(solution)/shard_map/ppermute | solution.py:348
  60.8 2.2 %collective-permute-done.5.par = bf16[16,4096]{1,0:T(8,128)(2,1)S(1)} collective-permute-done((bf16[16,4096]{1,0:T(8,128)(2,1)S(1)}, bf16[16,4096]{1,0:T(8,128)(2,1)S(1)}, u32[]{:S(2)}, u32[]{:S(2)}) %collective-permute-start.5) | collective-permute-done | bytes 131104 | tf_op jit(solution)/shard_map/ppermute | solution.py:348
  63.0 2.8 %collective-permute-done.3.pack = bf16[16,16,256]{2,1,0:T(8,128)(2,1)S(1)} collective-permute-done((bf16[16,16,256]{2,1,0:T(8,128)(2,1)S(1)}, bf16[16,16,256]{2,1,0:T(8,128)(2,1)S(1)}, u32[]{:S(2)}, u32[]{:S(2)}) %collective-permute-start.3) | collective-permute-done | bytes 131104 | tf_op jit(solution)/shard_map/ppermute | solution.py:348
  65.8 2.8 %collective-permute-done.4.logs = f32[128,256]{1,0:T(8,128)S(1)} collective-permute-done((f32[128,256]{1,0:T(8,128)S(1)}, f32[128,256]{1,0:T(8,128)S(1)}, u32[]{:S(2)}, u32[]{:S(2)}) %collective-permute-start.4) | collective-permute-done | bytes 131104 | tf_op jit(solution)/shard_map/ppermute | solution.py:348
  68.6 2.3 %all-to-all-done.1 = bf16[32,16,512]{2,1,0:T(8,128)(2,1)} async-done(((bf16[32,16,512]{2,1,0:T(8,128)(2,1)}), bf16[32,16,512]{2,1,0:T(8,128)(2,1)}, u32[]{:S(2)}, u32[]{:S(2)}) %all-to-all-start.1) | async-done | bytes 524320 | tf_op jit(solution)/shard_map/all_to_all | solution.py:423
  70.9 1.3 %collective-permute-start.6 = (bf16[32,16,512]{2,1,0:T(8,128)(2,1)}, bf16[32,16,512]{2,1,0:T(8,128)(2,1)S(1)}, u32[]{:S(2)}, u32[]{:S(2)}) collective-permute-start(bf16[32,16,512]{2,1,0:T(8,128)(2,1)} %all-to-all-done.1), channel_id=1, source_target_pairs={{0,64},{64,128},{128,192},{192,0},{1,65},{65,129},{129,193},{193,1... | collective-permute-start | bytes 1572872 | tf_op jit(solution)/shard_map/ppermute | solution.py:348
  72.2 8.9 %inner.1 = (f32[256,4096]{1,0:T(8,128)S(1)}, bf16[256,128]{1,0:T(8,128)(2,1)S(1)}, bf16[256,4096]{1,0:T(8,128)(2,1)S(1)}, bf16[144,2048]{1,0:T(8,128)(2,1)S(1)}, bf16[144,2048]{1,0:T(8,128)(2,1)S(1)}) custom-call(bf16[256,4096]{1,0:T(8,128)(2,1)} %mark.2.far, bf16[16,16,256]{2,1,0:T(8,128)(2,1)S(1)} %collective-permute-done.3.pack, ...), custom_call_target="tpu_custom_call" | custom-call | flops 1 | bytes 1 | tf_op jit(solution)/shard_map/inner/pallas_call | solution.py:430
  81.2 1.3 %collective-permute-start.7 = (bf16[144,2048]{1,0:T(8,128)(2,1)S(1)}, bf16[144,2048]{1,0:T(8,128)(2,1)S(1)}, u32[]{:S(2)}, u32[]{:S(2)}) collective-permute-start(bf16[144,2048]{1,0:T(8,128)(2,1)S(1)} %get-tuple-element.43), channel_id=1, source_target_pairs={{0,1},{2,3},{4,5},{6,7},{8,9},{10,11},{12,13},{14,15},{16,17},{18,... | collective-permute-start | bytes 1769480 | tf_op jit(solution)/shard_map/ppermute | solution.py:449
  82.5 5.9 %collective-permute-done.7.lead_fresh = bf16[144,2048]{1,0:T(8,128)(2,1)S(1)} collective-permute-done((bf16[144,2048]{1,0:T(8,128)(2,1)S(1)}, bf16[144,2048]{1,0:T(8,128)(2,1)S(1)}, u32[]{:S(2)}, u32[]{:S(2)}) %collective-permute-start.7) | collective-permute-done | bytes 589856 | tf_op jit(solution)/shard_map/ppermute | solution.py:449
  89.5 2.8 %outer_mine.1.done = bf16[256,4096]{1,0:T(8,128)(2,1)} custom-call(s32[3]{0:T(128)S(1)} %pad_add_fusion.flags, bf16[256,4096]{1,0:T(8,128)(2,1)S(1)} %get-tuple-element.39.u, f32[256,4096]{1,0:T(8,128)S(1)} %get-tuple-element.40.partial, bf16[128,2048]{1,0:T(8,128)(2,1)S(1)} %get-tuple-element.46.starts, ...), custom_call_target="tpu_custom_call" | custom-call | flops 600000000 | bytes 5000000 | tf_op jit(solution)/shard_map/outer_mine/pallas_call | solution.py:457
  92.3 2.8 %outer_other.1 = bf16[256,4096]{1,0:T(8,128)(2,1)} custom-call(s32[3]{0:T(128)S(1)} %pad_add_fusion.flags, bf16[256,4096]{1,0:T(8,128)(2,1)S(1)} %get-tuple-element.39.u, f32[256,4096]{1,0:T(8,128)S(1)} %get-tuple-element.40.partial, bf16[128,2048]{1,0:T(8,128)(2,1)S(1)} %collective-permute-done.8.starts, ...), custom_call_target="tpu_custom_call", output_to_operand_aliasing={{}: (7, {})} | custom-call | flops 600000000 | bytes 5000000 | tf_op jit(solution)/shard_map/outer_other/pallas_call | solution.py:467
  (35 shorter events, 2.1 us)
Async XLA Ops:
  0.0 30.8 %copy-start = (f32[1,64,128,64]{2,3,1,0:T(8,128)S(1)}, f32[1,64,128,64]{2,3,1,0:T(8,128)}, u32[]{:S(2)}) copy-start(f32[1,64,128,64]{2,3,1,0:T(8,128)} %param.16) | copy-start | bytes 6291460
  1.1 7.4 %collective-permute-start = (bf16[16,4096]{1,0:T(8,128)(2,1)S(1)}, bf16[16,4096]{1,0:T(8,128)(2,1)S(1)}, u32[]{:S(2)}, u32[]{:S(2)}) collective-permute-start(bf16[16,4096]{1,0:T(8,128)(2,1)S(1)} %slice_bitcast_fusion), channel_id=1, source_target_pairs={{0,1},{1,2},{2,3},{3,4},{4,5},{5,6},{6,7},{7,8},{8,9},{9,10},{10,1... | collective-permute-start | bytes 393224 | tf_op jit(solution)/shard_map/ppermute | solution.py:355
  6.1 2.3 %copy-start.3 = (f32[1,256,64]{1,2,0:T(8,128)S(1)}, f32[1,256,64]{1,2,0:T(8,128)}, u32[]{:S(2)}) copy-start(f32[1,256,64]{1,2,0:T(8,128)} %param.13) | copy-start | bytes 196612
  6.1 2.3 %copy-start.4 = (f32[1,256,64]{1,2,0:T(8,128)S(1)}, f32[1,256,64]{1,2,0:T(8,128)}, u32[]{:S(2)}) copy-start(f32[1,256,64]{1,2,0:T(8,128)} %param.12) | copy-start | bytes 196612
  6.1 2.3 %copy-start.1 = (bf16[1,3,4352]{2,1,0:T(4,128)(2,1)S(1)}, bf16[1,3,4352]{2,1,0:T(4,128)(2,1)}, u32[]{:S(2)}) copy-start(bf16[1,3,4352]{2,1,0:T(4,128)(2,1)} %param.17) | copy-start | bytes 78340
  6.1 2.3 %copy-start.2 = (bf16[1,4,4352]{2,1,0:T(4,128)(2,1)S(1)}, bf16[1,4,4352]{2,1,0:T(4,128)(2,1)}, u32[]{:S(2)}) copy-start(bf16[1,4,4352]{2,1,0:T(4,128)(2,1)} %param.11) | copy-start | bytes 104452
  12.2 4.0 %collective-permute-start.1 = (bf16[144,2048]{1,0:T(8,128)(2,1)S(1)}, bf16[144,2048]{1,0:T(8,128)(2,1)S(1)}, u32[]{:S(2)}, u32[]{:S(2)}) collective-permute-start(bf16[144,2048]{1,0:T(8,128)(2,1)S(1)} %get-tuple-element.31), channel_id=1, source_target_pairs={{0,1},{1,0},{2,3},{3,2},{4,5},{5,4},{6,7},{7,6},{8,9},{9,8},{10,11... | collective-permute-start | bytes 1769480 | tf_op jit(solution)/shard_map/ppermute | solution.py:351
  12.3 48.5 %collective-permute-start.2 = (bf16[256,4096]{1,0:T(8,128)(2,1)}, bf16[256,4096]{1,0:T(8,128)(2,1)}, u32[]{:S(2)}, u32[]{:S(2)}) collective-permute-start(bf16[256,4096]{1,0:T(8,128)(2,1)} %bitcast.3.u), channel_id=1, source_target_pairs={{0,64},{64,128},{128,192},{192,0},{1,65},{65,129},{129,193},{193,1... | collective-permute-start | bytes 6291464 | tf_op jit(solution)/shard_map/ppermute | solution.py:348
  16.1 14.5 %copy-start.6 = (f32[1,64]{1,0:T(1,128)S(1)}, f32[1,64]{1,0:T(1,128)}, u32[]{:S(2)}) copy-start(f32[1,64]{1,0:T(1,128)} %param.14) | copy-start | bytes 772
  17.9 39.0 %copy-start.5 = (bf16[1,4096]{1,0:T(2,128)(2,1)S(1)}, bf16[1,4096]{1,0:T(2,128)(2,1)}, u32[]{:S(2)}) copy-start(bf16[1,4096]{1,0:T(2,128)(2,1)} %param.15) | copy-start | bytes 24580
  17.9 29.6 %all-to-all-start = ((bf16[32,16,640]{2,1,0:T(8,128)(2,1)}), bf16[32,16,640]{2,1,0:T(8,128)(2,1)S(1)}, u32[]{:S(2)}, u32[]{:S(2)}) async-start(bf16[32,16,640]{2,1,0:T(8,128)(2,1)} %join.1), calls=%async_computation | async-start | bytes 1310720 | tf_op jit(solution)/shard_map/all_to_all | solution.py:411
  48.6 22.3 %all-to-all-start.1 = ((bf16[32,16,512]{2,1,0:T(8,128)(2,1)}), bf16[32,16,512]{2,1,0:T(8,128)(2,1)}, u32[]{:S(2)}, u32[]{:S(2)}) async-start(bf16[32,16,512]{2,1,0:T(8,128)(2,1)} %scan.1), calls=%async_computation.1 | async-start | bytes 1048576 | tf_op jit(solution)/shard_map/all_to_all | solution.py:423
  57.1 5.9 %collective-permute-start.5 = (bf16[16,4096]{1,0:T(8,128)(2,1)S(1)}, bf16[16,4096]{1,0:T(8,128)(2,1)S(1)}, u32[]{:S(2)}, u32[]{:S(2)}) collective-permute-start(bf16[16,4096]{1,0:T(8,128)(2,1)S(1)} %concatenate.7), channel_id=1, source_target_pairs={{0,64},{64,128},{128,192},{192,0},{1,65},{65,129},{129,193},{193,1... | collective-permute-start | bytes 393224 | tf_op jit(solution)/shard_map/ppermute | solution.py:348
  58.5 7.4 %collective-permute-start.3 = (bf16[16,16,256]{2,1,0:T(8,128)(2,1)S(1)}, bf16[16,16,256]{2,1,0:T(8,128)(2,1)S(1)}, u32[]{:S(2)}, u32[]{:S(2)}) collective-permute-start(bf16[16,16,256]{2,1,0:T(8,128)(2,1)S(1)} %get-tuple-element.33), channel_id=1, source_target_pairs={{0,64},{64,128},{128,192},{192,0},{1,65},{65,129},{129,193},{193,1... | collective-permute-start | bytes 393224 | tf_op jit(solution)/shard_map/ppermute | solution.py:348
  59.5 9.2 %collective-permute-start.4 = (f32[128,256]{1,0:T(8,128)S(1)}, f32[128,256]{1,0:T(8,128)S(1)}, u32[]{:S(2)}, u32[]{:S(2)}) collective-permute-start(f32[128,256]{1,0:T(8,128)S(1)} %pad_maximum_fusion.logs), channel_id=1, source_target_pairs={{0,64},{64,128},{128,192},{192,0},{1,65},{65,129},{129,193},{193,1... | collective-permute-start | bytes 393224 | tf_op jit(solution)/shard_map/ppermute | solution.py:348
  70.9 11.6 %collective-permute-start.6 = (bf16[32,16,512]{2,1,0:T(8,128)(2,1)}, bf16[32,16,512]{2,1,0:T(8,128)(2,1)S(1)}, u32[]{:S(2)}, u32[]{:S(2)}) collective-permute-start(bf16[32,16,512]{2,1,0:T(8,128)(2,1)} %all-to-all-done.1), channel_id=1, source_target_pairs={{0,64},{64,128},{128,192},{192,0},{1,65},{65,129},{129,193},{193,1... | collective-permute-start | bytes 1572872 | tf_op jit(solution)/shard_map/ppermute | solution.py:348
  81.2 7.2 %collective-permute-start.7 = (bf16[144,2048]{1,0:T(8,128)(2,1)S(1)}, bf16[144,2048]{1,0:T(8,128)(2,1)S(1)}, u32[]{:S(2)}, u32[]{:S(2)}) collective-permute-start(bf16[144,2048]{1,0:T(8,128)(2,1)S(1)} %get-tuple-element.43), channel_id=1, source_target_pairs={{0,1},{2,3},{4,5},{6,7},{8,9},{10,11},{12,13},{14,15},{16,17},{18,... | collective-permute-start | bytes 1769480 | tf_op jit(solution)/shard_map/ppermute | solution.py:449
  89.2 3.0 %collective-permute-start.8 = (bf16[128,2048]{1,0:T(8,128)(2,1)S(1)}, bf16[128,2048]{1,0:T(8,128)(2,1)S(1)}, u32[]{:S(2)}, u32[]{:S(2)}) collective-permute-start(bf16[128,2048]{1,0:T(8,128)(2,1)S(1)} %get-tuple-element.44), channel_id=1, source_target_pairs={{0,1},{1,0},{2,3},{3,2},{4,5},{5,4},{6,7},{7,6},{8,9},{9,8},{10,11... | collective-permute-start | bytes 1572872 | tf_op jit(solution)/shard_map/ppermute | solution.py:351
